TPU v7x, 32 devices: a whole 2x2x4 slice. The times are simulated.
32 devices in a mesh: seq: 8 (over z, x), head: 4 (over y, core).
Axes of the slice: x: 2, y: 2, z: 4, core: 2. Of those that a mesh axis runs over, the one named last changes fastest.
Arguments:
- block_input: bfloat16 [8192, 1024], P('seq'), may hold values from -6 to 6
- first_gain: bfloat16 [1024], replicated, may hold values from 0.5 to 1.5
- w_mix: bfloat16 [1024, 5120], P(None, 'head'), may hold values from -0.1875 to 0.1875
- conv_taps: bfloat16 [4, 5120], P(None, 'head'), may hold values from -3 to 3
- w_rates: bfloat16 [1024, 24], P(None, 'head'), may hold values from -1 to 1
- log_rate: float32 [8], P('head'), may hold values from -6.9 to -4
- rate_bias: float32 [8], P('head'), may hold values from -5 to -3
- w_outgate: bfloat16 [1024, 1024], P(None, 'head'), may hold values from -0.1875 to 0.1875
- head_gain: bfloat16 [128], replicated, may hold values from 0.5 to 1.5
- w_out: bfloat16 [1024, 1024], P('head'), may hold values from -0.25 to 0.25
- second_gain: bfloat16 [1024], replicated, may hold values from 0.5 to 1.5
- w_ffn: bfloat16 [1024, 2, 2816], P(None, None, 'head'), may hold values from -0.1875 to 0.1875
- w_down: bfloat16 [2816, 1024], P('head'), may hold values from -0.21875 to 0.21875
- grad_output: bfloat16 [8192, 1024], P('seq'), may hold values from -6 to 6
- seq_starts: int32 [8], P('seq'), may hold values from 1 to 1024, as said below
Outputs:
- block_output: bfloat16 [8192, 1024], P('seq')
- grad_input: float32 [8192, 1024], P('seq')
- grad_first_gain: float32 [1024], P('seq')
- grad_mix: float32 [1024, 5120], P('seq', 'head')
- grad_conv: float32 [4, 5120], P(None, 'head')
- grad_rates: float32 [1024, 24], P('seq', 'head')
- grad_log_rate: float32 [8], P('head')
- grad_rate_bias: float32 [8], P('head')
- grad_outgate: float32 [1024, 1024], P('seq', 'head')
- grad_head_gain: float32 [128], replicated
- grad_out: float32 [1024, 1024], P('head', 'seq')
- grad_second_gain: float32 [1024], P('seq')
- grad_ffn: float32 [1024, 2, 2816], P('seq', None, 'head')
- grad_down: float32 [2816, 1024], P('head', 'seq')
Inputs may be any that keep to these rules, and one draw needn't show every extreme that they name: `seq_starts`: token 0 starts a sequence; a block holds at most one more start, at an offset of 1 to 1021, and holds 1024 where none starts; blocks with starts are never neighbours and the last block has none, so every sequence is longer than 1024 tokens; 4 sequences in all.
All inputs are finite; a program needn't handle non-finite values.
Results may differ from a plain program's by a relative error of at most 0.011.
Values sent between devices are 32-bit elements; how exact they have to be, the bound alone decides.
No kernel may reach another device: no remote copies, remote signals or barrier semaphores. Data moves between devices by JAX's collectives and lax.ppermute only.
A program may use at most 256 MiB of HBM per device.

v0:
```python
from functools import partial

import jax
import jax.numpy as jnp
from jax import lax
from jax.sharding import PartitionSpec as P

STEPS = 2
CONV = 4
SPAN = 64


EPSILON = 1e-06
HIGH_ACCURACY = lax.Precision.HIGHEST


def shifted(value, axis, steps):
    count = lax.axis_size(axis)
    first, last = (max(0, -steps), min(count, count - steps))
    return lax.ppermute(value, axis, [(source, source + steps) for source in range(first, last)])


def prefix(value, axis, join, neutral, backward):
    count, mine = (lax.axis_size(axis), lax.axis_index(axis))
    pieces = jax.tree.map(lambda part: lax.all_gather(part, axis), value)
    if backward:
        pieces = jax.tree.map(lambda part: part[::-1], pieces)
        mine = count - 1 - mine
    running = jax.tree.map(
        lambda part, zero: jnp.full_like(part, 0) + jnp.asarray(zero, part.dtype), value, neutral
    )

    def turn(position, running):
        longer = join(running, jax.tree.map(lambda part: part[position], pieces))
        return jax.tree.map(lambda new, old: jnp.where(position < mine, new, old), longer, running)

    return lax.fori_loop(0, count - 1, turn, running)


def rms_gain(values, gain):
    return values * lax.rsqrt(jnp.mean(values * values, -1, keepdims=True) + EPSILON) * gain


def silu_product(gate, up):
    return jax.nn.silu(gate) * up


def contract(left, right, left_dim, right_dim):
    return lax.dot_general(
        left, right, (((left_dim,), (right_dim,)), ((), ())), preferred_element_type=jnp.float32
    )


def chain(earlier, later):
    first = jnp.einsum("hij,hjk->hik", earlier[0], later[0], precision=HIGH_ACCURACY)
    second = jnp.einsum("hij,hjk->hik", earlier[1], later[0], precision=HIGH_ACCURACY) + later[1]
    return (first, second)


def prepare(offset, span_len, widened, rates, log_rate, rate_bias, taps):
    tok_rows = rates.shape[0]
    heads = log_rate.shape[0]
    groups = 1 + 2 * STEPS
    width = taps.shape[1] // (groups * heads)
    blocks = tok_rows // span_len
    virt = STEPS * span_len
    place = jnp.arange(tok_rows)
    lags = taps.shape[0]
    conv = jnp.zeros((tok_rows, taps.shape[1]), jnp.float32)
    for lag in range(lags):
        source = place - (lags - 1) + lag
        valid = jnp.logical_not((source < offset) & (offset <= place)).astype(jnp.float32)
        conv = conv + taps[lag] * widened[lag : lag + tok_rows] * valid[:, None]
    acts = jax.nn.silu(conv).reshape(tok_rows, heads, groups, width)
    queries = acts[:, :, 0]
    key_rows = acts[:, :, 1 : 1 + STEPS]
    values = acts[:, :, 1 + STEPS :]
    key_rows = key_rows * lax.rsqrt(jnp.sum(key_rows * key_rows, -1, keepdims=True) + EPSILON)
    rates3 = rates.reshape(tok_rows, heads, STEPS + 1)
    betas = jax.nn.sigmoid(rates3[..., :STEPS])
    decay = -jnp.exp(log_rate) * jax.nn.softplus(rates3[..., STEPS] + rate_bias)

    def virtual_tokens(array):
        moved = jnp.moveaxis(array, 1, 0)
        return moved.reshape((heads, blocks, virt) + moved.shape[3:])

    virtual_key_rows = virtual_tokens(key_rows)
    virtual_value_rows = virtual_tokens(values)
    virtual_beta_rows = virtual_tokens(betas)
    padding = jnp.zeros(decay.shape + (STEPS - 1,), jnp.float32)
    vdecay = virtual_tokens(jnp.concatenate([decay[..., None], padding], -1))
    broadcast_query_rows = jnp.moveaxis(queries, 1, 0).reshape(heads, blocks, span_len, width)
    resets = (place == offset).astype(jnp.float32)
    reset_pad = jnp.zeros((tok_rows, STEPS - 1), jnp.float32)
    vresets = jnp.concatenate([resets[:, None], reset_pad], -1).reshape(blocks, virt)
    cumul = jnp.cumsum(vdecay, -1)
    segment = jnp.cumsum(vresets, -1)
    lower = jnp.tril(jnp.ones((virt, virt), jnp.bool_))
    strict = jnp.tril(jnp.ones((virt, virt), jnp.float32), -1)
    joined = (segment[:, :, None] == segment[:, None, :]) & lower
    spread = cumul[..., :, None] - cumul[..., None, :]
    ratio = jnp.exp(jnp.where(joined, spread, 0.0)) * joined.astype(jnp.float32)
    carried_state = jnp.exp(cumul) * (segment == 0).astype(jnp.float32)
    similarity_scores = jnp.einsum(
        "mlkv,mljv->mlkj", virtual_key_rows, virtual_key_rows, precision=HIGH_ACCURACY
    )
    system = (
        jnp.eye(virt, dtype=jnp.float32)
        + virtual_beta_rows[..., None] * similarity_scores * ratio * strict
    )
    right_side = jnp.concatenate(
        [
            virtual_beta_rows[..., None] * virtual_value_rows,
            (virtual_beta_rows * carried_state)[..., None] * virtual_key_rows,
        ],
        -1,
    )
    solved = jax.scipy.linalg.solve_triangular(system, right_side, lower=True, unit_diagonal=True)
    fresh_state = solved[..., :width]
    weight_matrices = solved[..., width:]
    scores = ratio[..., STEPS - 1 :: STEPS, :] * jnp.einsum(
        "jgoq,jgpq->jgop", broadcast_query_rows, virtual_key_rows, precision=HIGH_ACCURACY
    )
    local_out = jnp.einsum("hcis,hcsv->hciv", scores, fresh_state, precision=HIGH_ACCURACY)
    query_map = carried_state[..., STEPS - 1 :: STEPS, None] * broadcast_query_rows - jnp.einsum(
        "hcis,hcsk->hcik", scores, weight_matrices, precision=HIGH_ACCURACY
    )
    tail_tokens = ratio[..., virt - 1, :]
    transfer = carried_state[..., virt - 1, None, None] * jnp.eye(
        width, dtype=jnp.float32
    ) - jnp.einsum(
        "wfyz,wfya->wfza",
        weight_matrices * tail_tokens[..., None],
        virtual_key_rows,
        precision=HIGH_ACCURACY,
    )
    offset_lookup = jnp.einsum(
        "xyno,xynz->xyoz",
        fresh_state * tail_tokens[..., None],
        virtual_key_rows,
        precision=HIGH_ACCURACY,
    )
    return (local_out, query_map, transfer, offset_lookup)


def compose(transfer, offset_lookup):
    heads = transfer.shape[0]
    width = transfer.shape[-1]

    def advance(carry, item):
        return (chain(carry, item), carry)

    start = (
        jnp.broadcast_to(jnp.eye(width, dtype=jnp.float32), (heads, width, width)),
        jnp.zeros((heads, width, width), jnp.float32),
    )
    final, prefixes = lax.scan(
        advance, start, (jnp.moveaxis(transfer, 1, 0), jnp.moveaxis(offset_lookup, 1, 0))
    )
    return (jnp.moveaxis(prefixes[0], 0, 1), jnp.moveaxis(prefixes[1], 0, 1), final[0], final[1])


def finish(local_out, query_map, prefix_p, prefix_b, incoming):
    begin = jnp.einsum("hvk,hckj->hcvj", incoming, prefix_p, precision=HIGH_ACCURACY) + prefix_b
    result = local_out + jnp.einsum("hcik,hcvk->hciv", query_map, begin, precision=HIGH_ACCURACY)
    heads = result.shape[0]
    width = result.shape[-1]
    return jnp.moveaxis(result.reshape(heads, -1, width), 0, 1).reshape(-1, heads * width)


def post(mixed, outgate, head_gain):
    tok_rows = mixed.shape[0]
    width = head_gain.shape[0]
    normed = rms_gain(mixed.reshape(tok_rows, -1, width), head_gain).reshape(tok_rows, -1)
    return normed * jax.nn.silu(outgate)


def local_run(function, inputs):
    return jax.vjp(function, *inputs)


def body(
    block_input,
    first_gain,
    w_mix,
    conv_taps,
    w_rates,
    log_rate,
    rate_bias,
    w_outgate,
    head_gain,
    w_out,
    second_gain,
    w_ffn,
    w_down,
    grad_output,
    seq_starts,
):
    tok_rows, model = block_input.shape
    width = head_gain.shape[0]
    offset = seq_starts[0]
    edge_rows = CONV - 1
    inputs_f = block_input.astype(jnp.float32)
    normed1, first_back = jax.vjp(rms_gain, inputs_f, first_gain.astype(jnp.float32))
    normed1_low = normed1.astype(jnp.bfloat16)
    mixing = jnp.dot(normed1_low, w_mix, preferred_element_type=jnp.float32)
    rate_raw = jnp.dot(normed1_low, w_rates, preferred_element_type=jnp.float32)
    outgate = jnp.dot(normed1_low, w_outgate, preferred_element_type=jnp.float32)
    edge = shifted(mixing[tok_rows - edge_rows :], "seq", 1)
    widened = jnp.concatenate([edge, mixing], 0)
    prepare_fn = partial(prepare, offset, SPAN)
    prep_inputs = (widened, rate_raw, log_rate, rate_bias, conv_taps.astype(jnp.float32))
    pieces, prep_back = local_run(prepare_fn, prep_inputs)
    local_out, query_map, transfer, offset_lookup = pieces
    maps, compose_back = local_run(compose, (transfer, offset_lookup))
    prefix_p, prefix_b, device_p, device_b = maps
    identity = (
        jnp.broadcast_to(jnp.eye(width, dtype=jnp.float32), device_p.shape),
        jnp.zeros_like(device_b),
    )
    incoming = prefix((device_p, device_b), "seq", chain, identity, False)[1]
    finish_inputs = (local_out, query_map, prefix_p, prefix_b, incoming)
    mixed, finish_back = local_run(finish, finish_inputs)
    gated, post_back = jax.vjp(post, mixed, outgate, head_gain.astype(jnp.float32))
    gated_low = gated.astype(jnp.bfloat16)
    mixer_out = lax.psum(jnp.dot(gated_low, w_out, preferred_element_type=jnp.float32), "head")
    middle = inputs_f + mixer_out
    normed2, second_back = jax.vjp(rms_gain, middle, second_gain.astype(jnp.float32))
    normed2_low = normed2.astype(jnp.bfloat16)
    ffn_flat = w_ffn.reshape(model, -1)
    hidden_units = ffn_flat.shape[1] // 2
    both = jnp.dot(normed2_low, ffn_flat, preferred_element_type=jnp.float32)
    activ, glu_back = jax.vjp(silu_product, both[:, :hidden_units], both[:, hidden_units:])
    activ_low = activ.astype(jnp.bfloat16)
    ffn_out = lax.psum(jnp.dot(activ_low, w_down, preferred_element_type=jnp.float32), "head")
    block_output = (middle + ffn_out).astype(jnp.bfloat16)
    grad_activ = contract(grad_output, w_down, 1, 1)
    grad_down = contract(activ_low, grad_output, 0, 0)
    grad_gate, grad_up = glu_back(grad_activ)
    grad_both = jnp.concatenate([grad_gate, grad_up], 1).astype(jnp.bfloat16)
    grad_ffn = contract(normed2_low, grad_both, 0, 0).reshape(w_ffn.shape)
    grad_normed2 = lax.psum(contract(grad_both, ffn_flat, 1, 1), "head")
    grad_middle, grad_second_gain = second_back(grad_normed2)
    grad_middle = grad_middle + grad_output.astype(jnp.float32)
    grad_branch = grad_middle.astype(jnp.bfloat16)
    grad_gated = contract(grad_branch, w_out, 1, 1)
    grad_out = contract(gated_low, grad_branch, 0, 0)
    grad_mixed, grad_outgate_act, grad_head_gain = post_back(grad_gated)
    grad_local, grad_query, grad_prefix_p, grad_prefix_b, grad_incoming = finish_back(grad_mixed)
    transposed = jnp.swapaxes(device_p, 1, 2)
    grad_leaving = prefix((transposed, grad_incoming), "seq", chain, identity, True)[1]
    grad_device_p = jnp.einsum("hvk,hvj->hkj", incoming, grad_leaving, precision=HIGH_ACCURACY)
    grad_transfer, grad_offset = compose_back(
        (grad_prefix_p, grad_prefix_b, grad_device_p, grad_leaving)
    )
    grad_widened, grad_rate_act, grad_log_rate, grad_rate_bias, grad_taps = prep_back(
        (grad_local, grad_query, grad_transfer, grad_offset)
    )
    returned = shifted(grad_widened[:edge_rows], "seq", -1)
    grad_mixing = grad_widened[edge_rows:] + jnp.pad(returned, ((tok_rows - edge_rows, 0), (0, 0)))
    mixing_low = grad_mixing.astype(jnp.bfloat16)
    rate_low = grad_rate_act.astype(jnp.bfloat16)
    outgate_low = grad_outgate_act.astype(jnp.bfloat16)
    grad_mix = contract(normed1_low, mixing_low, 0, 0)
    grad_rates = contract(normed1_low, rate_low, 0, 0)
    grad_outgate = contract(normed1_low, outgate_low, 0, 0)
    normed1_part = (
        contract(mixing_low, w_mix, 1, 1)
        + contract(rate_low, w_rates, 1, 1)
        + contract(outgate_low, w_outgate, 1, 1)
    )
    grad_normed1, head_gain_sum = lax.psum((normed1_part, grad_head_gain), "head")
    grad_from_norm, grad_first_gain = first_back(grad_normed1)
    grad_input = grad_middle + grad_from_norm
    small = lax.psum((grad_taps, grad_log_rate, grad_rate_bias, head_gain_sum), "seq")
    summed = (
        lax.psum_scatter(grad_mix, "seq", scatter_dimension=0, tiled=True),
        lax.psum_scatter(grad_rates, "seq", scatter_dimension=0, tiled=True),
        lax.psum_scatter(grad_outgate, "seq", scatter_dimension=0, tiled=True),
        lax.psum_scatter(grad_out, "seq", scatter_dimension=1, tiled=True),
        lax.psum_scatter(grad_first_gain, "seq", scatter_dimension=0, tiled=True),
        lax.psum_scatter(grad_ffn, "seq", scatter_dimension=0, tiled=True),
        lax.psum_scatter(grad_down, "seq", scatter_dimension=1, tiled=True),
        lax.psum_scatter(grad_second_gain, "seq", scatter_dimension=0, tiled=True),
    )
    return (
        block_output,
        grad_input,
        summed[4],
        summed[0],
        small[0],
        summed[1],
        small[1],
        small[2],
        summed[2],
        small[3],
        summed[3],
        summed[7],
        summed[5],
        summed[6],
    )


def solution(mesh):
    return jax.shard_map(
        body,
        mesh=mesh,
        in_specs=(
            P("seq", None),
            P(),
            P(None, "head"),
            P(None, "head"),
            P(None, "head"),
            P("head"),
            P("head"),
            P(None, "head"),
            P(),
            P("head", None),
            P(),
            P(None, None, "head"),
            P("head", None),
            P("seq", None),
            P("seq"),
        ),
        out_specs=(
            P("seq", None),
            P("seq", None),
            P("seq"),
            P("seq", "head"),
            P(None, "head"),
            P("seq", "head"),
            P("head"),
            P("head"),
            P("seq", "head"),
            P(),
            P("head", "seq"),
            P("seq"),
            P("seq", None, "head"),
            P("head", "seq"),
        ),
        check_vma=False,
    )
```

profile of v0, /device:TPU:0, one launch (start us, length us, event | category | flops | bytes accessed | tf_op | source)
XLA Modules:
  0.0 1825.8 jit_solution(14227871845642374644)
XLA Ops:
  43.5 16.2 fusion.51
  76.6 8.0 fusion.216
  93.9 316.2 %custom-call.10 = f32[2,16,1,128,128]{3,4,2,1,0:T(8,128)} custom-call(f32[2,16,1,128,128]{4,3,2,1,0:T(8,128)} %get-tuple-element.672), custom_call_target="InvertDiagBlocksLowerTriangular" | custom-call | tf_op jit(solution)/shard_map/jvp(jit(_solve_triangular))/vmap(vmap())/triangular_solve | solution.py:118
  432.2 70.5 %while.66 = (s32[]{:T(128)}, f32[2,128,128]{1,2,0:T(8,128)S(1)}, f32[2,128,128]{1,2,0:T(8,128)S(1)}, f32[16,2,128,128]{2,3,1,0:T(8,128)}, f32[16,2,128,128]{2,3,...) while((s32[]{:T(128)}, f32[2,128,128]{1,2,0:T(8,128)S(1)}, ...), condition=%wide.region_5.6_spmd.clone, body=%wide.region_4.5_spmd.clone.sunk | while | flops 100761600 | bytes 2492012 | solution.py:157
  528.0 15.6 all-gather.9.cloned.1.call-done
  543.5 41.6 %all-gather.11.cloned.1.call-done = f32[16,128,128]{2,1,0:T(8,128)} async-done(((f32[2,128,128]{2,1,0:T(8,128)}), f32[16,128,128]{2,1,0:T(8,128)}) %all-gather.11.cloned.1.call-update) | async-done | bytes 1048592 | tf_op jit(solution)/shard_map/all_gather | solution.py:25
  585.2 16.8 while.67
  624.6 83.7 %all-reduce.30.cloned.1.call-done = f32[1024,1024]{1,0:T(8,128)} async-done(((f32[1024,1024]{1,0:T(8,128)}), f32[1024,1024]{1,0:T(8,128)}) %all-reduce.30.cloned.1.call-update) | async-done | bytes 4194320 | tf_op jit(solution)/shard_map/psum | solution.py:226
  727.9 23.5 %all-gather.13.cloned.1.call-done = f32[16,128,128]{2,1,0:T(8,128)} async-done(((f32[2,128,128]{2,1,0:T(8,128)}), f32[16,128,128]{2,1,0:T(8,128)}) %all-gather.13.cloned.1.call-update) | async-done | bytes 1048592 | tf_op jit(solution)/shard_map/all_gather | solution.py:25
  759.8 78.2 %all-reduce.32.cloned.1.call-done = f32[1024,1024]{1,0:T(8,128)} async-done(((f32[1024,1024]{1,0:T(8,128)}), f32[1024,1024]{1,0:T(8,128)}) %all-reduce.32.cloned.1.call-update) | async-done | bytes 4194320 | tf_op jit(solution)/shard_map/psum | solution.py:242
  881.5 17.2 pad.77
  913.2 9.0 while.68
  925.8 118.8 %while.65 = (s32[]{:T(128)}, f32[2,128,128]{1,2,0:T(8,128)S(1)}, f32[2,128,128]{1,2,0:T(8,128)S(1)}, f32[16,2,128,128]{3,2,1,0:T(8,128)}, f32[16,2,128,128]{2,3,...) while((s32[]{:T(128)}, f32[2,128,128]{1,2,0:T(8,128)S(1)}, ...), condition=%wide.region_18.19_spmd, body=%wide.region_17.18_spmd.sunk | while | flops 201424896 | bytes 3278993 | solution.py:157
  1074.6 7.6 multiply_select_fusion
  1129.8 16.7 multiply_reduce_fusion.2
  1169.1 8.3 add_add_fusion.2
  1191.6 9.2 fusion.102
  1217.2 115.1 %all-reduce.34.cloned.1.call-done = (f32[1024,1024]{1,0:T(8,128)}, f32[1024,1024]{1,0:T(8,128)}) async-done(((f32[1024,1024]{1,0:T(8,128)}, f32[1024,1024]{1,0:T(8,128)}), (f32[1024,1024]{1,0:T(8,128)}, f32[1024,1024]{1,0:T(8,128)})) %all-reduce.34.cloned.1.call-update) | async-done | bytes 8388624 | tf_op jit(solution)/shard_map/psum | solution.py:235
  1335.9 37.7 %all-reduce.24 = (f32[1024]{0:T(1024)S(1)}, f32[4,1280]{1,0:T(4,128)}, f32[2]{0:T(128)}, f32[2]{0:T(128)}, f32[128]{0:T(128)}, /*index=5*/f32[1024]{0:T(1024)S(1)}) all-reduce(f32[1024]{0:T(1024)S(1)} %get-tuple-element.571, f32[4,1280]{1,0:T(4,128)S(1)} %pad_add_fusion.6, ...), channel_id=6, replica_groups=mesh['seq'=8,'head'=4] {'seq'}, use_global_device_ids=true, to_apply=%region_33.34.clone | all-reduce | flops 7300 | bytes 58400
  1389.6 66.9 %reduce-scatter.13.cloned.1.call-done = f32[256,128]{1,0:T(8,128)} async-done(((f32[256,1024]{1,0:T(8,128)}), f32[256,128]{1,0:T(8,128)}) %reduce-scatter.13.cloned.1.call-update) | async-done | bytes 131088 | tf_op jit(solution)/shard_map/reduce_scatter | solution.py:280
  1456.5 66.5 %reduce-scatter.11.cloned.1.call-done = f32[128,256]{1,0:T(8,128)} async-done(((f32[1024,256]{1,0:T(8,128)}), f32[128,256]{1,0:T(8,128)}) %reduce-scatter.11.cloned.1.call-update) | async-done | bytes 131088 | tf_op jit(solution)/shard_map/reduce_scatter | solution.py:279
  1523.0 75.5 %reduce-scatter.17.cloned.1.call-done = f32[704,128]{1,0:T(8,128)} async-done(((f32[704,1024]{1,0:T(8,128)}), f32[704,128]{1,0:T(8,128)}) %reduce-scatter.17.cloned.1.call-update) | async-done | bytes 360464 | tf_op jit(solution)/shard_map/reduce_scatter | solution.py:283
  1598.5 113.6 %reduce-scatter.15.cloned.1.call-done = f32[128,2,704]{0,2,1:T(8,128)} async-done(((f32[1024,2,704]{0,2,1:T(8,128)}), f32[128,2,704]{0,2,1:T(8,128)}) %reduce-scatter.15.cloned.1.call-update) | async-done | bytes 720912 | tf_op jit(solution)/shard_map/reduce_scatter | solution.py:282
  1712.1 106.7 %reduce-scatter.7.cloned.1.call-done = f32[128,1280]{1,0:T(8,128)} async-done(((f32[1024,1280]{1,0:T(8,128)}), f32[128,1280]{1,0:T(8,128)}) %reduce-scatter.7.cloned.1.call-update) | async-done | bytes 655376 | tf_op jit(solution)/shard_map/reduce_scatter | solution.py:277
  (762 shorter events, 581.7 us)
Async XLA Ops:
  7.2 704.6 %copy-start = (bf16[1024,2,704]{0,2,1:T(8,128)(2,1)S(1)}, bf16[1024,2,704]{0,2,1:T(8,128)(2,1)}, u32[]{:S(2)}) copy-start(bf16[1024,2,704]{0,2,1:T(8,128)(2,1)} %param.34) | copy-start | bytes 8650756
  7.2 536.3 %all-gather.9.cloned.1.call-start = ((), (), s32[]{:S(2)}) async-start(), calls=%async_computation.14 | async-start | bytes 1179648 | tf_op jit(solution)/shard_map/all_gather | solution.py:25
  18.9 24.6 %collective-permute-start = (f32[3,1280]{1,0:T(4,128)}, f32[3,1280]{1,0:T(4,128)}, u32[]{:S(2)}, u32[]{:S(2)}) collective-permute-start(f32[3,1280]{1,0:T(4,128)} %slice.112), channel_id=1, source_target_pairs={{0,4},{4,8},{8,12},{12,16},{16,20},{20,24},{24,28},{1,5},{5,9},{9,... | collective-permute-start | bytes 46088 | tf_op jit(solution)/shard_map/ppermute | solution.py:20
  25.0 398.2 %copy-start.72 = (f32[128,128]{1,0:T(8,128)}, f32[128,128]{1,0:T(8,128)S(1)}, u32[]{:S(2)}) copy-start(f32[128,128]{1,0:T(8,128)S(1)} %get-tuple-element.696) | copy-start | bytes 196612
  42.0 369.1 %copy-start.90 = (f32[2,16,128]{2,1,0:T(8,128)}, f32[2,16,128]{2,1,0:T(8,128)S(1)}, u32[]{:S(2)}) copy-start(f32[2,16,128]{2,1,0:T(8,128)S(1)} %get-tuple-element.652) | copy-start | bytes 49156
  503.5 81.7 %all-gather.11.cloned.1.call-start = ((), (), s32[]{:S(2)}) async-start(), calls=%async_computation.15 | async-start | bytes 1179648 | tf_op jit(solution)/shard_map/all_gather | solution.py:25
  504.3 204.0 %all-reduce.30.cloned.1.call-start = ((), (), s32[]{:S(2)}) async-start(), calls=%async_computation.6 | async-start | bytes 8388608 | tf_op jit(solution)/shard_map/psum | solution.py:226
  623.8 127.6 %all-gather.13.cloned.1.call-start = ((), (), s32[]{:S(2)}) async-start(), calls=%async_computation.16 | async-start | bytes 1179648 | tf_op jit(solution)/shard_map/all_gather | solution.py:25
  624.5 213.5 %all-reduce.32.cloned.1.call-start = ((), (), s32[]{:S(2)}) async-start(), calls=%async_computation.7 | async-start | bytes 8388608 | tf_op jit(solution)/shard_map/psum | solution.py:242
  726.6 181.8 %all-gather.15.cloned.1.call-start = ((), (), s32[]{:S(2)}) async-start(), calls=%async_computation.17 | async-start | bytes 1179648 | tf_op jit(solution)/shard_map/all_gather | solution.py:25
  754.1 88.6 %copy-start.61 = (bf16[1024,1024]{1,0:T(8,128)(2,1)S(1)}, bf16[1024,1024]{1,0:T(8,128)(2,1)}, u32[]{:S(2)}) copy-start(bf16[1024,1024]{1,0:T(8,128)(2,1)} %param.36) | copy-start | bytes 6291460
  860.1 472.2 %all-reduce.34.cloned.1.call-start = ((), (), s32[]{:S(2)}) async-start(), calls=%async_computation.18 | async-start | bytes 16777216 | tf_op jit(solution)/shard_map/psum | solution.py:235
  925.8 118.8 %copy-start.78 = (f32[2,16,1,128]{3,2,1,0:T(1,128)S(1)}, f32[2,16,1,128]{3,2,1,0:T(1,128)}, u32[]{:S(2)}) copy-start(f32[2,16,1,128]{3,2,1,0:T(1,128)} %copy-done.77) | copy-start | bytes 49156
  1154.9 12.8 collective-permute-start.1
  1177.5 212.1 %reduce-scatter.9.cloned.1.call-start = ((), (), s32[]{:S(2)}) async-start(), calls=%async_computation.9 | async-start | bytes 36864 | tf_op jit(solution)/shard_map/reduce_scatter | solution.py:278
  1180.0 276.5 %reduce-scatter.13.cloned.1.call-start = ((), (), s32[]{:S(2)}) async-start(), calls=%async_computation.11 | async-start | bytes 1179648 | tf_op jit(solution)/shard_map/reduce_scatter | solution.py:280
  1184.1 339.0 %reduce-scatter.11.cloned.1.call-start = ((), (), s32[]{:S(2)}) async-start(), calls=%async_computation.10 | async-start | bytes 1179648 | tf_op jit(solution)/shard_map/reduce_scatter | solution.py:279
  1185.9 412.6 %reduce-scatter.17.cloned.1.call-start = ((), (), s32[]{:S(2)}) async-start(), calls=%async_computation.13 | async-start | bytes 3244032 | tf_op jit(solution)/shard_map/reduce_scatter | solution.py:283
  1191.3 520.8 %reduce-scatter.15.cloned.1.call-start = ((), (), s32[]{:S(2)}) async-start(), calls=%async_computation.12 | async-start | bytes 6488064 | tf_op jit(solution)/shard_map/reduce_scatter | solution.py:282
  1200.8 618.0 %reduce-scatter.7.cloned.1.call-start = ((), (), s32[]{:S(2)}) async-start(), calls=%async_computation.8 | async-start | bytes 5898240 | tf_op jit(solution)/shard_map/reduce_scatter | solution.py:277
  1208.2 124.1 %copy-start.12 = (bf16[1024,1024]{1,0:T(8,128)(2,1)S(1)}, bf16[1024,1024]{1,0:T(8,128)(2,1)}, u32[]{:S(2)}) copy-start(bf16[1024,1024]{1,0:T(8,128)(2,1)} %param.23) | copy-start | bytes 6291460
  1208.2 124.1 %copy-start.104 = (f32[1024]{0:T(1024)S(1)}, f32[1024]{0:T(1024)}, u32[]{:S(2)}) copy-start(f32[1024]{0:T(1024)} %copy-done.103) | copy-start | bytes 12292
  1208.2 124.1 %copy-start.106 = (f32[1024]{0:T(1024)S(1)}, f32[1024]{0:T(1024)}, u32[]{:S(2)}) copy-start(f32[1024]{0:T(1024)} %copy-done.105) | copy-start | bytes 12292
  1382.1 436.8 %copy-start.1 = (bf16[1024,2,704]{0,2,1:T(8,128)(2,1)S(1)}, bf16[1024,2,704]{0,2,1:T(8,128)(2,1)}, u32[]{:S(2)}) copy-start(bf16[1024,2,704]{0,2,1:T(8,128)(2,1)} %param.34) | copy-start | bytes 8650756
  (122 other events, 779.4 us)
Sparse Core Ops, SparseCore 0:
  503.6 39.9 all-gather.8
  546.2 38.8 all-gather.10
  624.0 84.2 all-reduce.29
  711.0 40.3 all-gather.12
  753.7 84.2 all-reduce.31
  860.2 40.3 all-gather.14
  1177.6 154.6 all-reduce.33
  1336.0 53.5 reduce-scatter.8
  1393.6 62.8 reduce-scatter.12
  1460.7 62.2 reduce-scatter.10
  1527.2 71.2 reduce-scatter.16
  1602.6 109.5 reduce-scatter.14
  1716.3 102.5 reduce-scatter.6
where the time goes:
time: 1840 us; the launch traced here: 1830 us
  waiting for transfers between devices  792 us (43%)
  other arithmetic  437 us (24%)
  matrix products  351 us (19%)
  local copies, waits for them, and re-layouts  174 us (9%)
  blocking collectives  44.5 us (2%)
    another operation x5, other arithmetic, prepare(): jax.scipy.linalg.solve_triangular(system, right_side, lower=True, unit_di...  323 us
    psum x1, waiting for transfers between devices, body(): lax.psum(jnp.dot(activ_low, w_down, preferred_element_type=jnp.float32),...  115 us
    reduce_scatter x1, waiting for transfers between devices, body(): lax.psum_scatter(grad_ffn, 'seq', scatter_dimension=0, tiled=True)  114 us
    reduce_scatter x1, waiting for transfers between devices, body(): lax.psum_scatter(grad_mix, 'seq', scatter_dimension=0, tiled=True)  107 us
    psum x1, waiting for transfers between devices, body(): lax.psum(jnp.dot(gated_low, w_out, preferred_element_type=jnp.float32), '...  83.7 us
    all_gather x4, waiting for transfers between devices, prefix(): pieces = jax.tree.map(lambda part: lax.all_gather(part, axis), value)  80.7 us
    dot_general x62, matrix products, chain(): jnp.einsum('hij,hjk->hik', earlier[1], later[0], precision=HIGH_ACCURACY)  78.3 us
    psum x1, waiting for transfers between devices, body(): grad_normed2 = lax.psum(contract(grad_both, ffn_flat, 1, 1), 'head')  78.2 us
  transfers between devices with their start and end apart: 15, of which 12 were waited for; matrix products, arithmetic and copies ran while one was open for 9% of the time, Pallas kernels for 0%

commit v1 on v0

v1 whole, which is shorter than its diff:
```python
from functools import partial

import jax
import jax.numpy as jnp
from jax import lax
from jax.experimental import pallas as pl
from jax.experimental.pallas import tpu as pltpu
from jax.sharding import PartitionSpec as P

STEPS = 2
CONV = 4
SPAN = 64
EDGE = 8
LANES = 128
GROUPS = 1 + 2 * STEPS
PACK = 2
DOCS = 4
EPSILON = 1e-06
VMEM_LIMIT = 56 * 1024 * 1024

F32 = jnp.float32
BF16 = jnp.bfloat16
NN = (1, 0)
NT = (1, 1)
TN = (0, 0)


def dot1(left, right, dims):
    return lax.dot_general(
        left.astype(BF16),
        right.astype(BF16),
        (((dims[0],), (dims[1],)), ((), ())),
        preferred_element_type=F32,
    )


def halves(value):
    high = value.astype(BF16)
    return high, (value - high.astype(F32)).astype(BF16)


def dot3(left, right, dims):
    left_high, left_low = halves(left)
    right_high, right_low = halves(right)
    return dot1(
        jnp.concatenate([left_high, left_low, left_high], dims[0]),
        jnp.concatenate([right_high, right_high, right_low], dims[1]),
        dims,
    )


def iota(shape, dim):
    return lax.broadcasted_iota(jnp.int32, shape, dim)


def twice(value):
    return jnp.concatenate([value, value], 0)


def spread(column):
    return jnp.broadcast_to(column, (column.shape[0], LANES))


def crossing(place, reach, offset):
    return (place < offset) & (offset <= place + reach)


def rate_parts(raw, rate_row, bias_row):
    shifted_raw = raw + bias_row
    soft = jnp.maximum(shifted_raw, 0.0) + jnp.log1p(jnp.exp(-jnp.abs(shifted_raw)))
    slope = -jnp.exp(rate_row)
    return jax.nn.sigmoid(raw), slope * soft, slope * jax.nn.sigmoid(shifted_raw)


def decay_parts(cumul, begin, offset):
    place = begin + iota(cumul.shape, 0)
    inside = offset >= begin
    carried = jnp.where(inside & (place >= offset), 0.0, jnp.exp(cumul))
    cut = (place < offset) & (offset <= begin + (SPAN - 1))
    tail = jnp.exp(jnp.where(cut, -1e30, cumul[SPAN - 1 :] - cumul))
    return carried, tail


def decay_ratio(cumul, begin, offset):
    across = jnp.transpose(twice(cumul))[:SPAN]
    row = iota(across.shape, 0)
    col = iota(across.shape, 1) & (SPAN - 1)
    cut = (begin + col < offset) & (offset <= begin + row)
    return jnp.exp(jnp.where((col <= row) & jnp.logical_not(cut), cumul - across, -1e30))


def strict_mask():
    shape = (STEPS * SPAN, STEPS * SPAN)
    row, col = iota(shape, 0), iota(shape, 1)
    row_tok, col_tok = row & (SPAN - 1), col & (SPAN - 1)
    strict = (col_tok < row_tok) | ((col_tok == row_tok) & (col < row))
    return strict, row_tok ^ col_tok, (row == col).astype(F32)


def local_kernel(
    heads,
    offset_ref,
    edge_ref,
    halo_ref,
    mix_ref,
    taps_ref,
    rates_ref,
    rate_row_ref,
    bias_row_ref,
    conv_ref,
    q_ref,
    k_ref,
    x_ref,
    n_ref,
    cumul_ref,
    u_ref,
    w_ref,
    score_ref,
    query_ref,
    prefix_ref,
    phi_ref,
    total_ref,
    run_ref,
):
    step = pl.program_id(0)
    rows = mix_ref.shape[0]
    offset = offset_ref[0]
    width = LANES
    strict, apart, eye = strict_mask()

    @pl.when(step == 0)
    def _():
        run_ref[...] = jnp.concatenate([jnp.broadcast_to(eye, run_ref.shape[:2] + (width,)), jnp.zeros(run_ref.shape[:2] + (width,), F32)], 2)

    place = step * rows + iota((rows, width), 0)
    keep = [1.0 - crossing(place - back, back, offset).astype(F32) for back in range(CONV)]
    acts = []
    for part in range(heads * GROUPS):
        cols = slice(part * width, (part + 1) * width)
        before = jnp.where(step == 0, edge_ref[:, cols], halo_ref[:, cols])
        wide = jnp.concatenate([before, mix_ref[:, cols]], 0)
        conv = taps_ref[CONV - 1 : CONV, cols] * wide[EDGE:]
        for back in range(1, CONV):
            moved = pltpu.roll(wide, back, 0)[EDGE:]
            conv = conv + taps_ref[CONV - 1 - back : CONV - back, cols] * (moved * keep[back])
        conv_ref[:, cols] = conv
        act = conv * jax.nn.sigmoid(conv)
        if 1 <= part % GROUPS < 1 + STEPS:
            act = act * lax.rsqrt(jnp.sum(act * act, -1, keepdims=True) + EPSILON)
        acts.append(act)

    beta_all, decay_all, _ = rate_parts(rates_ref[...], rate_row_ref[...], bias_row_ref[...])
    lower = (iota((SPAN, SPAN), 1) <= iota((SPAN, SPAN), 0)).astype(F32)
    chains = [(pos, head) for pos in range(rows // SPAN) for head in range(heads)]
    cumuls = [
        jnp.dot(
            lower,
            decay_all[pos * SPAN : (pos + 1) * SPAN],
            precision=lax.Precision.HIGHEST,
            preferred_element_type=F32,
        )
        for pos in range(rows // SPAN)
    ]
    queries, keys, scaleds, tails, carries, ratios, systems = [], [], [], [], [], [], []
    for pos, head in chains:
        here = slice(pos * SPAN, (pos + 1) * SPAN)
        begin = step * rows + pos * SPAN
        query, key1, key2, value1, value2 = (
            act[here] for act in acts[head * GROUPS : (head + 1) * GROUPS]
        )
        key = jnp.concatenate([key1, key2], 0)
        value = jnp.concatenate([value1, value2], 0)
        lane = head * (STEPS + 1)
        beta = jnp.concatenate(
            [spread(beta_all[here, lane + sub : lane + sub + 1]) for sub in range(STEPS)], 0
        )
        cumul = spread(cumuls[pos][:, lane + STEPS : lane + STEPS + 1])
        cumul_ref[head, pos] = cumul
        carried, tail = decay_parts(cumul, begin, offset)
        ratio = decay_ratio(cumul, begin, offset)
        key_low = key.astype(BF16)
        q_ref[head, pos] = query
        k_ref[head, pos] = key_low
        queries.append(query)
        keys.append(key)
        tails.append(twice(tail))
        carries.append(carried)
        ratios.append(ratio)
        scaleds.append(jnp.concatenate([beta * value, beta * twice(carried) * key], 1))
        systems.append(jnp.where(strict, beta * twice(ratio), 0.0) * dot1(key_low, key_low, NT))
    inverses = [eye - jnp.where(apart == 0, system, 0.0) for system in systems]
    for level in range(SPAN.bit_length() - 1):
        off_blocks = [jnp.where((apart >> level) == 1, system, 0.0) for system in systems]
        lows = [inverse.astype(BF16) for inverse in inverses]
        halfway = [dot1(low, off, NN) for low, off in zip(lows, off_blocks)]
        inverses = [
            inverse - dot1(half, low, NN) for inverse, half, low in zip(inverses, halfway, lows)
        ]
    solveds = [dot3(inverse, scaled, NN) for inverse, scaled in zip(inverses, scaleds)]
    all_scores = [ratio * dot3(query, key, NT) for ratio, query, key in zip(ratios, queries, keys)]
    all_maps = [
        dot3(
            key,
            jnp.concatenate([tail * solved[:, width:], tail * solved[:, :width]], 1),
            TN,
        )
        for key, tail, solved in zip(keys, tails, solveds)
    ]
    inner = [dot1(scores, solved[:, width:], NN) for scores, solved in zip(all_scores, solveds)]
    for index, (pos, head) in enumerate(chains):
        solved, maps, carried = solveds[index], all_maps[index], carries[index]
        phi = carried[SPAN - 1 :] * eye - maps[:, :width]
        x_ref[head, pos] = inverses[index].astype(BF16)
        n_ref[head, pos] = systems[index].astype(BF16)
        u_ref[head, pos] = solved[:, :width]
        w_ref[head, pos] = solved[:, width:]
        score_ref[head, pos] = all_scores[index]
        query_ref[head, pos] = carried * queries[index] - inner[index]
        phi_ref[head, pos] = phi
        run = run_ref[head]
        prefix_ref[head, pos] = run
        moved_run = dot3(phi, run, NN)
        run_ref[head] = jnp.concatenate(
            [moved_run[:, :width], moved_run[:, width:] + maps[:, width:]], 1
        )
    total_ref[...] = run_ref[...]


def specs_of(heads, pack):
    def per_block(*dims):
        return pl.BlockSpec((heads, pack) + dims, lambda g: (0, g) + (0,) * len(dims))

    return per_block


def whole(shape):
    return pl.BlockSpec(shape, lambda g: (0,) * len(shape))


SCALARS = pl.BlockSpec(memory_space=pltpu.SMEM)


def params():
    return pltpu.CompilerParams(vmem_limit_bytes=VMEM_LIMIT)


def local_maps(offset, edge, mixing, taps, rates, rate_row, bias_row):
    rows, columns = mixing.shape
    width = LANES
    heads = columns // (GROUPS * width)
    blocks = rows // SPAN
    virt = STEPS * SPAN
    tile = PACK * SPAN
    per_block = specs_of(heads, PACK)
    saved = [
        (per_block(SPAN, width), (SPAN, width), F32),
        (per_block(virt, width), (virt, width), BF16),
        (per_block(virt, virt), (virt, virt), BF16),
        (per_block(virt, virt), (virt, virt), BF16),
        (per_block(SPAN, width), (SPAN, width), F32),
        (per_block(virt, width), (virt, width), F32),
        (per_block(virt, width), (virt, width), F32),
        (per_block(SPAN, virt), (SPAN, virt), F32),
        (per_block(SPAN, width), (SPAN, width), F32),
        (per_block(width, 2 * width), (width, 2 * width), F32),
        (per_block(width, width), (width, width), F32),
    ]
    return pl.pallas_call(
        partial(local_kernel, heads),
        grid=(blocks // PACK,),
        in_specs=[
            SCALARS,
            whole((EDGE, columns)),
            pl.BlockSpec((EDGE, columns), lambda g: (jnp.maximum(g * (tile // EDGE) - 1, 0), 0)),
            pl.BlockSpec((tile, columns), lambda g: (g, 0)),
            whole(taps.shape),
            pl.BlockSpec((tile, LANES), lambda g: (g, 0)),
            whole((1, LANES)),
            whole((1, LANES)),
        ],
        out_specs=[pl.BlockSpec((tile, columns), lambda g: (g, 0))]
        + [spec for spec, _, _ in saved]
        + [whole((heads, width, 2 * width))],
        out_shape=[jax.ShapeDtypeStruct((rows, columns), F32)]
        + [jax.ShapeDtypeStruct((heads, blocks) + dims, kind) for _, dims, kind in saved]
        + [jax.ShapeDtypeStruct((heads, width, 2 * width), F32)],
        scratch_shapes=[pltpu.VMEM((heads, width, 2 * width), F32)],
        compiler_params=params(),
        name="local_maps",
    )(offset, edge, mixing, mixing, taps, rates, rate_row, bias_row)


def output_kernel(
    heads,
    offset_ref,
    incoming_ref,
    prefix_ref,
    u_ref,
    w_ref,
    score_ref,
    q_ref,
    cumul_ref,
    outgate_ref,
    gain_ref,
    state_ref,
    fresh_ref,
    mixed_ref,
    gated_ref,
):
    step = pl.program_id(0)
    pack = prefix_ref.shape[1]
    width = LANES
    offset = offset_ref[0]
    chains = [(pos, head) for pos in range(pack) for head in range(heads)]
    states = [
        dot3(prefix_ref[head, pos, :, :width], incoming_ref[head], NN)
        + prefix_ref[head, pos, :, width:]
        for pos, head in chains
    ]
    freshes = [
        u_ref[head, pos] - dot3(w_ref[head, pos], state, NN)
        for (pos, head), state in zip(chains, states)
    ]
    outs = []
    for (pos, head), state, fresh in zip(chains, states, freshes):
        carried, _ = decay_parts(cumul_ref[head, pos], (step * pack + pos) * SPAN, offset)
        outs.append(
            dot3(
                jnp.concatenate([carried * q_ref[head, pos], score_ref[head, pos]], 1),
                jnp.concatenate([state, fresh], 0),
                NN,
            )
        )
    for (pos, head), state, fresh, mixed in zip(chains, states, freshes, outs):
        here = slice(pos * SPAN, (pos + 1) * SPAN)
        cols = slice(head * width, (head + 1) * width)
        state_ref[head, pos] = state.astype(BF16)
        fresh_ref[head, pos] = fresh.astype(BF16)
        mixed_ref[here, cols] = mixed
        scale = lax.rsqrt(jnp.mean(mixed * mixed, -1, keepdims=True) + EPSILON)
        outgate = outgate_ref[here, cols]
        gated = mixed * scale * gain_ref[...] * (outgate * jax.nn.sigmoid(outgate))
        gated_ref[here, cols] = gated.astype(BF16).astype(gated_ref.dtype)


def outputs_of(offset, incoming, saved, outgate, gain, gated_type):
    prefix, u, w, scores, q, cumul = saved
    heads, blocks = prefix.shape[:2]
    width = LANES
    virt = STEPS * SPAN
    tile = PACK * SPAN
    rows = outgate.shape[0]
    per_block = specs_of(heads, PACK)
    flat = pl.BlockSpec((tile, heads * width), lambda g: (g, 0))
    return pl.pallas_call(
        partial(output_kernel, heads),
        grid=(blocks // PACK,),
        in_specs=[
            SCALARS,
            whole((heads, width, width)),
            per_block(width, 2 * width),
            per_block(virt, width),
            per_block(virt, width),
            per_block(SPAN, virt),
            per_block(SPAN, width),
            per_block(SPAN, width),
            flat,
            whole((1, width)),
        ],
        out_specs=[per_block(width, width), per_block(virt, width), flat, flat],
        out_shape=[
            jax.ShapeDtypeStruct((heads, blocks, width, width), BF16),
            jax.ShapeDtypeStruct((heads, blocks, virt, width), BF16),
            jax.ShapeDtypeStruct((rows, heads * width), F32),
            jax.ShapeDtypeStruct((rows, heads * width), gated_type),
        ],
        compiler_params=params(),
        name="mixer_outputs",
    )(offset, incoming, prefix, u, w, scores, q, cumul, outgate, gain)


def gate_back_kernel(
    heads,
    grad_ref,
    mixed_ref,
    outgate_ref,
    gain_ref,
    query_ref,
    prefix_ref,
    grad_mixed_ref,
    grad_outgate_ref,
    grad_gain_ref,
    term_ref,
    total_ref,
):
    step = pl.program_id(0)
    pack = prefix_ref.shape[1]
    width = LANES

    @pl.when(step == 0)
    def _():
        grad_gain_ref[...] = jnp.zeros_like(grad_gain_ref)
        total_ref[...] = jnp.zeros_like(total_ref)

    for head in range(heads):
        cols = slice(head * width, (head + 1) * width)
        mixed = mixed_ref[:, cols]
        outgate = outgate_ref[:, cols]
        grad = grad_ref[:, cols]
        gain = gain_ref[...]
        scale = lax.rsqrt(jnp.mean(mixed * mixed, -1, keepdims=True) + EPSILON)
        normed = mixed * scale
        sigma = jax.nn.sigmoid(outgate)
        silu = outgate * sigma
        grad_outgate = grad * normed * gain * (sigma * (1.0 + outgate * (1.0 - sigma)))
        grad_outgate_ref[:, cols] = grad_outgate.astype(BF16)
        through = grad * silu
        product = through * normed
        grad_gain_ref[...] += jnp.sum(product.reshape(-1, 8, width), 0)
        grad_normed = through * gain
        grad_mixed = scale * (
            grad_normed - normed * jnp.mean(grad_normed * normed, -1, keepdims=True)
        )
        grad_low = grad_mixed.astype(BF16)
        grad_mixed_ref[:, cols] = grad_low
        total = total_ref[head]
        for pos in range(pack):
            here = slice(pos * SPAN, (pos + 1) * SPAN)
            term = dot3(query_ref[head, pos], grad_mixed[here], TN)
            term_ref[head, pos] = term
            total = total + dot3(prefix_ref[head, pos], term, TN)
        total_ref[head] = total


def gate_back(grad, mixed, outgate, gain, query, prefix):
    heads, blocks = prefix.shape[:2]
    width = LANES
    tile = PACK * SPAN
    rows = mixed.shape[0]
    per_block = specs_of(heads, PACK)
    flat = pl.BlockSpec((tile, heads * width), lambda g: (g, 0))
    return pl.pallas_call(
        partial(gate_back_kernel, heads),
        grid=(blocks // PACK,),
        in_specs=[flat, flat, flat, whole((1, width)), per_block(SPAN, width), per_block(width, width)],
        out_specs=[
            flat,
            flat,
            whole((8, width)),
            per_block(width, width),
            whole((heads, width, width)),
        ],
        out_shape=[
            jax.ShapeDtypeStruct((rows, heads * width), BF16),
            jax.ShapeDtypeStruct((rows, heads * width), BF16),
            jax.ShapeDtypeStruct((8, width), F32),
            jax.ShapeDtypeStruct((heads, blocks, width, width), F32),
            jax.ShapeDtypeStruct((heads, width, width), F32),
        ],
        compiler_params=params(),
        name="gate_back",
    )(grad, mixed, outgate, gain, query, prefix)


def back_kernel(
    heads,
    offset_ref,
    leaving_ref,
    term_ref,
    phi_ref,
    state_ref,
    fresh_ref,
    grad_ref,
    score_ref,
    x_ref,
    n_ref,
    cumul_ref,
    q_ref,
    k_ref,
    rates_ref,
    rate_row_ref,
    bias_row_ref,
    conv_ref,
    edge_ref,
    halo_ref,
    mix_ref,
    taps_ref,
    grad_mix_ref,
    last_ref,
    before_ref,
    grad_rates_ref,
    decay_sum_ref,
    grad_taps_ref,
    run_ref,
    next_ref,
    act_ref,
):
    step = pl.program_id(0)
    steps = pl.num_programs(0)
    group = steps - 1 - step
    rows = mix_ref.shape[0]
    offset = offset_ref[0]
    width = LANES
    virt = STEPS * SPAN
    strict, _, _ = strict_mask()
    lane = iota((SPAN, width), 1)

    @pl.when(step == 0)
    def _():
        run_ref[...] = leaving_ref[...]
        next_ref[...] = jnp.zeros_like(next_ref)
        decay_sum_ref[...] = jnp.zeros_like(decay_sum_ref)
        grad_taps_ref[...] = jnp.zeros_like(grad_taps_ref)

    tok_row, tok_col = iota((SPAN, SPAN), 0), iota((SPAN, SPAN), 1)
    later = (tok_col >= tok_row).astype(BF16)
    earlier = tok_col < tok_row
    sums = jnp.concatenate([later, earlier.astype(BF16)], 1)
    beta_all, decay_all, slope_all = rate_parts(
        rates_ref[...], rate_row_ref[...], bias_row_ref[...]
    )
    chains = [(pos, head) for pos in reversed(range(rows // SPAN)) for head in range(heads)]
    leavings = []
    for pos, head in chains:
        leaving = run_ref[head]
        leavings.append(leaving)
        run_ref[head] = dot3(phi_ref[head, pos], leaving, TN) + term_ref[head, pos]
    betas, parts_of, ratios, masked = [], [], [], []
    for pos, head in chains:
        here = slice(pos * SPAN, (pos + 1) * SPAN)
        begin = group * rows + pos * SPAN
        first_lane = head * (STEPS + 1)
        beta = jnp.concatenate(
            [
                spread(beta_all[here, first_lane + sub : first_lane + sub + 1])
                for sub in range(STEPS)
            ],
            0,
        )
        cumul = cumul_ref[head, pos]
        betas.append(beta)
        parts_of.append(decay_parts(cumul, begin, offset))
        ratio = decay_ratio(cumul, begin, offset)
        ratios.append(ratio)
        masked.append(jnp.where(strict, beta * twice(ratio), 0.0))
    lows = [leaving.astype(BF16) for leaving in leavings]
    grads = [
        grad_ref[pos * SPAN : (pos + 1) * SPAN, head * width : (head + 1) * width]
        for pos, head in chains
    ]
    scores_low = [score_ref[head, pos].astype(BF16) for pos, head in chains]
    states = [state_ref[head, pos] for pos, head in chains]
    freshes = [fresh_ref[head, pos] for pos, head in chains]
    queries = [q_ref[head, pos] for pos, head in chains]
    keys = [k_ref[head, pos] for pos, head in chains]
    key_leavings = [
        twice(tail) * dot1(key, low, NN) for key, low, (_, tail) in zip(keys, lows, parts_of)
    ]
    grad_freshes = [
        dot1(scores, grad, TN) + key_leaving
        for scores, grad, key_leaving in zip(scores_low, grads, key_leavings)
    ]
    solveds = [
        dot1(x_ref[head, pos], grad_fresh, TN)
        for (pos, head), grad_fresh in zip(chains, grad_freshes)
    ]
    scaleds = [beta * solved for beta, solved in zip(betas, solveds)]
    grad_scores = [dot1(grad, fresh, NT) for grad, fresh in zip(grads, freshes)]
    grad_systems = [-dot1(solved, fresh, NT) for solved, fresh in zip(solveds, freshes)]
    grad_states = [
        carried * dot1(grad, state, NT)
        for grad, state, (carried, _) in zip(grads, states, parts_of)
    ]
    scaled_states = [
        twice(carried) * dot1(scaled, state, NT)
        for scaled, state, (carried, _) in zip(scaleds, states, parts_of)
    ]
    boths = [
        jnp.concatenate([grad_score * ratio, grad_system * mask], 0).astype(BF16)
        for grad_score, ratio, grad_system, mask in zip(grad_scores, ratios, grad_systems, masked)
    ]
    from_keys = [dot1(both, key, NN) for both, key in zip(boths, keys)]
    to_keys = [
        dot1(both, jnp.concatenate([query.astype(BF16), key], 0), TN)
        for both, query, key in zip(boths, queries, keys)
    ]
    from_leavings = [
        twice(tail) * dot1(fresh, low, NT) for fresh, low, (_, tail) in zip(freshes, lows, parts_of)
    ]
    all_pairs = []
    for index, (pos, head) in enumerate(chains):
        system_pairs = grad_systems[index] * n_ref[head, pos].astype(F32)
        pairs = grad_scores[index] * score_ref[head, pos]
        pairs = pairs + system_pairs[:SPAN] + system_pairs[SPAN:]
        all_pairs.append(pairs[:, :SPAN] + pairs[:, SPAN:])
    crossed = [jnp.where(earlier, dot1(later, pairs, NN), 0.0) for pairs in all_pairs]
    all_ends = []
    for index, (pos, head) in enumerate(chains):
        read = scaled_states[index] * keys[index].astype(F32)
        arriving = grad_states[index] * queries[index] - read[:SPAN] - read[SPAN:]
        written = key_leavings[index] * freshes[index].astype(F32)
        written = written[:SPAN] + written[SPAN:]
        all_ends.append(dot1(sums, jnp.concatenate([arriving, written], 0), NN))
    rates_of = [jnp.zeros((SPAN, width), F32) for _ in range(rows // SPAN)]
    for index, (pos, head) in enumerate(chains):
        here = slice(pos * SPAN, (pos + 1) * SPAN)
        first_lane = head * (STEPS + 1)
        grad_query = from_keys[index][:SPAN] + grad_states[index]
        grad_key = (
            from_keys[index][SPAN:]
            - scaled_states[index]
            + to_keys[index]
            + from_leavings[index]
        )
        scaled = scaleds[index]
        for place_of, part in enumerate(
            (grad_query, grad_key[:SPAN], grad_key[SPAN:], scaled[:SPAN], scaled[SPAN:])
        ):
            at = (head * GROUPS + place_of) * width
            act_ref[here, at : at + width] = part
        fresh = freshes[index].astype(F32)
        step_part = (1.0 - betas[index]) * jnp.sum(solveds[index] * fresh, -1, keepdims=True)
        kept = parts_of[index][0][SPAN - 1 :] * jnp.sum(
            leavings[index] * states[index].astype(F32), 0, keepdims=True
        )
        grad_decay = jnp.sum(crossed[index], -1, keepdims=True) + jnp.sum(
            all_ends[index] + kept, -1, keepdims=True
        )
        for sub in range(STEPS):
            rates_of[pos] = jnp.where(
                lane == first_lane + sub,
                step_part[sub * SPAN : (sub + 1) * SPAN],
                rates_of[pos],
            )
        rates_of[pos] = jnp.where(lane == first_lane + STEPS, spread(grad_decay), rates_of[pos])
    is_decay = lane % (STEPS + 1) == STEPS
    for pos, grad_rates in enumerate(rates_of):
        here = slice(pos * SPAN, (pos + 1) * SPAN)
        decay_part = jnp.where(is_decay, grad_rates * decay_all[here], 0.0)
        grad_rates = jnp.where(is_decay, grad_rates * slope_all[here], grad_rates)
        grad_rates_ref[here] = grad_rates.astype(BF16)
        decay_sum_ref[0:1] += jnp.sum(decay_part, 0, keepdims=True)
        decay_sum_ref[1:2] += jnp.sum(jnp.where(is_decay, grad_rates, 0.0), 0, keepdims=True)

    place = group * rows + iota((rows, width), 0)
    keep_back = [1.0 - crossing(place - back, back, offset).astype(F32) for back in range(CONV)]
    keep_fore = [1.0 - crossing(place, fore, offset).astype(F32) for fore in range(CONV)]
    edge_place = iota((EDGE, width), 0) - EDGE
    keep_edge = [1.0 - crossing(edge_place, fore, offset).astype(F32) for fore in range(CONV)]
    for part in range(heads * GROUPS):
        cols = slice(part * width, (part + 1) * width)
        conv = conv_ref[:, cols]
        grad = act_ref[:, cols]
        sigma = jax.nn.sigmoid(conv)
        if 1 <= part % GROUPS < 1 + STEPS:
            act = conv * sigma
            scale = lax.rsqrt(jnp.sum(act * act, -1, keepdims=True) + EPSILON)
            unit = act * scale
            grad = scale * (grad - unit * jnp.sum(unit * grad, -1, keepdims=True))
        grad_conv = grad * (sigma * (1.0 + conv * (1.0 - sigma)))
        wide = jnp.concatenate([grad_conv, next_ref[:, cols]], 0)
        before = jnp.concatenate([jnp.zeros((EDGE, width), F32), grad_conv[:EDGE]], 0)
        above = jnp.where(group == 0, edge_ref[:, cols], halo_ref[:, cols])
        mix_wide = jnp.concatenate([above, mix_ref[:, cols]], 0)
        tap = taps_ref[CONV - 1 : CONV, cols]
        grad_mix = tap * grad_conv
        grad_before = jnp.zeros((EDGE, width), F32)
        sums_of = jnp.sum(grad_conv * mix_wide[EDGE:], 0, keepdims=True)
        grad_taps_ref[CONV - 1 : CONV, cols] += sums_of
        for shift in range(1, CONV):
            tap = taps_ref[CONV - 1 - shift : CONV - shift, cols]
            moved = pltpu.roll(wide, rows + EDGE - shift, 0)[:rows]
            grad_mix = grad_mix + tap * (moved * keep_fore[shift])
            moved = pltpu.roll(before, 2 * EDGE - shift, 0)[:EDGE]
            grad_before = grad_before + tap * (moved * keep_edge[shift])
            moved = pltpu.roll(mix_wide, shift, 0)[EDGE:] * keep_back[shift]
            grad_taps_ref[CONV - 1 - shift : CONV - shift, cols] += jnp.sum(
                grad_conv * moved, 0, keepdims=True
            )
        next_ref[:, cols] = grad_conv[:EDGE]
        grad_mix_ref[:, cols] = grad_mix.astype(BF16)
        before_ref[:, cols] = grad_before

        @pl.when(step == 0)
        def _():
            last_ref[:, cols] = grad_mix[rows - 2 * EDGE :]


def recurrence_back(offset, leaving, saved, rates, rate_row, bias_row, conv, edge, mixing, taps):
    term, phi, state, fresh, grad, scores, x, n, cumul, q, k = saved
    rows, columns = mixing.shape
    heads, blocks = term.shape[:2]
    width = LANES
    virt = STEPS * SPAN
    tile = PACK * SPAN
    steps = blocks // PACK

    def per_block(*dims):
        return pl.BlockSpec(
            (heads, PACK) + dims, lambda g: (0, steps - 1 - g) + (0,) * len(dims)
        )

    def flat(size):
        return pl.BlockSpec((tile, size), lambda g: (steps - 1 - g, 0))

    return pl.pallas_call(
        partial(back_kernel, heads),
        grid=(steps,),
        in_specs=[
            SCALARS,
            whole((heads, width, width)),
            per_block(width, width),
            per_block(width, width),
            per_block(width, width),
            per_block(virt, width),
            flat(heads * width),
            per_block(SPAN, virt),
            per_block(virt, virt),
            per_block(virt, virt),
            per_block(SPAN, width),
            per_block(SPAN, width),
            per_block(virt, width),
            flat(LANES),
            whole((1, LANES)),
            whole((1, LANES)),
            flat(columns),
            whole((EDGE, columns)),
            pl.BlockSpec(
                (EDGE, columns),
                lambda g: (jnp.maximum((steps - 1 - g) * (tile // EDGE) - 1, 0), 0),
            ),
            flat(columns),
            whole(taps.shape),
        ],
        out_specs=[
            flat(columns),
            whole((2 * EDGE, columns)),
            whole((EDGE, columns)),
            flat(LANES),
            whole((8, LANES)),
            whole((8, columns)),
        ],
        out_shape=[
            jax.ShapeDtypeStruct((rows, columns), BF16),
            jax.ShapeDtypeStruct((2 * EDGE, columns), F32),
            jax.ShapeDtypeStruct((EDGE, columns), F32),
            jax.ShapeDtypeStruct((rows, LANES), BF16),
            jax.ShapeDtypeStruct((8, LANES), F32),
            jax.ShapeDtypeStruct((8, columns), F32),
        ],
        scratch_shapes=[
            pltpu.VMEM((heads, width, width), F32),
            pltpu.VMEM((EDGE, columns), F32),
            pltpu.VMEM((tile, columns), F32),
        ],
        compiler_params=params(),
        name="recurrence_back",
    )(
        offset, leaving, term, phi, state, fresh, grad, scores, x, n, cumul, q, k,
        rates, rate_row, bias_row, conv, edge, mixing, mixing, taps,
    )


def exchange(value, axis, bit):
    count = lax.axis_size(axis)
    return lax.ppermute(value, axis, [(place, place ^ bit) for place in range(count)])


def shifted(value, axis, steps):
    count = lax.axis_size(axis)
    first, last = (max(0, -steps), min(count, count - steps))
    return lax.ppermute(value, axis, [(source, source + steps) for source in range(first, last)])


def bits_of(axis):
    count = lax.axis_size(axis)
    return [1 << power for power in range(count.bit_length() - 1)]


def gather_near(value, axis):
    found = [value]
    for bit in reversed(bits_of(axis)):
        found = [found, [exchange(part, axis, bit) for part in found]]
        found = found[0] + found[1]
    order = [0]
    for bit in reversed(bits_of(axis)):
        order = order + [place ^ bit for place in order]
    return [part for _, part in sorted(zip(order, found), key=lambda pair: pair[0])]


def scatter_sum(pieces, axis):
    mine = lax.axis_index(axis)
    for bit in bits_of(axis):
        side = (mine // bit) % 2
        pairs = pieces.reshape((pieces.shape[0] // 2, 2) + pieces.shape[1:])
        kept = lax.dynamic_index_in_dim(pairs, side, 1, keepdims=False)
        sent = lax.dynamic_index_in_dim(pairs, 1 - side, 1, keepdims=False)
        pieces = kept + exchange(sent, axis, bit)
    return pieces[0]


def contract(left, right, left_dim, right_dim):
    return lax.dot_general(
        left, right, (((left_dim,), (right_dim,)), ((), ())), preferred_element_type=F32
    )


def carried_in(total, own, axis, backward):
    count = lax.axis_size(axis)
    sign = -1 if backward else 1
    reach = count - DOCS - 1
    if reach > DOCS - 1:
        reach = count - 1
    dims = (1, 1) if backward else (2, 1)

    def move(map_of, state):
        return lax.dot_general(
            map_of, state, (((dims[0],), (1,)), ((0,), (0,))), precision=lax.Precision.HIGHEST
        )

    if reach < count - 1:
        maps = [shifted(total, axis, sign * step) for step in range(1, reach)]
        terms = [shifted(own, axis, sign * step) for step in range(1, reach + 1)]
    else:
        every_map, every_term = lax.all_gather(total, axis), lax.all_gather(own, axis)
        mine = lax.axis_index(axis)

        def at(array, step):
            place = mine - sign * step
            picked = lax.dynamic_index_in_dim(array, jnp.clip(place, 0, count - 1), 0, False)
            return jnp.where((place >= 0) & (place < count), picked, 0.0)

        maps = [at(every_map, step) for step in range(1, reach)]
        terms = [at(every_term, step) for step in range(1, reach + 1)]
    state = terms[-1]
    for map_of, term in zip(reversed(maps), reversed(terms[:-1])):
        state = move(map_of, state) + term
    return state


def normalize(values):
    return values * lax.rsqrt(jnp.mean(values * values, -1, keepdims=True) + EPSILON)


def norm_back(values, gain, grad):
    scale = lax.rsqrt(jnp.mean(values * values, -1, keepdims=True) + EPSILON)
    normed = values * scale
    through = grad * gain
    back = scale * (through - normed * jnp.mean(through * normed, -1, keepdims=True))
    return back, jnp.sum(grad * normed, 0)


def lanes_of(per_head):
    row = jnp.repeat(per_head, STEPS + 1)
    return jnp.pad(row, (0, LANES - row.shape[0]))[None]


def place_rows(parts, axis):
    mine = lax.axis_index(axis)
    count = len(parts)
    rows = parts[0].shape[0]
    out = jnp.zeros((count * rows,) + parts[0].shape[1:], parts[0].dtype)
    for near, part in enumerate(parts):
        out = lax.dynamic_update_slice_in_dim(out, part, (mine ^ near) * rows, 0)
    return out


def project_kernel(parts, *refs):
    gated_refs, weight_refs = refs[:parts], refs[parts : 2 * parts]
    input_ref, gain_ref, middle_ref, normed_ref, low_ref = refs[2 * parts :]

    @pl.when(pl.program_id(0) == 0)
    def _():
        for part in range(parts):
            low_ref[part] = weight_refs[part][...].astype(BF16)

    middle = input_ref[...].astype(F32)
    for part in range(parts):
        middle = middle + dot1(gated_refs[part][...], low_ref[part], NN)
    middle_ref[...] = middle
    scale = lax.rsqrt(jnp.mean(middle * middle, -1, keepdims=True) + EPSILON)
    normed_ref[...] = (middle * scale * gain_ref[...]).astype(BF16)


def mixer_project(gated_near, weight_near, block_input, gain):
    parts = len(gated_near)
    rows, model = block_input.shape
    tile = rows // 4
    depth = gated_near[0].shape[1]
    return pl.pallas_call(
        partial(project_kernel, parts),
        grid=(rows // tile,),
        in_specs=[pl.BlockSpec((tile, depth), lambda g: (g, 0))] * parts
        + [whole((depth, model))] * parts
        + [pl.BlockSpec((tile, model), lambda g: (g, 0)), whole((1, model))],
        out_specs=[pl.BlockSpec((tile, model), lambda g: (g, 0))] * 2,
        out_shape=[
            jax.ShapeDtypeStruct((rows, model), F32),
            jax.ShapeDtypeStruct((rows, model), BF16),
        ],
        scratch_shapes=[pltpu.VMEM((parts, depth, model), BF16)],
        compiler_params=params(),
        name="mixer_project",
    )(*gated_near, *weight_near, block_input, gain)


def body(
    block_input,
    first_gain,
    w_mix,
    conv_taps,
    w_rates,
    log_rate,
    rate_bias,
    w_outgate,
    head_gain,
    w_out,
    second_gain,
    w_ffn,
    w_down,
    grad_output,
    seq_starts,
):
    rows, model = block_input.shape
    heads = log_rate.shape[0]
    parts = lax.axis_size("head")
    quarter = rows // parts
    head_index = lax.axis_index("head")
    gain1, gain2 = first_gain.astype(F32), second_gain.astype(F32)
    head_gain_row = head_gain.astype(F32)[None]
    taps = conv_taps.astype(F32)
    rate_row, bias_row = lanes_of(log_rate), lanes_of(rate_bias)
    rate_lanes = w_rates.shape[1]
    w_rates_wide = jnp.pad(w_rates, ((0, 0), (0, LANES - rate_lanes)))

    inputs_f = block_input.astype(F32)
    normed1_low = (normalize(inputs_f) * gain1).astype(BF16)
    mixing = contract(normed1_low, w_mix, 1, 0)
    edge = shifted(mixing[rows - EDGE :], "seq", 1)
    rates = contract(normed1_low, w_rates_wide, 1, 0)
    outgate = contract(normed1_low, w_outgate, 1, 0)
    w_out_near = gather_near(w_out.astype(F32), "head")

    conv, q, k, x, system, cumul, u, w, scores, query_map, prefix, phi, total = local_maps(
        seq_starts, edge, mixing, taps, rates, rate_row, bias_row
    )
    width = LANES
    device_map, device_term = total[..., :width], total[..., width:]
    incoming = carried_in(device_map, device_term, "seq", False)
    state, fresh, mixed, gated = outputs_of(
        seq_starts, incoming, (prefix, u, w, scores, q, cumul), outgate, head_gain_row, F32
    )
    gated_near = gather_near(gated, "head")
    middle, normed2_low = mixer_project(gated_near, w_out_near, block_input, gain2[None])
    ffn_flat = w_ffn.reshape(model, -1)
    hidden_units = ffn_flat.shape[1] // 2
    both = contract(normed2_low, ffn_flat, 1, 0)
    gate, up = both[:, :hidden_units], both[:, hidden_units:]
    sigma = jax.nn.sigmoid(gate)
    activ_low = (gate * sigma * up).astype(BF16)
    grad_activ = contract(grad_output, w_down, 1, 1)
    grad_gate = grad_activ * up * (sigma * (1.0 + gate * (1.0 - sigma)))
    grad_up = grad_activ * (gate * sigma)
    grad_both = jnp.concatenate([grad_gate, grad_up], 1).astype(BF16)
    normed2_part = contract(grad_both, ffn_flat, 1, 1)
    grad_normed2 = scatter_sum(normed2_part.reshape(parts, quarter, model), "head")

    own_rows = lambda array: lax.dynamic_slice_in_dim(array, head_index * quarter, quarter, 0)
    grad_middle_own, grad_second_gain = norm_back(own_rows(middle), gain2, grad_normed2)
    grad_middle_own = grad_middle_own + own_rows(grad_output).astype(F32)
    grad_middle = place_rows(gather_near(grad_middle_own, "head"), "head")
    grad_branch = grad_middle.astype(BF16)
    grad_gated = contract(grad_branch, w_out, 1, 1)
    grad_mixed, outgate_low, grad_gain, term, grad_total = gate_back(
        grad_gated, mixed, outgate, head_gain_row, query_map, prefix
    )
    leaving = carried_in(device_map, grad_total, "seq", True)

    ffn_out = lax.psum(contract(activ_low, w_down, 1, 0), "head")
    block_output = (middle + ffn_out).astype(BF16)
    grad_ffn = contract(normed2_low, grad_both, 0, 0)
    grad_down = contract(activ_low, grad_output, 0, 0)
    grad_out = contract(gated.astype(BF16), grad_branch, 0, 0)

    grad_mix_rows, last_rows, before_rows, rate_low, decay_sums, grad_taps = recurrence_back(
        seq_starts,
        leaving,
        (term, phi, state, fresh, grad_mixed, scores, x, system, cumul, q, k),
        rates,
        rate_row,
        bias_row,
        conv,
        edge,
        mixing,
        taps,
    )
    returned = shifted(before_rows, "seq", -1)
    last_rows = last_rows + jnp.pad(returned, ((EDGE, 0), (0, 0)))
    mixing_low = lax.dynamic_update_slice_in_dim(
        grad_mix_rows, last_rows.astype(BF16), rows - 2 * EDGE, 0
    )
    normed1_part = (
        contract(mixing_low, w_mix, 1, 1)
        + contract(rate_low, w_rates_wide, 1, 1)
        + contract(outgate_low, w_outgate, 1, 1)
    )
    grad_normed1 = scatter_sum(normed1_part.reshape(parts, quarter, model), "head")
    from_norm, grad_first_gain = norm_back(own_rows(inputs_f), gain1, grad_normed1)
    grad_input = place_rows(gather_near(grad_middle_own + from_norm, "head"), "head")
    grad_mix = contract(normed1_low, mixing_low, 0, 0)
    grad_rates = contract(normed1_low, rate_low, 0, 0)[:, :rate_lanes]
    grad_outgate = contract(normed1_low, outgate_low, 0, 0)

    seq = lax.axis_size("seq")
    seq_index = lax.axis_index("seq")
    split_rows = lambda array: array.reshape(seq, array.shape[0] // seq, array.shape[1])
    split_columns = lambda array: jnp.moveaxis(array.reshape(array.shape[0], seq, -1), 1, 0)
    ffn_sum = scatter_sum(split_rows(grad_ffn), "seq")
    down_sum = scatter_sum(split_columns(grad_down), "seq")
    out_sum = scatter_sum(split_columns(grad_out), "seq")
    mix_sum = scatter_sum(split_rows(grad_mix), "seq")
    outgate_sum = scatter_sum(split_rows(grad_outgate), "seq")
    rates_sum = lax.psum_scatter(grad_rates, "seq", scatter_dimension=0, tiled=True)
    taps_sum, decay_sum = lax.psum((grad_taps[:CONV], decay_sums[:2]), "seq")
    gains = lax.psum(
        (grad_first_gain, grad_second_gain, jnp.sum(grad_gain, 0)), ("seq", "head")
    )
    own_gain = lambda array: lax.dynamic_slice_in_dim(
        array, seq_index * (model // seq), model // seq, 0
    )
    decay_lanes = decay_sum[:, STEPS : heads * (STEPS + 1) : STEPS + 1]
    return (
        block_output,
        grad_input,
        own_gain(gains[0]),
        mix_sum,
        taps_sum,
        rates_sum,
        decay_lanes[0],
        decay_lanes[1],
        outgate_sum,
        gains[2],
        out_sum,
        own_gain(gains[1]),
        ffn_sum.reshape((-1,) + w_ffn.shape[1:]),
        down_sum,
    )


def solution(mesh):
    return jax.shard_map(
        body,
        mesh=mesh,
        in_specs=(
            P("seq", None),
            P(),
            P(None, "head"),
            P(None, "head"),
            P(None, "head"),
            P("head"),
            P("head"),
            P(None, "head"),
            P(),
            P("head", None),
            P(),
            P(None, None, "head"),
            P("head", None),
            P("seq", None),
            P("seq"),
        ),
        out_specs=(
            P("seq", None),
            P("seq", None),
            P("seq"),
            P("seq", "head"),
            P(None, "head"),
            P("seq", "head"),
            P("head"),
            P("head"),
            P("seq", "head"),
            P(),
            P("head", "seq"),
            P("seq"),
            P("seq", None, "head"),
            P("head", "seq"),
        ),
        check_vma=False,
    )
```

time: 1840 us -> 635 us (0.35)
  waiting for transfers between devices: 792 us -> 183 us
  other arithmetic: 437 us -> 44.6 us
  matrix products: 351 us -> 53.9 us
  local copies, waits for them, and re-layouts: 174 us -> 49.6 us
  blocking collectives: 44.5 us -> 137 us
  Pallas kernels: 0 us -> 87.4 us
  starting transfers between devices: 8.02 us -> 54.8 us
    reduce_scatter x5 -> x0, waiting for transfers between devices: 429 us -> none  [the longest x1 114 us: body(): lax.psum_scatter(grad_ffn, 'seq', scatter_dimension=0, tiled=True)]
    another operation x8 -> x0, other arithmetic: 328 us -> none  [the longest x5 323 us: prepare(): jax.scipy.linalg.solve_triangular(system, right_side, lower=True, unit_di...]
    dot_general x142 -> x4, matrix products: 283 us -> 4.43 us  [move(): lax.dot_general(map_of, state, (((dims[0],), (1,)), ((0,), (0,))), precis...]
    psum x3 -> x1, waiting for transfers between devices: 277 us -> 0.01 us  [body(): ffn_out = lax.psum(contract(activ_low, w_down, 1, 0), 'head')]
    ppermute x0 -> x31, waiting for transfers between devices: none -> 174 us  [exchange(): lax.ppermute(value, axis, [(place, place ^ bit) for place in range(count)])]
    psum x1 -> x2, blocking collectives: 6.8 us -> 137 us  [the longest x1 92.2 us: body(): taps_sum, decay_sum = lax.psum((grad_taps[:CONV], decay_sums[:2]), 'seq')]
    pallas_call x0 -> x5, Pallas kernels: none -> 87.4 us  [the longest x1 29.5 us: local_maps(): pl.pallas_call(partial(local_kernel, heads), grid=(blocks // PACK,), in_s...]
    all_gather x4 -> x0, waiting for transfers between devices: 80.7 us -> none  [prefix(): pieces = jax.tree.map(lambda part: lax.all_gather(part, axis), value)]
  transfers between devices with their start and end apart: 15 -> 45, of which waited for: 12 -> 12; matrix products, arithmetic and copies ran while one was open for 9% -> 17% of each run, Pallas kernels for 0% -> 8%
where the time goes in v1:
time: 635 us; the launch traced here: 627 us
  waiting for transfers between devices  183 us (29%)
  blocking collectives  137 us (22%)
  Pallas kernels  87.4 us (14%)
  starting transfers between devices  54.8 us (9%)
  matrix products  53.9 us (8%)
  local copies, waits for them, and re-layouts  49.6 us (8%)
  other arithmetic  44.6 us (7%)
  between operations  17.3 us (3%)
    ppermute x31, waiting for transfers between devices, exchange(): lax.ppermute(value, axis, [(place, place ^ bit) for place in range(count)])  174 us
    psum x1, blocking collectives, body(): taps_sum, decay_sum = lax.psum((grad_taps[:CONV], decay_sums[:2]), 'seq')  92.2 us
    dot_general x17, matrix products, contract(): lax.dot_general(left, right, (((left_dim,), (right_dim,)), ((), ())), pre...  49.4 us
    psum x1, blocking collectives, body(): lax.psum((grad_first_gain, grad_second_gain, jnp.sum(grad_gain, 0)), ('se...  44.4 us
    ppermute x12, starting transfers between devices, shifted(): lax.ppermute(value, axis, [(source, source + steps) for source in range(f...  31.6 us
    pallas_call x1, Pallas kernels, local_maps(): pl.pallas_call(partial(local_kernel, heads), grid=(blocks // PACK,), in_s...  29.5 us
    pallas_call x1, Pallas kernels, recurrence_back(): pl.pallas_call(partial(back_kernel, heads), grid=(steps,), in_specs=[SCAL...  28.3 us
    ppermute x31, starting transfers between devices, exchange(): lax.ppermute(value, axis, [(place, place ^ bit) for place in range(count)])  23.1 us
  transfers between devices with their start and end apart: 45, of which 12 were waited for; matrix products, arithmetic and copies ran while one was open for 17% of the time, Pallas kernels for 8%

profile of v1, /device:TPU:0, one launch (start us, length us, event | category | flops | bytes accessed | tf_op | source)
XLA Modules:
  0.0 627.2 jit_solution(2508149361171639158)
XLA Ops:
  18.1 5.0 collective-permute-start
  33.3 29.5 %local_maps.1 = (f32[1024,1280]{1,0:T(8,128)}, f32[2,16,64,128]{3,2,1,0:T(8,128)}, bf16[2,16,128,128]{3,2,1,0:T(8,128)(2,1)}, bf16[2,16,128,128]{3,2,1,0:T(8,128...) custom-call(s32[1]{0:T(128)S(6)} %copy.103.offset_ref, ...), custom_call_target="tpu_custom_call" | custom-call | tf_op jit(solution)/shard_map/local_maps/pallas_call | solution.py:268
  63.8 4.5 collective-permute-start.3
  77.7 4.7 collective-permute-start.5
  85.3 10.8 %mixer_outputs.1 = (bf16[2,16,128,128]{3,2,1,0:T(8,128)(2,1)}, bf16[2,16,128,128]{3,2,1,0:T(8,128)(2,1)}, f32[1024,256]{1,0:T(8,128)}, f32[1024,256]{1,0:T(8,128)}) custom-call(s32[1]{0:T(128)S(6)} %copy.103.offset_ref, f32[2,128,128]{2,1,0:T(8,128)} %convolution_add_fusion.2.incoming_ref, f32[2,16,128,256]{3,2,1,0:T(8,128)} %get-tuple-element.45.prefix_ref, ...), custom_call_target="tpu_custom_call" | custom-call | tf_op jit(solution)/shard_map/mixer_outputs/pallas_call | solution.py:355
  97.1 21.6 %collective-permute-done.7.refs_2_ = f32[1024,256]{1,0:T(8,128)} collective-permute-done((f32[1024,256]{1,0:T(8,128)}, f32[1024,256]{1,0:T(8,128)}, u32[]{:S(2)}, u32[]{:S(2)}) %collective-permute-start.7) | collective-permute-done | bytes 1048608 | tf_op jit(solution)/shard_map/ppermute | solution.py:766
  121.8 8.8 %mixer_project.1 = (f32[1024,1024]{1,0:T(8,128)}, bf16[1024,1024]{1,0:T(8,128)(2,1)}) custom-call(f32[1024,256]{1,0:T(8,128)} %get-tuple-element.51.refs_0_, f32[1024,256]{1,0:T(8,128)} %collective-permute-done.6.refs_1_, f32[1024,256]{1,0:T(8,128)} %collective-permute-done.7.refs_2_, f32[1024,256]{1,0:T(8,128)} %collective-permute-done.8.refs_3_, ...), custom_call_target="tpu_custom_call" | custom-call | tf_op jit(solution)/shard_map/mixer_project/pallas_call | solution.py:890
  130.6 5.2 fusion.31
  167.1 5.6 fusion.32
  174.3 67.6 %collective-permute-done.40 = f32[4,704,128]{2,1,0:T(8,128)} collective-permute-done((f32[4,704,128]{2,1,0:T(8,128)}, f32[4,704,128]{2,1,0:T(8,128)}, u32[]{:S(2)}, u32[]{:S(2)}) %collective-permute-start.40) | collective-permute-done | bytes 1441824 | tf_op jit(solution)/shard_map/ppermute | solution.py:766
  246.5 3.7 collective-permute-start.41
  253.9 31.2 %collective-permute-done.13 = f32[1,256,1024]{2,1,0:T(8,128)S(1)} collective-permute-done((f32[1,256,1024]{2,1,0:T(8,128)S(1)}, f32[1,256,1024]{2,1,0:T(8,128)S(1)}, u32[]{:S(2)}, u32[]{:S(2)}) %collective-permute-start.13) | collective-permute-done | bytes 1048608 | tf_op jit(solution)/shard_map/ppermute | solution.py:766
  296.2 5.6 add_convert_fusion
  301.7 10.5 %collective-permute-done.42 = f32[1,704,128]{2,1,0:T(8,128)} collective-permute-done((f32[1,704,128]{2,1,0:T(8,128)}, f32[1,704,128]{2,1,0:T(8,128)}, u32[]{:S(2)}, u32[]{:S(2)}) %collective-permute-start.42) | collective-permute-done | bytes 360480 | tf_op jit(solution)/shard_map/ppermute | solution.py:766
  326.4 3.9 fusion.13.grad_ref
  330.3 10.0 %gate_back.1 = (bf16[1024,256]{1,0:T(8,128)(2,1)}, bf16[1024,256]{1,0:T(8,128)(2,1)}, f32[8,128]{1,0:T(8,128)}, f32[2,16,128,128]{3,2,1,0:T(8,128)}, f32[2,128,128]{2,1,0:T(8,128)}) custom-call(f32[1024,256]{1,0:T(8,128)} %fusion.13.grad_ref, f32[1024,256]{1,0:T(8,128)} %get-tuple-element.54.mixed_ref, f32[1024,256]{1,0:T(8,128)} %fusion.30.outgate_ref, ...), custom_call_target="tpu_custom_call" | custom-call | tf_op jit(solution)/shard_map/gate_back/pallas_call | solution.py:442
  343.1 13.2 %collective-permute-done.39 = f32[1,128,1408]{2,1,0:T(8,128)S(1)} collective-permute-done((f32[1,128,1408]{2,1,0:T(8,128)S(1)}, f32[1,128,1408]{2,1,0:T(8,128)S(1)}, u32[]{:S(2)}, u32[]{:S(2)}) %collective-permute-start.39) | collective-permute-done | bytes 720928 | tf_op jit(solution)/shard_map/ppermute | solution.py:766
  360.1 4.2 collective-permute-done.21
  366.3 28.3 %recurrence_back.1 = (bf16[1024,1280]{1,0:T(8,128)(2,1)}, f32[16,1280]{1,0:T(8,128)}, f32[8,1280]{1,0:T(8,128)}, bf16[1024,128]{1,0:T(8,128)(2,1)}, f32[8,128]{1,0:T(8,128)}, /*index=5*/f32[8,1280]{1,0:T(8,128)}) custom-call(s32[1]{0:T(128)S(6)} %copy.103.offset_ref, f32[2,128,128]{2,1,0:T(8,128)} %convolution_add_fusion.leaving_ref, ...), custom_call_target="tpu_custom_call" | custom-call | tf_op jit(solution)/shard_map/recurrence_back/pallas_call | solution.py:706
  401.5 4.9 fusion.34
  425.0 92.2 %all-reduce.5 = (f32[4,1280]{1,0:T(4,128)}, f32[2,128]{1,0:T(2,128)S(1)}) all-reduce(f32[4,1280]{1,0:T(4,128)S(1)} %slice.38, f32[2,128]{1,0:T(2,128)S(1)} %slice.40), channel_id=1, replica_groups=mesh['seq'=8,'head'=4] {'seq'}, use_global_device_ids=true, to_apply=%region_8.9 | all-reduce | flops 5376 | bytes 43008 | tf_op jit(solution)/shard_map/psum | solution.py:1024
  529.6 14.1 %collective-permute-done.24 = f32[1,256,1024]{2,1,0:T(8,128)S(1)} collective-permute-done((f32[1,256,1024]{2,1,0:T(8,128)S(1)}, f32[1,256,1024]{2,1,0:T(8,128)S(1)}, u32[]{:S(2)}, u32[]{:S(2)}) %collective-permute-start.24) | collective-permute-done | bytes 1048608 | tf_op jit(solution)/shard_map/ppermute | solution.py:766
  549.1 13.2 %collective-permute-done.29 = f32[2,128,1280]{2,1,0:T(8,128)S(1)} collective-permute-done((f32[2,128,1280]{2,1,0:T(8,128)S(1)}, f32[2,128,1280]{2,1,0:T(8,128)S(1)}, u32[]{:S(2)}, u32[]{:S(2)}) %collective-permute-start.29) | collective-permute-done | bytes 1310752 | tf_op jit(solution)/shard_map/ppermute | solution.py:766
  565.9 44.4 %all-reduce.4 = (f32[1024]{0:T(1024)S(1)}, f32[128]{0:T(128)}, f32[1024]{0:T(1024)S(1)}) all-reduce(f32[1024]{0:T(1024)S(1)} %get-tuple-element.90, f32[128]{0:T(128)S(1)} %reduce_sum.78, f32[1024]{0:T(1024)S(1)} %copy-done.36), channel_id=1, replica_groups=mesh['seq'=8,'head'=4] {'seq','head'}, use_global_device_ids=true, to_apply=%region_7.8 | all-reduce | flops 2176 | bytes 17408 | tf_op jit(solution)/shard_map/psum | solution.py:1025
  (283 shorter events, 167.1 us)
Async XLA Ops:
  8.0 288.1 %all-reduce.8.cloned.1.call-start = ((), (), s32[]{:S(2)}) async-start(), calls=%async_computation.1 | async-start | bytes 8388608 | tf_op jit(solution)/shard_map/psum | solution.py:979
  24.2 72.9 %collective-permute-start.10 = (f32[256,1024]{1,0:T(8,128)}, f32[256,1024]{1,0:T(8,128)}, u32[]{:S(2)}, u32[]{:S(2)}) collective-permute-start(f32[256,1024]{1,0:T(8,128)} %convert_element_type.50.refs_4_), channel_id=1, source_target_pairs={{0,2},{1,3},{2,0},{3,1},{4,6},{5,7},{6,4},{7,5},{8,10},{9,11},{10,... | collective-permute-start | bytes 3145736 | tf_op jit(solution)/shard_map/ppermute | solution.py:766
  145.7 104.5 %collective-permute-start.37 = (f32[4,128,1408]{2,1,0:T(8,128)}, f32[4,128,1408]{2,1,0:T(8,128)}, u32[]{:S(2)}, u32[]{:S(2)}) collective-permute-start(f32[4,128,1408]{2,1,0:T(8,128)} %dynamic-slice_bitcast_fusion), channel_id=1, source_target_pairs={{0,4},{4,0},{8,12},{12,8},{16,20},{20,16},{24,28},{28,24},{1,5},{5... | collective-permute-start | bytes 8650760 | tf_op jit(solution)/shard_map/ppermute | solution.py:766
  153.1 90.5 %collective-permute-start.12 = (f32[2,256,1024]{2,1,0:T(8,128)}, f32[2,256,1024]{2,1,0:T(8,128)}, u32[]{:S(2)}, u32[]{:S(2)}) collective-permute-start(f32[2,256,1024]{2,1,0:T(8,128)} %dynamic-slice_bitcast_fusion.3), channel_id=1, source_target_pairs={{0,1},{1,0},{2,3},{3,2},{4,5},{5,4},{6,7},{7,6},{8,9},{9,8},{10,11... | collective-permute-start | bytes 6291464 | tf_op jit(solution)/shard_map/ppermute | solution.py:766
  160.3 81.6 %collective-permute-start.40 = (f32[4,704,128]{2,1,0:T(8,128)}, f32[4,704,128]{2,1,0:T(8,128)}, u32[]{:S(2)}, u32[]{:S(2)}) collective-permute-start(f32[4,704,128]{2,1,0:T(8,128)} %bitcast.159), channel_id=1, source_target_pairs={{0,4},{4,0},{8,12},{12,8},{16,20},{20,16},{24,28},{28,24},{1,5},{5... | collective-permute-start | bytes 4325384 | tf_op jit(solution)/shard_map/ppermute | solution.py:766
  165.6 193.2 %collective-permute-start.15 = (f32[2,128,128]{2,1,0:T(8,128)S(1)}, f32[2,128,128]{2,1,0:T(8,128)}, u32[]{:S(2)}, u32[]{:S(2)}) collective-permute-start(f32[2,128,128]{2,1,0:T(8,128)S(1)} %get-tuple-element.110), channel_id=1, source_target_pairs={{8,0},{12,4},{16,8},{20,12},{24,16},{28,20},{9,1},{13,5},{17,9},{2... | collective-permute-start | bytes 393224 | tf_op jit(solution)/shard_map/ppermute | solution.py:772
  172.7 446.8 %reduce-scatter.2.cloned.1.call-start = ((), (), s32[]{:S(2)}) async-start(), calls=%async_computation.2 | async-start | bytes 36864 | tf_op jit(solution)/shard_map/reduce_scatter | solution.py:1023
  245.9 39.2 %collective-permute-start.13 = (f32[1,256,1024]{2,1,0:T(8,128)S(1)}, f32[1,256,1024]{2,1,0:T(8,128)S(1)}, u32[]{:S(2)}, u32[]{:S(2)}) collective-permute-start(f32[1,256,1024]{2,1,0:T(8,128)S(1)} %constant_dynamic-slice_fusion.10), channel_id=1, source_target_pairs={{0,2},{1,3},{2,0},{3,1},{4,6},{5,7},{6,4},{7,5},{8,10},{9,11},{10,... | collective-permute-start | bytes 3145736 | tf_op jit(solution)/shard_map/ppermute | solution.py:766
  246.5 45.3 %collective-permute-start.41 = (f32[2,704,128]{2,1,0:T(8,128)S(1)}, f32[2,704,128]{2,1,0:T(8,128)S(1)}, u32[]{:S(2)}, u32[]{:S(2)}) collective-permute-start(f32[2,704,128]{2,1,0:T(8,128)S(1)} %dynamic-slice_bitcast_fusion.6), channel_id=1, source_target_pairs={{0,8},{4,12},{8,0},{12,4},{16,24},{20,28},{24,16},{28,20},{1,9},{5... | collective-permute-start | bytes 2162696 | tf_op jit(solution)/shard_map/ppermute | solution.py:766
  253.8 62.7 %collective-permute-start.38 = (f32[2,128,1408]{2,1,0:T(8,128)}, f32[2,128,1408]{2,1,0:T(8,128)}, u32[]{:S(2)}, u32[]{:S(2)}) collective-permute-start(f32[2,128,1408]{2,1,0:T(8,128)} %dynamic-slice_bitcast_fusion.4), channel_id=1, source_target_pairs={{0,8},{4,12},{8,0},{12,4},{16,24},{20,28},{24,16},{28,20},{1,9},{5... | collective-permute-start | bytes 4325384 | tf_op jit(solution)/shard_map/ppermute | solution.py:766
  291.3 25.2 %collective-permute-start.17 = (f32[256,1024]{1,0:T(8,128)}, f32[256,1024]{1,0:T(8,128)}, u32[]{:S(2)}, u32[]{:S(2)}) collective-permute-start(f32[256,1024]{1,0:T(8,128)} %get-tuple-element.101), channel_id=1, source_target_pairs={{0,2},{1,3},{2,0},{3,1},{4,6},{5,7},{6,4},{7,5},{8,10},{9,11},{10,... | collective-permute-start | bytes 3145736 | tf_op jit(solution)/shard_map/ppermute | solution.py:766
  296.2 24.5 %collective-permute-start.16 = (f32[256,1024]{1,0:T(8,128)}, f32[256,1024]{1,0:T(8,128)}, u32[]{:S(2)}, u32[]{:S(2)}) collective-permute-start(f32[256,1024]{1,0:T(8,128)} %get-tuple-element.101), channel_id=1, source_target_pairs={{0,1},{1,0},{2,3},{3,2},{4,5},{5,4},{6,7},{7,6},{8,9},{9,8},{10,11... | collective-permute-start | bytes 3145736 | tf_op jit(solution)/shard_map/ppermute | solution.py:766
  312.2 47.9 %collective-permute-start.14 = (f32[2,128,128]{2,1,0:T(8,128)S(1)}, f32[2,128,128]{2,1,0:T(8,128)}, u32[]{:S(2)}, u32[]{:S(2)}) collective-permute-start(f32[2,128,128]{2,1,0:T(8,128)S(1)} %get-tuple-element.110), channel_id=1, source_target_pairs={{4,0},{8,4},{12,8},{16,12},{20,16},{24,20},{28,24},{5,1},{9,5},{13... | collective-permute-start | bytes 393224 | tf_op jit(solution)/shard_map/ppermute | solution.py:772
  318.1 38.2 %collective-permute-start.39 = (f32[1,128,1408]{2,1,0:T(8,128)S(1)}, f32[1,128,1408]{2,1,0:T(8,128)S(1)}, u32[]{:S(2)}, u32[]{:S(2)}) collective-permute-start(f32[1,128,1408]{2,1,0:T(8,128)S(1)} %constant_dynamic-slice_fusion.3), channel_id=1, source_target_pairs={{0,16},{4,20},{8,24},{12,28},{16,0},{20,4},{24,8},{28,12},{1,17},{... | collective-permute-start | bytes 2162696 | tf_op jit(solution)/shard_map/ppermute | solution.py:766
  411.1 114.8 %collective-permute-start.28 = (f32[4,128,1280]{2,1,0:T(8,128)}, f32[4,128,1280]{2,1,0:T(8,128)}, u32[]{:S(2)}, u32[]{:S(2)}) collective-permute-start(f32[4,128,1280]{2,1,0:T(8,128)} %dynamic-slice_bitcast_fusion.1), channel_id=1, source_target_pairs={{0,4},{4,0},{8,12},{12,8},{16,20},{20,16},{24,28},{28,24},{1,5},{5... | collective-permute-start | bytes 7864328 | tf_op jit(solution)/shard_map/ppermute | solution.py:766
  414.0 108.4 %collective-permute-start.23 = (f32[2,256,1024]{2,1,0:T(8,128)}, f32[2,256,1024]{2,1,0:T(8,128)}, u32[]{:S(2)}, u32[]{:S(2)}) collective-permute-start(f32[2,256,1024]{2,1,0:T(8,128)} %dynamic-slice_bitcast_fusion.2), channel_id=1, source_target_pairs={{0,1},{1,0},{2,3},{3,2},{4,5},{5,4},{6,7},{7,6},{8,9},{9,8},{10,11... | collective-permute-start | bytes 6291464 | tf_op jit(solution)/shard_map/ppermute | solution.py:766
  419.7 99.2 %collective-permute-start.34 = (f32[4,256,128]{2,1,0:T(8,128)}, f32[4,256,128]{2,1,0:T(8,128)S(1)}, u32[]{:S(2)}, u32[]{:S(2)}) collective-permute-start(f32[4,256,128]{2,1,0:T(8,128)} %bitcast.160), channel_id=1, source_target_pairs={{0,4},{4,0},{8,12},{12,8},{16,20},{20,16},{24,28},{28,24},{1,5},{5... | collective-permute-start | bytes 1572872 | tf_op jit(solution)/shard_map/ppermute | solution.py:766
  423.8 95.2 %collective-permute-start.31 = (f32[4,128,256]{2,1,0:T(8,128)}, f32[4,128,256]{2,1,0:T(8,128)}, u32[]{:S(2)}, u32[]{:S(2)}) collective-permute-start(f32[4,128,256]{2,1,0:T(8,128)} %dynamic-slice_bitcast_fusion.7), channel_id=1, source_target_pairs={{0,4},{4,0},{8,12},{12,8},{16,20},{20,16},{24,28},{28,24},{1,5},{5... | collective-permute-start | bytes 1572872 | tf_op jit(solution)/shard_map/ppermute | solution.py:766
  520.7 28.2 %collective-permute-start.32 = (f32[2,128,256]{2,1,0:T(8,128)S(1)}, f32[2,128,256]{2,1,0:T(8,128)S(1)}, u32[]{:S(2)}, u32[]{:S(2)}) collective-permute-start(f32[2,128,256]{2,1,0:T(8,128)S(1)} %dynamic-slice_bitcast_fusion.9), channel_id=1, source_target_pairs={{0,8},{4,12},{8,0},{12,4},{16,24},{20,28},{24,16},{28,20},{1,9},{5... | collective-permute-start | bytes 786440 | tf_op jit(solution)/shard_map/ppermute | solution.py:766
  529.0 33.4 %collective-permute-start.29 = (f32[2,128,1280]{2,1,0:T(8,128)S(1)}, f32[2,128,1280]{2,1,0:T(8,128)S(1)}, u32[]{:S(2)}, u32[]{:S(2)}) collective-permute-start(f32[2,128,1280]{2,1,0:T(8,128)S(1)} %dynamic-slice_bitcast_fusion.5), channel_id=1, source_target_pairs={{0,8},{4,12},{8,0},{12,4},{16,24},{20,28},{24,16},{28,20},{1,9},{5... | collective-permute-start | bytes 3932168 | tf_op jit(solution)/shard_map/ppermute | solution.py:766
  529.5 35.1 %collective-permute-start.36 = (f32[1,256,128]{2,1,0:T(8,128)S(1)}, f32[1,256,128]{2,1,0:T(8,128)S(1)}, u32[]{:S(2)}, u32[]{:S(2)}) collective-permute-start(f32[1,256,128]{2,1,0:T(8,128)S(1)} %constant_dynamic-slice_fusion.4), channel_id=1, source_target_pairs={{0,16},{4,20},{8,24},{12,28},{16,0},{20,4},{24,8},{28,12},{1,17},{... | collective-permute-start | bytes 393224 | tf_op jit(solution)/shard_map/ppermute | solution.py:766
  549.0 62.5 %collective-permute-start.25 = (f32[256,1024]{1,0:T(8,128)}, f32[256,1024]{1,0:T(8,128)}, u32[]{:S(2)}, u32[]{:S(2)}) collective-permute-start(f32[256,1024]{1,0:T(8,128)} %get-tuple-element.98), channel_id=1, source_target_pairs={{0,1},{1,0},{2,3},{3,2},{4,5},{5,4},{6,7},{7,6},{8,9},{9,8},{10,11... | collective-permute-start | bytes 3145736 | tf_op jit(solution)/shard_map/ppermute | solution.py:766
  564.5 51.8 %collective-permute-start.30 = (f32[1,128,1280]{2,1,0:T(8,128)}, f32[1,128,1280]{2,1,0:T(8,128)S(1)}, u32[]{:S(2)}, u32[]{:S(2)}) collective-permute-start(f32[1,128,1280]{2,1,0:T(8,128)} %constant_dynamic-slice_fusion.8), channel_id=1, source_target_pairs={{0,16},{4,20},{8,24},{12,28},{16,0},{20,4},{24,8},{28,12},{1,17},{... | collective-permute-start | bytes 1966088 | tf_op jit(solution)/shard_map/ppermute | solution.py:766
  564.5 52.7 %collective-permute-start.27 = (f32[256,1024]{1,0:T(8,128)}, f32[256,1024]{1,0:T(8,128)}, u32[]{:S(2)}, u32[]{:S(2)}) collective-permute-start(f32[256,1024]{1,0:T(8,128)} %collective-permute-done.26), channel_id=1, source_target_pairs={{0,1},{1,0},{2,3},{3,2},{4,5},{5,4},{6,7},{7,6},{8,9},{9,8},{10,11... | collective-permute-start | bytes 3145736 | tf_op jit(solution)/shard_map/ppermute | solution.py:766
  (72 other events, 1075.5 us)
Sparse Core Ops, SparseCore 0:
  172.8 104.4 all-reduce.7
Sparse Core Ops, SparseCore 1:
  518.4 61.2 reduce-scatter.1

commit v2 on v1

--- a/solution.py
+++ b/solution.py
@@ -13,7 +13,7 @@
 EDGE = 8
 LANES = 128
 GROUPS = 1 + 2 * STEPS
-PACK = 2
+PACK = 4
 DOCS = 4
 EPSILON = 1e-06
 VMEM_LIMIT = 56 * 1024 * 1024
@@ -100,13 +100,16 @@
 def local_kernel(
     heads,
     offset_ref,
-    edge_ref,
+    raw_ref,
+    gain_ref,
+    weight_ref,
     halo_ref,
     mix_ref,
     taps_ref,
     rates_ref,
     rate_row_ref,
     bias_row_ref,
+    edge_ref,
     conv_ref,
     q_ref,
     k_ref,
@@ -130,6 +133,9 @@
 
     @pl.when(step == 0)
     def _():
+        raw = raw_ref[...]
+        scale = lax.rsqrt(jnp.mean(raw * raw, -1, keepdims=True) + EPSILON)
+        edge_ref[...] = dot1(raw * scale * gain_ref[...], weight_ref[...], NN)
         run_ref[...] = jnp.concatenate([jnp.broadcast_to(eye, run_ref.shape[:2] + (width,)), jnp.zeros(run_ref.shape[:2] + (width,), F32)], 2)
 
     place = step * rows + iota((rows, width), 0)
@@ -187,7 +193,7 @@
         carries.append(carried)
         ratios.append(ratio)
         scaleds.append(jnp.concatenate([beta * value, beta * twice(carried) * key], 1))
-        systems.append(jnp.where(strict, beta * twice(ratio), 0.0) * dot1(key_low, key_low, NT))
+        systems.append(jnp.where(strict, beta * twice(ratio), 0.0) * dot3(key, key, NT))
     inverses = [eye - jnp.where(apart == 0, system, 0.0) for system in systems]
     for level in range(SPAN.bit_length() - 1):
         off_blocks = [jnp.where((apart >> level) == 1, system, 0.0) for system in systems]
@@ -196,6 +202,12 @@
         inverses = [
             inverse - dot1(half, low, NN) for inverse, half, low in zip(inverses, halfway, lows)
         ]
+    residues = [
+        (eye - inverse) - dot3(system, inverse, NN) for inverse, system in zip(inverses, systems)
+    ]
+    inverses = [
+        inverse + dot1(inverse, residue, NN) for inverse, residue in zip(inverses, residues)
+    ]
     solveds = [dot3(inverse, scaled, NN) for inverse, scaled in zip(inverses, scaleds)]
     all_scores = [ratio * dot3(query, key, NT) for ratio, query, key in zip(ratios, queries, keys)]
     all_maps = [
@@ -244,7 +256,10 @@
     return pltpu.CompilerParams(vmem_limit_bytes=VMEM_LIMIT)
 
 
-def local_maps(offset, edge, mixing, taps, rates, rate_row, bias_row):
+LIGHT = pl.CostEstimate(flops=1, bytes_accessed=1, transcendentals=0)
+
+
+def local_maps(offset, raw, gain, weight, mixing, taps, rates, rate_row, bias_row):
     rows, columns = mixing.shape
     width = LANES
     heads = columns // (GROUPS * width)
@@ -270,7 +285,9 @@
         grid=(blocks // PACK,),
         in_specs=[
             SCALARS,
-            whole((EDGE, columns)),
+            whole(raw.shape),
+            whole(gain.shape),
+            whole(weight.shape),
             pl.BlockSpec((EDGE, columns), lambda g: (jnp.maximum(g * (tile // EDGE) - 1, 0), 0)),
             pl.BlockSpec((tile, columns), lambda g: (g, 0)),
             whole(taps.shape),
@@ -278,16 +295,20 @@
             whole((1, LANES)),
             whole((1, LANES)),
         ],
-        out_specs=[pl.BlockSpec((tile, columns), lambda g: (g, 0))]
+        out_specs=[whole((EDGE, columns)), pl.BlockSpec((tile, columns), lambda g: (g, 0))]
         + [spec for spec, _, _ in saved]
         + [whole((heads, width, 2 * width))],
-        out_shape=[jax.ShapeDtypeStruct((rows, columns), F32)]
+        out_shape=[
+            jax.ShapeDtypeStruct((EDGE, columns), F32),
+            jax.ShapeDtypeStruct((rows, columns), F32),
+        ]
         + [jax.ShapeDtypeStruct((heads, blocks) + dims, kind) for _, dims, kind in saved]
         + [jax.ShapeDtypeStruct((heads, width, 2 * width), F32)],
         scratch_shapes=[pltpu.VMEM((heads, width, 2 * width), F32)],
         compiler_params=params(),
+        cost_estimate=LIGHT,
         name="local_maps",
-    )(offset, edge, mixing, mixing, taps, rates, rate_row, bias_row)
+    )(offset, raw, gain, weight, mixing, mixing, taps, rates, rate_row, bias_row)
 
 
 def output_kernel(
@@ -375,39 +396,58 @@
             jax.ShapeDtypeStruct((rows, heads * width), gated_type),
         ],
         compiler_params=params(),
+        cost_estimate=LIGHT,
         name="mixer_outputs",
     )(offset, incoming, prefix, u, w, scores, q, cumul, outgate, gain)
 
 
 def gate_back_kernel(
     heads,
-    grad_ref,
-    mixed_ref,
-    outgate_ref,
-    gain_ref,
-    query_ref,
-    prefix_ref,
-    grad_mixed_ref,
-    grad_outgate_ref,
-    grad_gain_ref,
-    term_ref,
-    total_ref,
+    parts,
+    place_ref,
+    *refs,
 ):
+    piece_refs = refs[:parts]
+    (
+        weight_ref,
+        mixed_ref,
+        outgate_ref,
+        gain_ref,
+        query_ref,
+        prefix_ref,
+        branch_ref,
+        grad_mixed_ref,
+        grad_outgate_ref,
+        grad_gain_ref,
+        term_ref,
+        total_ref,
+        sum_ref,
+    ) = refs[parts:]
     step = pl.program_id(0)
     pack = prefix_ref.shape[1]
     width = LANES
+    rows = branch_ref.shape[0]
 
     @pl.when(step == 0)
     def _():
+        sum_ref[...] = sum(ref[rows:] for ref in piece_refs)
         grad_gain_ref[...] = jnp.zeros_like(grad_gain_ref)
         total_ref[...] = jnp.zeros_like(total_ref)
 
+    for near in range(parts):
+
+        @pl.when(step == near)
+        def _():
+            branch_ref[...] = piece_refs[near][:rows].astype(BF16)
+
+    grad_all = dot1(branch_ref[...], weight_ref[...], NT)
+    gain = gain_ref[...]
+    grads_mixed = []
     for head in range(heads):
         cols = slice(head * width, (head + 1) * width)
         mixed = mixed_ref[:, cols]
         outgate = outgate_ref[:, cols]
-        grad = grad_ref[:, cols]
-        gain = gain_ref[...]
+        grad = grad_all[:, cols]
         scale = lax.rsqrt(jnp.mean(mixed * mixed, -1, keepdims=True) + EPSILON)
         normed = mixed * scale
         sigma = jax.nn.sigmoid(outgate)
@@ -421,45 +461,316 @@
         grad_mixed = scale * (
             grad_normed - normed * jnp.mean(grad_normed * normed, -1, keepdims=True)
         )
-        grad_low = grad_mixed.astype(BF16)
-        grad_mixed_ref[:, cols] = grad_low
-        total = total_ref[head]
-        for pos in range(pack):
-            here = slice(pos * SPAN, (pos + 1) * SPAN)
-            term = dot3(query_ref[head, pos], grad_mixed[here], TN)
-            term_ref[head, pos] = term
-            total = total + dot3(prefix_ref[head, pos], term, TN)
-        total_ref[head] = total
-
-
-def gate_back(grad, mixed, outgate, gain, query, prefix):
+        grad_mixed_ref[:, cols] = grad_mixed.astype(BF16)
+        grads_mixed.append(grad_mixed)
+    chains = [(pos, head) for pos in range(pack) for head in range(heads)]
+    terms = [
+        dot3(query_ref[head, pos], grads_mixed[head][pos * SPAN : (pos + 1) * SPAN], TN)
+        for pos, head in chains
+    ]
+    moved = [dot3(prefix_ref[head, pos], term, TN) for (pos, head), term in zip(chains, terms)]
+    totals = [total_ref[head] for head in range(heads)]
+    for (pos, head), term, part in zip(chains, terms, moved):
+        term_ref[head, pos] = term
+        totals[head] = totals[head] + part
+    for head in range(heads):
+        total_ref[head] = totals[head]
+
+
+def gate_back(place, pieces, weight, mixed, outgate, gain, query, prefix):
     heads, blocks = prefix.shape[:2]
     width = LANES
-    tile = PACK * SPAN
+    parts = len(pieces)
+    model = pieces[0].shape[1]
     rows = mixed.shape[0]
-    per_block = specs_of(heads, PACK)
-    flat = pl.BlockSpec((tile, heads * width), lambda g: (g, 0))
+    tile = rows // parts
+    pack = tile // SPAN
+
+    def fixed(*shape):
+        return pl.BlockSpec(shape, lambda g, at: (0,) * len(shape))
+
+    def per_block(*dims):
+        return pl.BlockSpec((heads, pack) + dims, lambda g, at: (0, at[g]) + (0,) * len(dims))
+
+    def flat(size):
+        return pl.BlockSpec((tile, size), lambda g, at: (at[g], 0))
+
     return pl.pallas_call(
-        partial(gate_back_kernel, heads),
-        grid=(blocks // PACK,),
-        in_specs=[flat, flat, flat, whole((1, width)), per_block(SPAN, width), per_block(width, width)],
-        out_specs=[
-            flat,
-            flat,
-            whole((8, width)),
-            per_block(width, width),
-            whole((heads, width, width)),
-        ],
+        partial(gate_back_kernel, heads, parts),
+        grid_spec=pltpu.PrefetchScalarGridSpec(
+            num_scalar_prefetch=1,
+            grid=(parts,),
+            in_specs=[fixed(tile + EDGE, model)] * parts
+            + [
+                fixed(*weight.shape),
+                flat(heads * width),
+                flat(heads * width),
+                fixed(1, width),
+                per_block(SPAN, width),
+                per_block(width, width),
+            ],
+            out_specs=[
+                flat(model),
+                flat(heads * width),
+                flat(heads * width),
+                fixed(8, width),
+                per_block(width, width),
+                fixed(heads, width, width),
+                fixed(EDGE, model),
+            ],
+        ),
         out_shape=[
+            jax.ShapeDtypeStruct((rows, model), BF16),
             jax.ShapeDtypeStruct((rows, heads * width), BF16),
             jax.ShapeDtypeStruct((rows, heads * width), BF16),
             jax.ShapeDtypeStruct((8, width), F32),
             jax.ShapeDtypeStruct((heads, blocks, width, width), F32),
             jax.ShapeDtypeStruct((heads, width, width), F32),
+            jax.ShapeDtypeStruct((EDGE, model), F32),
         ],
         compiler_params=params(),
+        cost_estimate=LIGHT,
         name="gate_back",
-    )(grad, mixed, outgate, gain, query, prefix)
+    )(place, *pieces, weight, mixed, outgate, gain, query, prefix)
+
+
+def place_kernel(parts, place_ref, *refs):
+    out_ref, sum_ref = refs[parts:]
+    rows = refs[0].shape[0] - EDGE
+    for near in range(parts):
+        here = pl.ds(pl.multiple_of(place_ref[near] * rows, rows), rows)
+        out_ref[here] = refs[near][:rows].astype(out_ref.dtype)
+    sum_ref[...] = sum(ref[rows:] for ref in refs[:parts])
+
+
+def place_rows(place, pieces, kind):
+    parts = len(pieces)
+    rows, columns = pieces[0].shape
+    return pl.pallas_call(
+        partial(place_kernel, parts),
+        in_specs=[SCALARS] + [IN_VMEM] * parts,
+        out_specs=[IN_VMEM, IN_VMEM],
+        out_shape=[
+            jax.ShapeDtypeStruct((parts * (rows - EDGE), columns), kind),
+            jax.ShapeDtypeStruct((EDGE, columns), F32),
+        ],
+        compiler_params=params(),
+        cost_estimate=LIGHT,
+        name="place_rows",
+    )(place, *pieces)
+
+
+def low_weight_kernel(*refs):
+    refs[-2][...] = jnp.concatenate([ref[...].astype(BF16) for ref in refs[:-3]], 0)
+
+
+def low_weight(pieces, passed):
+    depth, columns = pieces[0].shape
+    steps = 2
+    return pl.pallas_call(
+        low_weight_kernel,
+        grid=(steps,),
+        in_specs=[pl.BlockSpec((depth, columns // steps), lambda g: (0, g))] * len(pieces)
+        + [pl.BlockSpec(memory_space=pl.ANY)],
+        out_specs=[
+            pl.BlockSpec((depth * len(pieces), columns // steps), lambda g: (0, g)),
+            pl.BlockSpec(memory_space=pl.ANY),
+        ],
+        out_shape=[
+            jax.ShapeDtypeStruct((depth * len(pieces), columns), BF16),
+            jax.ShapeDtypeStruct(passed.shape, passed.dtype),
+        ],
+        input_output_aliases={len(pieces): 1},
+        compiler_params=params(),
+        cost_estimate=LIGHT,
+        name="low_weight",
+    )(*pieces, passed)
+
+
+def first_kernel(
+    input_ref,
+    gain_ref,
+    mix_ref,
+    rates_ref,
+    outgate_ref,
+    normed_ref,
+    mixing_ref,
+    rates_out_ref,
+    outgate_out_ref,
+):
+    values = input_ref[...].astype(F32)
+    scale = lax.rsqrt(jnp.mean(values * values, -1, keepdims=True) + EPSILON)
+    normed = (values * scale * gain_ref[...]).astype(BF16)
+    normed_ref[...] = normed
+    mixing_ref[...] = dot1(normed, mix_ref[...], NN)
+    rates_out_ref[...] = dot1(normed, rates_ref[...], NN)
+    outgate_out_ref[...] = dot1(normed, outgate_ref[...], NN)
+
+
+def first_projections(block_input, gain, w_mix, w_rates, w_outgate):
+    rows, model = block_input.shape
+    steps = 4
+    tile = rows // steps
+    flat = lambda size: pl.BlockSpec((tile, size), lambda g: (g, 0))
+    weights = (w_mix, w_rates, w_outgate)
+    return pl.pallas_call(
+        first_kernel,
+        grid=(steps,),
+        in_specs=[flat(model), whole((1, model))] + [whole(weight.shape) for weight in weights],
+        out_specs=[flat(model)] + [flat(weight.shape[1]) for weight in weights],
+        out_shape=[jax.ShapeDtypeStruct((rows, model), BF16)]
+        + [jax.ShapeDtypeStruct((rows, weight.shape[1]), F32) for weight in weights],
+        compiler_params=params(),
+        cost_estimate=LIGHT,
+        name="first_projections",
+    )(block_input, gain, *weights)
+
+
+def dense_kernel(parts, *refs):
+    gated_refs = refs[1 : 1 + parts]
+    (
+        weight_ref,
+        input_ref,
+        gain_ref,
+        ffn_ref,
+        down_ref,
+        grad_ref,
+    ) = refs[1 + parts : 7 + parts]
+    (
+        middle_ref,
+        normed_ref,
+        activ_ref,
+        *some_refs,
+        back_ref,
+        fore_ref,
+    ) = refs[-6 - len(CUTS) :]
+    hidden = down_ref.shape[0]
+    gated = jnp.concatenate([ref[...].astype(BF16) for ref in gated_refs], 1)
+    middle = input_ref[...].astype(F32) + dot1(gated, weight_ref[...], NN)
+    middle_ref[...] = middle
+    scale = lax.rsqrt(jnp.mean(middle * middle, -1, keepdims=True) + EPSILON)
+    normed = (middle * scale * gain_ref[...]).astype(BF16)
+    normed_ref[...] = normed
+    both = dot1(normed, ffn_ref[...], NN)
+    gate, up = both[:, :hidden], both[:, hidden:]
+    grad_activ = dot1(grad_ref[...], down_ref[...], NT)
+    sigma = jax.nn.sigmoid(gate)
+    silu = gate * sigma
+    activ = (silu * up).astype(BF16)
+    activ_ref[:, :hidden] = activ
+    activ_ref[:, hidden:] = jnp.zeros_like(activ_ref[:, hidden:])
+    grad_gate = grad_activ * up * (sigma * (1.0 + gate * (1.0 - sigma)))
+    grad_both = jnp.concatenate([grad_gate, grad_activ * silu], 1).astype(BF16)
+    for ref, low, high in zip(some_refs, (0,) + CUTS, CUTS + (2 * hidden,)):
+        ref[...] = grad_both[:, low:high]
+    back_ref[...] = dot1(grad_both, ffn_ref[...], NT)
+    fore_ref[...] = dot1(activ, down_ref[...], NN)
+
+
+DENSE_STEPS = 2
+CUTS = (384, 768)
+
+
+def dense_half(half, gated_near, weight, block_input, gain, ffn, w_down, grad, filled):
+    parts = len(gated_near)
+    rows, model = block_input.shape
+    steps = DENSE_STEPS
+    tile = rows // (2 * steps)
+    depth = gated_near[0].shape[1]
+    hidden = w_down.shape[0]
+
+    def fixed(*shape):
+        return pl.BlockSpec(shape, lambda g, at: (0,) * len(shape))
+
+    def flat(size):
+        return pl.BlockSpec((tile, size), lambda g, at: (at[0] * steps + g, 0))
+
+    sizes = [
+        (model, F32),
+        (model, BF16),
+        (hidden + -hidden % LANES, BF16),
+    ] + [(high - low, BF16) for low, high in zip((0,) + CUTS, CUTS + (2 * hidden,))]
+    operands = [half, *gated_near, weight, block_input, gain, ffn, w_down, grad]
+    in_specs = [flat(depth)] * parts + [
+        fixed(parts * depth, model),
+        flat(model),
+        fixed(1, model),
+        fixed(model, 2 * hidden),
+        fixed(hidden, model),
+        flat(model),
+    ]
+    aliases = {}
+    if filled is not None:
+        aliases = {len(operands) + index: index for index in range(len(filled))}
+        in_specs = in_specs + [pl.BlockSpec(memory_space=pl.ANY)] * len(filled)
+        operands = operands + list(filled)
+    return pl.pallas_call(
+        partial(dense_kernel, parts),
+        grid_spec=pltpu.PrefetchScalarGridSpec(
+            num_scalar_prefetch=1,
+            grid=(steps,),
+            in_specs=in_specs,
+            out_specs=[flat(size) for size, _ in sizes]
+            + [pl.BlockSpec((tile, model), lambda g, at: (g, 0))] * 2,
+        ),
+        out_shape=[jax.ShapeDtypeStruct((rows, size), kind) for size, kind in sizes]
+        + [jax.ShapeDtypeStruct((rows // 2, model), F32)] * 2,
+        input_output_aliases=aliases,
+        compiler_params=params(),
+        cost_estimate=LIGHT,
+        name="dense_half",
+    )(*operands)
+
+
+def first_back_kernel(count, place_ref, *refs):
+    grad_refs, weight_refs = refs[:count], refs[count : 2 * count]
+    sent_ref, kept_ref = refs[2 * count :]
+    result = sum(
+        dot1(grad_ref[...], weight_ref[...], NT)
+        for grad_ref, weight_ref in zip(grad_refs, weight_refs)
+    )
+    half = pl.num_programs(0) // 2
+
+    @pl.when(pl.program_id(0) < half)
+    def _():
+        sent_ref[...] = result
+
+    @pl.when(pl.program_id(0) >= half)
+    def _():
+        kept_ref[...] = result
+
+
+def first_back(half, grads, weights):
+    rows = grads[0].shape[0]
+    model = weights[0].shape[0]
+    steps = 4
+    tile = rows // steps
+    side = steps // 2
+
+    def rows_at(g, at):
+        kept = (g >= side).astype(jnp.int32)
+        return (kept * at[0] + (1 - kept) * (1 - at[0])) * side + g - kept * side
+
+    def spec_of(grad):
+        return pl.BlockSpec((tile, grad.shape[1]), lambda g, at: (rows_at(g, at), 0))
+
+    return pl.pallas_call(
+        partial(first_back_kernel, len(grads)),
+        grid_spec=pltpu.PrefetchScalarGridSpec(
+            num_scalar_prefetch=1,
+            grid=(steps,),
+            in_specs=[spec_of(grad) for grad in grads]
+            + [pl.BlockSpec(weight.shape, lambda g, at: (0, 0)) for weight in weights],
+            out_specs=[
+                pl.BlockSpec((tile, model), lambda g, at: (jnp.minimum(g, side - 1), 0)),
+                pl.BlockSpec((tile, model), lambda g, at: (jnp.maximum(g - side, 0), 0)),
+            ],
+        ),
+        out_shape=[jax.ShapeDtypeStruct((rows // 2, model), F32)] * 2,
+        compiler_params=params(),
+        cost_estimate=LIGHT,
+        name="first_back",
+    )(half, *grads, *weights)
 
 
 def back_kernel(
@@ -754,6 +1065,7 @@
             pltpu.VMEM((tile, columns), F32),
         ],
         compiler_params=params(),
+        cost_estimate=LIGHT,
         name="recurrence_back",
     )(
         offset, leaving, term, phi, state, fresh, grad, scores, x, n, cumul, q, k,
@@ -761,6 +1073,272 @@
     )
 
 
+def piece_at(index, total, low, mine, bit):
+    half = total // 2
+    later = (index >= half).astype(jnp.int32)
+    rest = index - later * half
+    side = (mine // bit) % 2
+    picked = later * side + (1 - later) * (1 - side)
+    return ((rest >> low) << (low + 1)) | (picked << low) | (rest & ((1 << low) - 1))
+
+
+def sent_at(index, total):
+    return jnp.minimum(index, total // 2 - 1)
+
+
+def kept_at(index, total):
+    return jnp.maximum(index - total // 2, 0)
+
+
+def grad_kernel(half, pairs, *refs):
+    sent_ref, kept_ref = refs[-2:]
+    depth = sent_ref.shape[1]
+
+    def put(out_ref):
+        place = 0
+        for index in range(pairs):
+            first = 1 + index * (half + 1)
+            left = jnp.concatenate([ref[...] for ref in refs[first : first + half]], 1)
+            right_ref = refs[first + half]
+            size = right_ref.shape[1]
+            result = dot1(left, right_ref[...], TN)
+            for piece in range(half):
+                out_ref[piece, :, place : place + size] = result[piece * depth : (piece + 1) * depth]
+            place += size
+
+    @pl.when(pl.program_id(0) == 0)
+    def _():
+        put(sent_ref)
+
+    @pl.when(pl.program_id(0) == 1)
+    def _():
+        put(kept_ref)
+
+
+def weight_grad(mine, bit, total, pairs):
+    low = bit.bit_length() - 1
+    half = total // 2
+    rows = pairs[0][0].shape[0]
+    depth = pairs[0][0].shape[1] // total
+
+    def pick(piece):
+        return lambda g, at: (0, piece_at(g * half + piece, total, low, at[0], bit))
+
+    def fixed(place):
+        return lambda g, at: (0, place)
+
+    in_specs, operands, width = [], [], 0
+    for left, right, place, size in pairs:
+        in_specs += [pl.BlockSpec((rows, depth), pick(piece)) for piece in range(half)]
+        in_specs.append(pl.BlockSpec((rows, size), fixed(place)))
+        operands += [left] * half + [right]
+        width += size
+    out = (half, depth, width)
+    return pl.pallas_call(
+        partial(grad_kernel, half, len(pairs)),
+        grid_spec=pltpu.PrefetchScalarGridSpec(
+            num_scalar_prefetch=1,
+            grid=(2,),
+            in_specs=in_specs,
+            out_specs=[pl.BlockSpec(out, lambda g, at: (0, 0, 0))] * 2,
+        ),
+        out_shape=[jax.ShapeDtypeStruct(out, F32)] * 2,
+        compiler_params=params(),
+        cost_estimate=LIGHT,
+        name="weight_grad",
+    )(mine, *operands)
+
+
+def down_grad_kernel(grad_ref, activ_ref, out_ref):
+    out_ref[...] = dot1(grad_ref[...], activ_ref[...], TN)
+
+
+def down_grad(grad, activ):
+    rows, model = grad.shape
+    steps = 4
+    tile = model // steps
+    return pl.pallas_call(
+        down_grad_kernel,
+        grid=(steps,),
+        in_specs=[pl.BlockSpec((rows, tile), lambda g: (0, g)), whole(activ.shape)],
+        out_specs=pl.BlockSpec((tile, activ.shape[1]), lambda g: (g, 0)),
+        out_shape=jax.ShapeDtypeStruct((model, activ.shape[1]), F32),
+        compiler_params=params(),
+        cost_estimate=LIGHT,
+        name="down_grad",
+    )(grad, activ)
+
+
+def combine_kernel(bit, mine_ref, kept_ref, arrived_ref, sent_ref, next_ref):
+    side = (mine_ref[0] // bit) % 2
+    sent_ref[...] = (kept_ref[:, 1 - side] + arrived_ref[:, 1 - side]).reshape(sent_ref.shape)
+    next_ref[...] = (kept_ref[:, side] + arrived_ref[:, side]).reshape(next_ref.shape)
+
+
+IN_VMEM = pl.BlockSpec(memory_space=pltpu.VMEM)
+
+
+def combine(mine, bit, low, kept, arrived):
+    total, rows, columns = kept.shape
+    half = total // 2
+    view = lambda array: array.reshape((half >> low, 2, 1 << low, rows, columns))
+    return pl.pallas_call(
+        partial(combine_kernel, bit),
+        in_specs=[SCALARS, IN_VMEM, IN_VMEM],
+        out_specs=[IN_VMEM, IN_VMEM],
+        out_shape=[jax.ShapeDtypeStruct((half, rows, columns), F32)] * 2,
+        compiler_params=params(),
+        cost_estimate=LIGHT,
+        name="combine",
+    )(mine, view(kept), view(arrived))
+
+
+def norm_back_kernel(
+    place_ref, kept_ref, arrived_ref, value_ref, gain_ref, residual_ref, out_ref
+):
+    step = pl.program_id(0)
+    tile = kept_ref.shape[0]
+    rows = out_ref.shape[0] - EDGE
+    values = value_ref[...].astype(F32)
+    grad = kept_ref[...] + arrived_ref[...]
+    scale = lax.rsqrt(jnp.mean(values * values, -1, keepdims=True) + EPSILON)
+    normed = values * scale
+    through = grad * gain_ref[...]
+    back = scale * (through - normed * jnp.mean(through * normed, -1, keepdims=True))
+    out_ref[pl.ds(pl.multiple_of(step * tile, tile), tile)] = back + residual_ref[...].astype(F32)
+    sums = jnp.sum((grad * normed).reshape(-1, EDGE, grad.shape[1]), 0)
+
+    @pl.when(step == 0)
+    def _():
+        out_ref[rows:] = sums
+
+    @pl.when(step != 0)
+    def _():
+        out_ref[rows:] += sums
+
+
+def norm_back(place, kept, arrived, values, gain, residual):
+    rows, model = kept.shape
+    steps = 2
+    tile = rows // steps
+    local = pl.BlockSpec((tile, model), lambda g, at: (g, 0))
+
+    def spec_of(array):
+        if array.shape[0] == rows + EDGE:
+            return local
+        return pl.BlockSpec((tile, model), lambda g, at: (at[0] * steps + g, 0))
+
+    return pl.pallas_call(
+        norm_back_kernel,
+        grid_spec=pltpu.PrefetchScalarGridSpec(
+            num_scalar_prefetch=1,
+            grid=(steps,),
+            in_specs=[
+                local,
+                local,
+                spec_of(values),
+                pl.BlockSpec((1, model), lambda g, at: (0, 0)),
+                spec_of(residual),
+            ],
+            out_specs=pl.BlockSpec((rows + EDGE, model), lambda g, at: (0, 0)),
+        ),
+        out_shape=jax.ShapeDtypeStruct((rows + EDGE, model), F32),
+        compiler_params=params(),
+        cost_estimate=LIGHT,
+        name="norm_back",
+    )(place, kept, arrived, values, gain, residual)
+
+
+def own_output_kernel(kept_ref, arrived_ref, middle_ref, gain_ref, out_ref):
+    rows, model = kept_ref.shape
+    width = gain_ref.shape[1]
+    out_ref[:rows] = kept_ref[...] + arrived_ref[...] + middle_ref[...]
+    out_ref[rows:] = jnp.concatenate(
+        [gain_ref[...], jnp.zeros((EDGE, model - width), F32)], 1
+    )
+
+
+def own_output(place, kept, arrived, middle, grad_gain):
+    rows, model = kept.shape
+    return pl.pallas_call(
+        lambda place_ref, *refs: own_output_kernel(*refs),
+        grid_spec=pltpu.PrefetchScalarGridSpec(
+            num_scalar_prefetch=1,
+            grid=(1,),
+            in_specs=[
+                pl.BlockSpec((rows, model), lambda g, at: (0, 0)),
+                pl.BlockSpec((rows, model), lambda g, at: (0, 0)),
+                pl.BlockSpec((rows, model), lambda g, at: (at[0], 0)),
+                pl.BlockSpec(grad_gain.shape, lambda g, at: (0, 0)),
+            ],
+            out_specs=pl.BlockSpec((rows + EDGE, model), lambda g, at: (0, 0)),
+        ),
+        out_shape=jax.ShapeDtypeStruct((rows + EDGE, model), F32),
+        compiler_params=params(),
+        cost_estimate=LIGHT,
+        name="own_output",
+    )(place, kept, arrived, middle, grad_gain)
+
+
+def pack_kernel(heads, first_ref, second_ref, gain_ref, *refs):
+    decay_refs, taps_refs, out_ref = refs[:heads], refs[heads : 2 * heads], refs[-1]
+    place = 0
+    for ref in (first_ref, second_ref):
+        for start in range(0, ref.shape[1], LANES):
+            out_ref[place : place + 1] = jnp.sum(ref[:, start : start + LANES], 0, keepdims=True)
+            place += 1
+    for ref in taps_refs:
+        for start in range(0, ref.shape[1], LANES):
+            out_ref[place : place + EDGE] = ref[:, start : start + LANES]
+            place += EDGE
+    out_ref[place : place + EDGE] = gain_ref[:, :LANES]
+    out_ref[place + EDGE : place + 2 * EDGE] = sum(ref[...] for ref in decay_refs)
+
+
+def pack_small(first, second, gain, decays, taps):
+    columns = sum(part.shape[1] for part in taps)
+    rows = 2 * (first.shape[1] // LANES) + EDGE * (columns // LANES) + 2 * EDGE
+    return pl.pallas_call(
+        partial(pack_kernel, len(taps)),
+        out_shape=jax.ShapeDtypeStruct((rows, LANES), F32),
+        compiler_params=params(),
+        cost_estimate=LIGHT,
+        name="pack_small",
+    )(first, second, gain, *decays, *taps)
+
+
+def unpack_kernel(
+    mine_ref, small_ref, first_ref, second_ref, gain_ref, decay_ref, taps_ref, *, count, model
+):
+    blocks = model // LANES
+    size = model // count
+    index = mine_ref[0]
+    for base, ref in ((0, first_ref), (blocks, second_ref)):
+        row = small_ref[pl.ds(base + index * size // LANES, 1)]
+        if size < LANES:
+            row = pltpu.roll(row, (LANES - index * size % LANES) % LANES, 1)
+        ref[...] = row[:, :size]
+    place = 2 * blocks
+    for start in range(0, taps_ref.shape[1], LANES):
+        taps_ref[:, start : start + LANES] = small_ref[place : place + CONV]
+        place += EDGE
+    gain_ref[...] = jnp.sum(small_ref[place : place + EDGE], 0, keepdims=True)
+    decay_ref[...] = small_ref[place + EDGE : place + 2 * EDGE]
+
+
+def unpack_small(mine, small, count, model, columns):
+    size = model // count
+    shapes = [(1, size), (1, size), (1, LANES), (EDGE, LANES), (CONV, columns)]
+    return pl.pallas_call(
+        partial(unpack_kernel, count=count, model=model),
+        in_specs=[SCALARS, IN_VMEM],
+        out_shape=[jax.ShapeDtypeStruct(shape, F32) for shape in shapes],
+        compiler_params=params(),
+        cost_estimate=LIGHT,
+        name="unpack_small",
+    )(mine, small)
+
+
 def exchange(value, axis, bit):
     count = lax.axis_size(axis)
     return lax.ppermute(value, axis, [(place, place ^ bit) for place in range(count)])
@@ -777,26 +1355,97 @@
     return [1 << power for power in range(count.bit_length() - 1)]
 
 
-def gather_near(value, axis):
-    found = [value]
-    for bit in reversed(bits_of(axis)):
-        found = [found, [exchange(part, axis, bit) for part in found]]
-        found = found[0] + found[1]
-    order = [0]
-    for bit in reversed(bits_of(axis)):
-        order = order + [place ^ bit for place in order]
-    return [part for _, part in sorted(zip(order, found), key=lambda pair: pair[0])]
-
-
-def scatter_sum(pieces, axis):
-    mine = lax.axis_index(axis)
-    for bit in bits_of(axis):
-        side = (mine // bit) % 2
-        pairs = pieces.reshape((pieces.shape[0] // 2, 2) + pieces.shape[1:])
-        kept = lax.dynamic_index_in_dim(pairs, side, 1, keepdims=False)
-        sent = lax.dynamic_index_in_dim(pairs, 1 - side, 1, keepdims=False)
-        pieces = kept + exchange(sent, axis, bit)
-    return pieces[0]
+class GatherNear:
+    def __init__(self, value, axis):
+        self.axis = axis
+        self.bits = bits_of(axis)
+        self.found = {0: value}
+        for bit in self.bits[::-1]:
+            self.found[bit] = exchange(value, axis, bit)
+
+    def finish(self, *others):
+        for bit in self.bits[::-1]:
+            if others and bit == self.bits[-1]:
+                self.found[bit] = after(self.found[bit], *others)
+            for near in sorted(self.found):
+                if near > bit and not near & bit and near | bit not in self.found:
+                    self.found[near | bit] = exchange(self.found[near], self.axis, bit)
+        return [self.found[near] for near in sorted(self.found)]
+
+
+def gather_near(value, axis, *others):
+    start = GatherNear(value, axis)
+    others = sum([list(one()) if callable(one) else [one] for one in others], [])
+    return start.finish(*others)
+
+
+def after(value, *others):
+    return lax.optimization_barrier((value,) + others)[0]
+
+
+def join(*values):
+    return lax.optimization_barrier(values)
+
+
+class Scatter:
+    def __init__(self, mine, axis, order, kept, sent):
+        self.mine = mine
+        self.axis = axis
+        self.bits = sorted(order)
+        self.order = list(order)
+        self.kept = kept
+        self.sent = sent
+
+    def send(self):
+        bit = self.order.pop(0)
+        self.bits.remove(bit)
+        self.arrived = exchange(self.sent, self.axis, bit)
+        self.sent = None
+        return self
+
+    def add(self):
+        if self.order:
+            bit = self.order[0]
+            self.sent, self.kept = combine(
+                self.mine, bit, self.bits.index(bit), self.kept, self.arrived
+            )
+        else:
+            self.total = self.kept[0] + self.arrived[0]
+        return self
+
+    def step(self):
+        self.add()
+        return self.send() if self.order else self
+
+
+class WholeSum:
+    def __init__(self, pairs):
+        self.kept = self.sent = jnp.concatenate(
+            [
+                contract(left, lax.slice_in_dim(right, place * size, (place + 1) * size, axis=1), 0, 0)
+                for left, right, place, size in pairs
+            ],
+            1,
+        )
+        self.order = []
+
+    def send(self):
+        self.arrived = lax.psum_scatter(self.sent, "seq", scatter_dimension=0, tiled=True)
+        return self
+
+    def add(self):
+        self.total = self.kept = self.arrived
+        return self
+
+    def step(self):
+        return self.add()
+
+
+def arrive(*scatters, also=()):
+    found = join(*[one.arrived for one in scatters], *also)
+    for one, value in zip(scatters, found):
+        one.arrived = value
+    return found[len(scatters) :]
 
 
 def contract(left, right, left_dim, right_dim):
@@ -805,13 +1454,14 @@
     )
 
 
-def carried_in(total, own, axis, backward):
+def carried_in(total, own, axis, backward, maps=None):
     count = lax.axis_size(axis)
     sign = -1 if backward else 1
     reach = count - DOCS - 1
     if reach > DOCS - 1:
         reach = count - 1
     dims = (1, 1) if backward else (2, 1)
+    width = LANES
 
     def move(map_of, state):
         return lax.dot_general(
@@ -819,10 +1469,16 @@
         )
 
     if reach < count - 1:
-        maps = [shifted(total, axis, sign * step) for step in range(1, reach)]
-        terms = [shifted(own, axis, sign * step) for step in range(1, reach + 1)]
+        if own is None:
+            both = [shifted(total, axis, sign * step) for step in range(1, reach)]
+            maps = [pair[..., :width] for pair in both]
+            terms = [pair[..., width:] for pair in both]
+            terms.append(shifted(total[..., width:], axis, sign * reach))
+        else:
+            terms = [shifted(own, axis, sign * step) for step in range(1, reach + 1)]
     else:
-        every_map, every_term = lax.all_gather(total, axis), lax.all_gather(own, axis)
+        every_map = lax.all_gather(total[..., :width], axis)
+        every_term = lax.all_gather(total[..., width:] if own is None else own, axis)
         mine = lax.axis_index(axis)
 
         def at(array, step):
@@ -838,70 +1494,21 @@
     return state
 
 
+def maps_between(total, axis):
+    count = lax.axis_size(axis)
+    reach = count - DOCS - 1
+    if reach > DOCS - 1:
+        return None
+    return [shifted(total[..., :LANES], axis, -step) for step in range(1, reach)]
+
+
 def normalize(values):
     return values * lax.rsqrt(jnp.mean(values * values, -1, keepdims=True) + EPSILON)
-
-
-def norm_back(values, gain, grad):
-    scale = lax.rsqrt(jnp.mean(values * values, -1, keepdims=True) + EPSILON)
-    normed = values * scale
-    through = grad * gain
-    back = scale * (through - normed * jnp.mean(through * normed, -1, keepdims=True))
-    return back, jnp.sum(grad * normed, 0)
 
 
 def lanes_of(per_head):
     row = jnp.repeat(per_head, STEPS + 1)
     return jnp.pad(row, (0, LANES - row.shape[0]))[None]
-
-
-def place_rows(parts, axis):
-    mine = lax.axis_index(axis)
-    count = len(parts)
-    rows = parts[0].shape[0]
-    out = jnp.zeros((count * rows,) + parts[0].shape[1:], parts[0].dtype)
-    for near, part in enumerate(parts):
-        out = lax.dynamic_update_slice_in_dim(out, part, (mine ^ near) * rows, 0)
-    return out
-
-
-def project_kernel(parts, *refs):
-    gated_refs, weight_refs = refs[:parts], refs[parts : 2 * parts]
-    input_ref, gain_ref, middle_ref, normed_ref, low_ref = refs[2 * parts :]
-
-    @pl.when(pl.program_id(0) == 0)
-    def _():
-        for part in range(parts):
-            low_ref[part] = weight_refs[part][...].astype(BF16)
-
-    middle = input_ref[...].astype(F32)
-    for part in range(parts):
-        middle = middle + dot1(gated_refs[part][...], low_ref[part], NN)
-    middle_ref[...] = middle
-    scale = lax.rsqrt(jnp.mean(middle * middle, -1, keepdims=True) + EPSILON)
-    normed_ref[...] = (middle * scale * gain_ref[...]).astype(BF16)
-
-
-def mixer_project(gated_near, weight_near, block_input, gain):
-    parts = len(gated_near)
-    rows, model = block_input.shape
-    tile = rows // 4
-    depth = gated_near[0].shape[1]
-    return pl.pallas_call(
-        partial(project_kernel, parts),
-        grid=(rows // tile,),
-        in_specs=[pl.BlockSpec((tile, depth), lambda g: (g, 0))] * parts
-        + [whole((depth, model))] * parts
-        + [pl.BlockSpec((tile, model), lambda g: (g, 0)), whole((1, model))],
-        out_specs=[pl.BlockSpec((tile, model), lambda g: (g, 0))] * 2,
-        out_shape=[
-            jax.ShapeDtypeStruct((rows, model), F32),
-            jax.ShapeDtypeStruct((rows, model), BF16),
-        ],
-        scratch_shapes=[pltpu.VMEM((parts, depth, model), BF16)],
-        compiler_params=params(),
-        name="mixer_project",
-    )(*gated_near, *weight_near, block_input, gain)
 
 
 def body(
@@ -926,62 +1533,133 @@
     parts = lax.axis_size("head")
     quarter = rows // parts
     head_index = lax.axis_index("head")
+    seq, seq_index = lax.axis_size("seq"), lax.axis_index("seq")
     gain1, gain2 = first_gain.astype(F32), second_gain.astype(F32)
     head_gain_row = head_gain.astype(F32)[None]
     taps = conv_taps.astype(F32)
     rate_row, bias_row = lanes_of(log_rate), lanes_of(rate_bias)
     rate_lanes = w_rates.shape[1]
     w_rates_wide = jnp.pad(w_rates, ((0, 0), (0, LANES - rate_lanes)))
-
-    inputs_f = block_input.astype(F32)
-    normed1_low = (normalize(inputs_f) * gain1).astype(BF16)
-    mixing = contract(normed1_low, w_mix, 1, 0)
-    edge = shifted(mixing[rows - EDGE :], "seq", 1)
-    rates = contract(normed1_low, w_rates_wide, 1, 0)
-    outgate = contract(normed1_low, w_outgate, 1, 0)
+    ffn_flat = w_ffn.reshape(model, -1)
+
+    head_bits = bits_of("head")
+    core = head_index % 2
+    kept_half, sent_half = core[None], (1 - core)[None]
+
+    def block_of(index):
+        return sum(
+            ((index // bit) % 2) * (parts // (2 * bit)) for bit in head_bits
+        )
+
+    places = jnp.stack([block_of(head_index ^ near) for near in range(parts)]).astype(jnp.int32)
+    own_block = places[0]
+    own_rows = lambda array: lax.dynamic_slice_in_dim(array, own_block * quarter, quarter, 0)
+
+    head_mine, seq_mine = head_index[None], seq_index[None]
+    head_order, seq_bits = head_bits, bits_of("seq")
+
+    raw_edge = shifted(block_input[rows - EDGE :].astype(F32), "seq", 1)
+    normed1_low, mixing, rates, outgate = first_projections(
+        block_input, gain1[None], w_mix, w_rates_wide, w_outgate
+    )
     w_out_near = gather_near(w_out.astype(F32), "head")
-
-    conv, q, k, x, system, cumul, u, w, scores, query_map, prefix, phi, total = local_maps(
-        seq_starts, edge, mixing, taps, rates, rate_row, bias_row
+    edge, conv, q, k, x, system, cumul, u, w, scores, query_map, prefix, phi, total = local_maps(
+        seq_starts, raw_edge, gain1[None], w_mix, mixing, taps, rates, rate_row, bias_row
     )
     width = LANES
-    device_map, device_term = total[..., :width], total[..., width:]
-    incoming = carried_in(device_map, device_term, "seq", False)
+    incoming = carried_in(total, None, "seq", False)
     state, fresh, mixed, gated = outputs_of(
         seq_starts, incoming, (prefix, u, w, scores, q, cumul), outgate, head_gain_row, F32
     )
-    gated_near = gather_near(gated, "head")
-    middle, normed2_low = mixer_project(gated_near, w_out_near, block_input, gain2[None])
-    ffn_flat = w_ffn.reshape(model, -1)
-    hidden_units = ffn_flat.shape[1] // 2
-    both = contract(normed2_low, ffn_flat, 1, 0)
-    gate, up = both[:, :hidden_units], both[:, hidden_units:]
-    sigma = jax.nn.sigmoid(gate)
-    activ_low = (gate * sigma * up).astype(BF16)
-    grad_activ = contract(grad_output, w_down, 1, 1)
-    grad_gate = grad_activ * up * (sigma * (1.0 + gate * (1.0 - sigma)))
-    grad_up = grad_activ * (gate * sigma)
-    grad_both = jnp.concatenate([grad_gate, grad_up], 1).astype(BF16)
-    normed2_part = contract(grad_both, ffn_flat, 1, 1)
-    grad_normed2 = scatter_sum(normed2_part.reshape(parts, quarter, model), "head")
-
-    own_rows = lambda array: lax.dynamic_slice_in_dim(array, head_index * quarter, quarter, 0)
-    grad_middle_own, grad_second_gain = norm_back(own_rows(middle), gain2, grad_normed2)
-    grad_middle_own = grad_middle_own + own_rows(grad_output).astype(F32)
-    grad_middle = place_rows(gather_near(grad_middle_own, "head"), "head")
-    grad_branch = grad_middle.astype(BF16)
-    grad_gated = contract(grad_branch, w_out, 1, 1)
-    grad_mixed, outgate_low, grad_gain, term, grad_total = gate_back(
-        grad_gated, mixed, outgate, head_gain_row, query_map, prefix
-    )
-    leaving = carried_in(device_map, grad_total, "seq", True)
-
-    ffn_out = lax.psum(contract(activ_low, w_down, 1, 0), "head")
-    block_output = (middle + ffn_out).astype(BF16)
-    grad_ffn = contract(normed2_low, grad_both, 0, 0)
-    grad_down = contract(activ_low, grad_output, 0, 0)
-    grad_out = contract(gated.astype(BF16), grad_branch, 0, 0)
-
+    gated_start = GatherNear(gated, "head")
+    w_out_low, ffn_flat = low_weight([after(piece, gated) for piece in w_out_near], ffn_flat)
+    maps = maps_between(after(total, gated), "seq") or ()
+    ffn_flat, w_out_low, *maps = join(ffn_flat, w_out_low, *maps)
+    gated_near = gated_start.finish(ffn_flat, w_out_low)
+
+    dense = lambda half, filled: dense_half(
+        half, gated_near, w_out_low, block_input, gain2[None], ffn_flat, w_down, grad_output, filled
+    )
+    *filled, back_sent, fore_sent = dense(sent_half, None)
+    split = lambda half: half.reshape(parts // 2, quarter, model)
+    back = Scatter(head_mine, "head", head_order, None, split(back_sent)).send()
+    *filled, back_kept, fore_kept = dense(kept_half, filled)
+    middle, normed2_low, activ_low, *grads_both = filled
+    back.kept = split(back_kept)
+    back.step()
+
+    near_first, far_first = seq_bits, seq_bits[1:] + seq_bits[:1]
+    tiled = model // seq % LANES == 0
+
+    def grad_sum(order, *pairs, tie=()):
+        (left, *rest), *others = pairs
+        pairs = [(after(left, *tie), *rest)] + others
+        if not tiled:
+            return WholeSum(pairs)
+        sent, kept = weight_grad(seq_mine, order[0], seq, pairs)
+        return Scatter(seq_mine, "seq", order, kept, sent)
+
+    ffn_sums, tie = [], back.kept
+    for order, right in zip((near_first, far_first, near_first), grads_both):
+        ffn_sums.append(grad_sum(order, (normed2_low, right, 0, right.shape[1]), tie=(tie,)))
+        tie = ffn_sums[-1].kept
+    ffn_one, ffn_two, ffn_three = ffn_sums
+    ffn_one.send()
+    ffn_two.send()
+    fore = Scatter(
+        head_mine, "head", head_order, split(fore_kept), after(split(fore_sent), back.kept)
+    ).send()
+    down_sum = grad_sum(
+        near_first, (grad_output, activ_low, 0, activ_low.shape[1]), tie=(ffn_three.kept,)
+    )
+    ffn_three.sent, down_sum.sent = arrive(
+        back, fore, ffn_one, ffn_two, also=(ffn_three.sent, down_sum.sent)
+    )
+    grad_middle_own = norm_back(
+        places[:1], back.kept[0], back.arrived[0], middle, gain2[None], grad_output
+    )
+
+    middle_start = GatherNear(grad_middle_own, "head")
+    ffn_three.sent = after(ffn_three.sent, grad_middle_own)
+    ffn_three.send()
+    tie = grad_middle_own
+    for one in (ffn_one, ffn_two):
+        one.arrived = after(one.arrived, tie)
+        one.step()
+        tie = one.kept
+    fore.arrived = after(fore.arrived, tie)
+    fore.add()
+    middle_start.found[2], fore.sent = arrive(
+        *ffn_sums, also=(middle_start.found[2], fore.sent)
+    )
+
+    fore.send()
+    grad_branch, grad_mixed, outgate_low, grad_gain, term, grad_total, grad_second_gain = gate_back(
+        places, middle_start.finish(), w_out, mixed, outgate, head_gain_row, query_map, prefix
+    )
+    leaving = carried_in(total, grad_total, "seq", True, maps)
+    out_width, outgate_width = gated.shape[1], outgate_low.shape[1]
+    side_sum = grad_sum(
+        near_first,
+        (grad_branch, gated.astype(BF16), 0, out_width),
+        (normed1_low, outgate_low, 0, outgate_width),
+        tie=(grad_total,),
+    )
+    tie = side_sum.kept
+    for one in (ffn_three, ffn_one):
+        one.arrived = after(one.arrived, tie)
+        one.add()
+        tie = one.kept
+    leaving, side_sum.sent, ffn_three.sent, ffn_one.sent, down_sum.sent = arrive(
+        fore, also=(leaving, side_sum.sent, ffn_three.sent, ffn_one.sent, down_sum.sent)
+    )
+    output_own = own_output(places[:1], fore.kept[0], fore.arrived[0], middle, grad_gain)
+
+    output_start = GatherNear(output_own, "head")
+    down_sum.send()
+    ffn_three.send()
+    ffn_one.send()
+    leaving, output_start.found[1] = join(after(leaving, output_own), output_start.found[1])
     grad_mix_rows, last_rows, before_rows, rate_low, decay_sums, grad_taps = recurrence_back(
         seq_starts,
         leaving,
@@ -994,56 +1672,123 @@
         mixing,
         taps,
     )
+    before_rows, output_start.found[2] = arrive(
+        ffn_one, ffn_three, down_sum, also=(before_rows, output_start.found[2])
+    )
+
     returned = shifted(before_rows, "seq", -1)
+    down_sum.add()
+    ffn_three.arrived = after(ffn_three.arrived, down_sum.kept)
+    ffn_three.add()
+    returned, side_sum.sent, down_sum.sent, ffn_three.sent = join(
+        returned, side_sum.sent, down_sum.sent, ffn_three.sent
+    )
+    for one in (side_sum, down_sum, ffn_three):
+        one.send()
     last_rows = last_rows + jnp.pad(returned, ((EDGE, 0), (0, 0)))
     mixing_low = lax.dynamic_update_slice_in_dim(
         grad_mix_rows, last_rows.astype(BF16), rows - 2 * EDGE, 0
     )
-    normed1_part = (
-        contract(mixing_low, w_mix, 1, 1)
-        + contract(rate_low, w_rates_wide, 1, 1)
-        + contract(outgate_low, w_outgate, 1, 1)
-    )
-    grad_normed1 = scatter_sum(normed1_part.reshape(parts, quarter, model), "head")
-    from_norm, grad_first_gain = norm_back(own_rows(inputs_f), gain1, grad_normed1)
-    grad_input = place_rows(gather_near(grad_middle_own + from_norm, "head"), "head")
-    grad_mix = contract(normed1_low, mixing_low, 0, 0)
-    grad_rates = contract(normed1_low, rate_low, 0, 0)[:, :rate_lanes]
-    grad_outgate = contract(normed1_low, outgate_low, 0, 0)
-
-    seq = lax.axis_size("seq")
-    seq_index = lax.axis_index("seq")
-    split_rows = lambda array: array.reshape(seq, array.shape[0] // seq, array.shape[1])
-    split_columns = lambda array: jnp.moveaxis(array.reshape(array.shape[0], seq, -1), 1, 0)
-    ffn_sum = scatter_sum(split_rows(grad_ffn), "seq")
-    down_sum = scatter_sum(split_columns(grad_down), "seq")
-    out_sum = scatter_sum(split_columns(grad_out), "seq")
-    mix_sum = scatter_sum(split_rows(grad_mix), "seq")
-    outgate_sum = scatter_sum(split_rows(grad_outgate), "seq")
-    rates_sum = lax.psum_scatter(grad_rates, "seq", scatter_dimension=0, tiled=True)
-    taps_sum, decay_sum = lax.psum((grad_taps[:CONV], decay_sums[:2]), "seq")
-    gains = lax.psum(
-        (grad_first_gain, grad_second_gain, jnp.sum(grad_gain, 0)), ("seq", "head")
-    )
-    own_gain = lambda array: lax.dynamic_slice_in_dim(
-        array, seq_index * (model // seq), model // seq, 0
+    columns = mixing_low.shape[1]
+    half_columns, narrow = columns // 2, columns // 10
+    mix_one = grad_sum(near_first, (normed1_low, mixing_low, 0, half_columns))
+    part_sent, part_kept = first_back(
+        kept_half,
+        (after(mixing_low, mix_one.kept), outgate_low, rate_low),
+        (w_mix, w_outgate, w_rates_wide),
+    )
+    output_near = output_start.finish()
+    part_sent, part_kept, mix_one.sent, *output_near = arrive(
+        side_sum, down_sum, ffn_three,
+        also=(part_sent, part_kept, mix_one.sent, *output_near),
+    )
+    part = Scatter(head_mine, "head", head_order, split(part_kept), split(part_sent)).send()
+    part.step()
+    mix_one.send()
+    tie = part.kept
+    for one in (side_sum, down_sum):
+        one.arrived = after(one.arrived, tie)
+        one.step()
+        tie = one.kept
+
+    mix_two = grad_sum(
+        near_first,
+        *[(normed1_low, mixing_low, 5 + piece, narrow) for piece in range(3)],
+        tie=(tie,),
+    ).send()
+    output, grad_head_gain = place_rows(
+        places, [after(piece, mix_two.kept) for piece in output_near], BF16
+    )
+    mix_three = grad_sum(
+        near_first,
+        *[(normed1_low, mixing_low, 8 + piece, narrow) for piece in range(2)],
+        (normed1_low, rate_low, 0, LANES),
+        tie=(output,),
+    )
+    mix_one.arrived = after(mix_one.arrived, mix_three.kept)
+    mix_one.step()
+    mix_three.sent, _ = arrive(
+        part, side_sum, down_sum, also=(mix_three.sent, mix_one.kept)
+    )
+    grad_input_own = norm_back(
+        places[:1], part.kept[0], part.arrived[0], block_input, gain1[None], grad_middle_own
+    )
+
+    input_start = GatherNear(grad_input_own, "head")
+    mix_three.sent, side_sum.arrived, _ = join(mix_three.sent, side_sum.arrived, grad_input_own)
+    mix_three.send()
+    tie = grad_input_own
+    for one in (side_sum, mix_two):
+        one.arrived = after(one.arrived, tie)
+        one.step()
+        tie = one.kept
+    mix_one.arrived, side_sum.arrived, _ = join(mix_one.arrived, side_sum.arrived, tie)
+    mix_one.step()
+    input_start.found[2], tie = arrive(
+        mix_two, mix_three, also=(input_start.found[2], mix_one.kept)
+    )
+    for one in (mix_three, mix_two):
+        one.step()
+    grad_input, grad_first_gain = place_rows(places, input_start.finish(), F32)
+    ffn_two.arrived, mix_three.arrived, _ = join(ffn_two.arrived, mix_three.arrived, grad_input)
+    ffn_two.step()
+    small = pack_small(
+        grad_first_gain,
+        grad_second_gain,
+        grad_head_gain,
+        [decay_sums],
+        [grad_taps],
+    )
+    for bit in seq_bits:
+        small = small + exchange(small, "seq", bit)
+    gain1_own, gain2_own, gain_sum, decay_sum, taps_sum = unpack_small(
+        seq_mine, small, seq, model, mixing.shape[1]
     )
     decay_lanes = decay_sum[:, STEPS : heads * (STEPS + 1) : STEPS + 1]
+
+    def total_of(one):
+        while one.order:
+            one.step()
+        return one.add().total
+
+    side_total = total_of(side_sum)
+    ffn_total = jnp.concatenate([total_of(one) for one in ffn_sums], 1)
+    mix_total = jnp.concatenate([total_of(one) for one in (mix_one, mix_two, mix_three)], 1)
     return (
-        block_output,
+        output,
         grad_input,
-        own_gain(gains[0]),
-        mix_sum,
+        gain1_own[0],
+        mix_total[:, :columns],
         taps_sum,
-        rates_sum,
+        mix_total[:, columns : columns + rate_lanes],
         decay_lanes[0],
         decay_lanes[1],
-        outgate_sum,
-        gains[2],
-        out_sum,
-        own_gain(gains[1]),
-        ffn_sum.reshape((-1,) + w_ffn.shape[1:]),
-        down_sum,
+        side_total[:, out_width:],
+        gain_sum[0],
+        side_total[:, :out_width].T,
+        gain2_own[0],
+        ffn_total.reshape((-1,) + w_ffn.shape[1:]),
+        total_of(down_sum)[:, : w_down.shape[0]].T,
     )
 
 

time: 635 us -> 449 us (0.71)
  Pallas kernels: 87.4 us -> 230 us
  blocking collectives: 137 us -> 0 us
  waiting for transfers between devices: 183 us -> 79.8 us
  matrix products: 53.9 us -> 2.63 us
  starting transfers between devices: 54.8 us -> 89.9 us
  other arithmetic: 44.6 us -> 12.7 us
  local copies, waits for them, and re-layouts: 49.6 us -> 24 us
  between operations: 17.3 us -> 2.29 us
    pallas_call x2 -> x40, Pallas kernels: 18.8 us -> 169 us  [the longest x19 49.2 us: combine(): pl.pallas_call(partial(combine_kernel, bit), in_specs=[SCALARS, IN_VMEM,...]
    psum x2 -> x0, blocking collectives: 137 us -> none  [the longest x1 92.2 us: body(): taps_sum, decay_sum = lax.psum((grad_taps[:CONV], decay_sums[:2]), 'seq')]
    ppermute x31 -> x48, waiting for transfers between devices: 174 us -> 75.2 us  [exchange(): lax.ppermute(value, axis, [(place, place ^ bit) for place in range(count)])]
    dot_general x17 -> x0, matrix products: 49.4 us -> none  [contract(): lax.dot_general(left, right, (((left_dim,), (right_dim,)), ((), ())), pre...]
    ppermute x31 -> x48, starting transfers between devices: 23.1 us -> 67.3 us  [exchange(): lax.ppermute(value, axis, [(place, place ^ bit) for place in range(count)])]
    dynamic_update_slice x6 -> x0, local copies, waits for them, and re-layouts: 12.8 us -> none  [place_rows(): out = lax.dynamic_update_slice_in_dim(out, part, (mine ^ near) * rows, 0)]
    squeeze x17 -> x0, local copies, waits for them, and re-layouts: 11.3 us -> none  [scatter_sum(): sent = lax.dynamic_index_in_dim(pairs, 1 - side, 1, keepdims=False)]
    add x13 -> x11, other arithmetic: 14.7 us -> 4.69 us  [the longest x8 4.05 us: add(): self.total = self.kept[0] + self.arrived[0]]
  transfers between devices with their start and end apart: 45 -> 58, of which waited for: 12 -> 16; matrix products, arithmetic and copies ran while one was open for 17% -> 6% of each run, Pallas kernels for 8% -> 48%
where the time goes in v2:
time: 449 us; the launch traced here: 441 us
  Pallas kernels  230 us (51%)
  starting transfers between devices  89.9 us (20%)
  waiting for transfers between devices  79.8 us (18%)
  local copies, waits for them, and re-layouts  24 us (5%)
  other arithmetic  12.7 us (3%)
    ppermute x48, waiting for transfers between devices, exchange(): lax.ppermute(value, axis, [(place, place ^ bit) for place in range(count)])  75.2 us
    ppermute x48, starting transfers between devices, exchange(): lax.ppermute(value, axis, [(place, place ^ bit) for place in range(count)])  67.3 us
    pallas_call x19, Pallas kernels, combine(): pl.pallas_call(partial(combine_kernel, bit), in_specs=[SCALARS, IN_VMEM,...  49.2 us
    pallas_call x8, Pallas kernels, weight_grad(): pl.pallas_call(partial(grad_kernel, half, len(pairs)), grid_spec=pltpu.Pr...  42.9 us
    pallas_call x1, Pallas kernels, local_maps(): pl.pallas_call(partial(local_kernel, heads), grid=(blocks // PACK,), in_s...  25.9 us
    pallas_call x1, Pallas kernels, recurrence_back(): pl.pallas_call(partial(back_kernel, heads), grid=(steps,), in_specs=[SCAL...  25.8 us
    pallas_call x2, Pallas kernels, dense_half(): pl.pallas_call(partial(dense_kernel, parts), grid_spec=pltpu.PrefetchScal...  25 us
    ppermute x10, starting transfers between devices, shifted(): lax.ppermute(value, axis, [(source, source + steps) for source in range(f...  22.6 us
  transfers between devices with their start and end apart: 58, of which 16 were waited for; matrix products, arithmetic and copies ran while one was open for 6% of the time, Pallas kernels for 48%

profile of v2, /device:TPU:0, one launch (start us, length us, event | category | flops | bytes accessed | tf_op | source)
XLA Modules:
  0.0 440.8 jit_solution(9539926647401776410)
XLA Ops:
  14.1 8.5 %first_projections.1 = (bf16[1024,1024]{1,0:T(8,128)(2,1)}, f32[1024,1280]{1,0:T(8,128)}, f32[1024,128]{1,0:T(8,128)}, f32[1024,256]{1,0:T(8,128)}) custom-call(bf16[1024,1024]{1,0:T(8,128)(2,1)} %value_ref.1, f32[1,1024]{1,0:T(1,128)} %bitcast.141, bf16[1024,1280]{1,0:T(8,128)(2,1)} %refs_3_.2, bf16[1024,128]{1,0:T(8,128)(2,1)} %pad.15.rates_ref.refs_5_, ...), custom_call_target="tpu_custom_call" | custom-call | flops 1 | bytes 1 | tf_op jit(solution)/shard_map/first_projections/pallas_call | solution.py:616
  24.4 25.9 %local_maps.1 = (f32[8,1280]{1,0:T(8,128)}, f32[1024,1280]{1,0:T(8,128)}, f32[2,16,64,128]{3,2,1,0:T(8,128)}, bf16[2,16,128,128]{3,2,1,0:T(8,128)(2,1)}, bf16[2,...) custom-call(s32[1]{0:T(128)S(6)} %copy.59.offset_ref, ...), custom_call_target="tpu_custom_call" | custom-call | flops 1 | bytes 1 | tf_op jit(solution)/shard_map/local_maps/pallas_call | solution.py:283
  58.4 4.4 collective-permute-start.3
  67.2 8.3 %mixer_outputs.1 = (bf16[2,16,128,128]{3,2,1,0:T(8,128)(2,1)}, bf16[2,16,128,128]{3,2,1,0:T(8,128)(2,1)}, f32[1024,256]{1,0:T(8,128)}, f32[1024,256]{1,0:T(8,128)}) custom-call(s32[1]{0:T(128)S(6)} %copy.59.offset_ref, f32[2,128,128]{2,1,0:T(8,128)} %convolution_add_fusion.2.incoming_ref, f32[2,16,128,256]{3,2,1,0:T(8,128)} %get-tuple-element.222.prefix_ref.refs_9_, ...), custom_call_target="tpu_custom_call" | custom-call | flops 1 | bytes 1 | tf_op jit(solution)/shard_map/mixer_outputs/pallas_call | solution.py:376
  78.9 4.6 %copy.44.refs_4_ = bf16[1024,1408]{1,0:T(8,128)(2,1)} copy(bf16[1024,1408]{0,1:T(8,128)(2,1)} %bitcast.99) | data formatting | bytes 5767168 | tf_op jit(solution)/shard_map/reshape | solution.py:1543
  89.1 12.3 %collective-permute-done.5.refs_3_ = f32[1024,256]{1,0:T(8,128)S(1)} collective-permute-done((f32[1024,256]{1,0:T(8,128)}, f32[1024,256]{1,0:T(8,128)S(1)}, u32[]{:S(2)}, u32[]{:S(2)}) %collective-permute-start.5) | collective-permute-done | bytes 1048608 | tf_op jit(solution)/shard_map/ppermute | solution.py:1344
  104.2 12.5 %dense_half.2 = (f32[1024,1024]{1,0:T(8,128)}, bf16[1024,1024]{1,0:T(8,128)(2,1)}, bf16[1024,768]{1,0:T(8,128)(2,1)}, bf16[1024,384]{1,0:T(8,128)(2,1)}, bf16[10...) custom-call(s32[1]{0:T(128)} %bitcast.12.refs_0_, ...), custom_call_target="tpu_custom_call" | custom-call | flops 1 | bytes 1 | tf_op jit(solution)/shard_map/dense_half/pallas_call | solution.py:707
  116.8 12.5 %dense_half.3 = (f32[1024,1024]{1,0:T(8,128)}, bf16[1024,1024]{1,0:T(8,128)(2,1)}, bf16[1024,768]{1,0:T(8,128)(2,1)}, bf16[1024,384]{1,0:T(8,128)(2,1)}, bf16[10...) custom-call(s32[1]{0:T(128)} %bitcast.5.refs_0_.place_ref, ...), custom_call_target="tpu_custom_call", output_to_operand_aliasing={{0}: (11, {}), {1}: (12, {}), {2}: (13, {}), {3}: (14, {}),... | custom-call | flops 1 | bytes 1 | tf_op jit(solution)/shard_map/dense_half/pallas_call | solution.py:707
  151.4 5.4 %weight_grad.10 = (f32[4,128,640]{2,1,0:T(8,128)}, f32[4,128,640]{2,1,0:T(8,128)}) custom-call(s32[1]{0:T(128)} %bitcast.4.refs_0_.mine_ref, bf16[1024,1024]{1,0:T(8,128)(2,1)} %get-tuple-element.261.refs_1_.refs_2_.refs_3_.refs_4_, bf16[1024,1024]{1,0:T(8,128)(2,1)} %get-tuple-element.261.refs_1_.refs_2_.refs_3_.refs_4_, ...), custom_call_target="tpu_custom_call" | custom-call | flops 1 | bytes 1 | tf_op jit(solution)/shard_map/weight_grad/pallas_call | solution.py:1137
  156.8 6.0 %weight_grad.11 = (f32[4,128,768]{2,1,0:T(8,128)}, f32[4,128,768]{2,1,0:T(8,128)}) custom-call(s32[1]{0:T(128)} %bitcast.4.refs_0_.mine_ref, bf16[1024,1024]{1,0:T(8,128)(2,1)} %residual_ref.1, bf16[1024,1024]{1,0:T(8,128)(2,1)} %residual_ref.1, bf16[1024,1024]{1,0:T(8,128)(2,1)} %residual_ref.1, bf16[1024,1024]{1,0:T(8,128)(2,1)} %residual_ref.1, ...), custom_call_target="tpu_custom_call" | custom-call | flops 1 | bytes 1 | tf_op jit(solution)/shard_map/weight_grad/pallas_call | solution.py:1137
  162.8 6.2 %collective-permute-done.16 = f32[4,128,384]{2,1,0:T(8,128)} collective-permute-done((f32[4,128,384]{2,1,0:T(8,128)}, f32[4,128,384]{2,1,0:T(8,128)}, u32[]{:S(2)}, u32[]{:S(2)}) %collective-permute-start.16) | collective-permute-done | bytes 786464 | tf_op jit(solution)/shard_map/ppermute | solution.py:1344
  181.8 4.5 %collective-permute-start.18 = (f32[2,128,384]{2,1,0:T(8,128)}, f32[2,128,384]{2,1,0:T(8,128)S(1)}, u32[]{:S(2)}, u32[]{:S(2)}) collective-permute-start(f32[2,128,384]{2,1,0:T(8,128)} %get-tuple-element.276), channel_id=1, source_target_pairs={{0,16},{4,20},{8,24},{12,28},{16,0},{20,4},{24,8},{28,12},{1,17},{... | collective-permute-start | bytes 1179656 | tf_op jit(solution)/shard_map/ppermute | solution.py:1344
  193.6 8.4 %collective-permute-done.18 = f32[2,128,384]{2,1,0:T(8,128)S(1)} collective-permute-done((f32[2,128,384]{2,1,0:T(8,128)}, f32[2,128,384]{2,1,0:T(8,128)S(1)}, u32[]{:S(2)}, u32[]{:S(2)}) %collective-permute-start.18) | collective-permute-done | bytes 393248 | tf_op jit(solution)/shard_map/ppermute | solution.py:1344
  206.4 10.7 %gate_back.1 = (bf16[1024,1024]{1,0:T(8,128)(2,1)}, bf16[1024,256]{1,0:T(8,128)(2,1)}, bf16[1024,256]{1,0:T(8,128)(2,1)}, f32[8,128]{1,0:T(8,128)}, f32[2,16,128...) custom-call(s32[4]{0:T(128)} %pad_add_fusion.place_ref, f32[264,1024]{1,0:T(8,128)} %norm_back.2.refs_0_.residual_ref, ...), custom_call_target="tpu_custom_call" | custom-call | flops 1 | bytes 1 | tf_op jit(solution)/shard_map/gate_back/pallas_call | solution.py:498
  221.8 5.0 %weight_grad.12 = (f32[4,128,512]{2,1,0:T(8,128)}, f32[4,128,512]{2,1,0:T(8,128)}) custom-call(s32[1]{0:T(128)} %bitcast.4.refs_0_.mine_ref, bf16[1024,1024]{1,0:T(8,128)(2,1)} %get-tuple-element.292.refs_1_.refs_2_.refs_3_.refs_4_, bf16[1024,1024]{1,0:T(8,128)(2,1)} %get-tuple-element.292.refs_1_.refs_2_.refs_3_.refs_4_, ...), custom_call_target="tpu_custom_call" | custom-call | flops 1 | bytes 1 | tf_op jit(solution)/shard_map/weight_grad/pallas_call | solution.py:1137
  246.5 25.8 %recurrence_back.1 = (bf16[1024,1280]{1,0:T(8,128)(2,1)}, f32[16,1280]{1,0:T(8,128)}, f32[8,1280]{1,0:T(8,128)}, bf16[1024,128]{1,0:T(8,128)(2,1)}, f32[8,128]{1,0:T(8,128)}, /*index=5*/f32[8,1280]{1,0:T(8,128)}) custom-call(s32[1]{0:T(128)S(6)} %copy.59.offset_ref, f32[2,128,128]{2,1,0:T(8,128)} %convolution_add_fusion.leaving_ref, ...), custom_call_target="tpu_custom_call" | custom-call | flops 1 | bytes 1 | tf_op jit(solution)/shard_map/recurrence_back/pallas_call | solution.py:1017
  287.2 5.8 %weight_grad.13 = (f32[4,128,640]{2,1,0:T(8,128)}, f32[4,128,640]{2,1,0:T(8,128)}) custom-call(s32[1]{0:T(128)} %bitcast.4.refs_0_.mine_ref, bf16[1024,1024]{1,0:T(8,128)(2,1)} %get-tuple-element.371.refs_6_.refs_7_.refs_8_.refs_9_.refs_1_.refs_2_.refs_3_.refs_4_.refs_11_.refs_12_.refs_13_.refs_14_, ...), custom_call_target="tpu_custom_call" | custom-call | flops 1 | bytes 1 | tf_op jit(solution)/shard_map/weight_grad/pallas_call | solution.py:1137
  293.1 8.9 %first_back.1 = (f32[512,1024]{1,0:T(8,128)}, f32[512,1024]{1,0:T(8,128)}) custom-call(s32[1]{0:T(128)} %bitcast.5.refs_0_.place_ref, bf16[1024,1280]{1,0:T(8,128)(2,1)} %fusion.2.refs_5_.refs_0_.refs_10_.refs_15_, bf16[1024,256]{1,0:T(8,128)(2,1)} %get-tuple-element.294.refs_10_.refs_1_, bf16[1024,128]{1,0:T(8,128)(2,1)} %get-tuple-element.342.refs_2_.refs_15_, ...), custom_call_target="tpu_custom_call" | custom-call | flops 1 | bytes 1 | tf_op jit(solution)/shard_map/first_back/pallas_call | solution.py:757
  301.9 5.6 %collective-permute-done.35 = f32[1,128,640]{2,1,0:T(8,128)S(1)} collective-permute-done((f32[1,128,640]{2,1,0:T(8,128)}, f32[1,128,640]{2,1,0:T(8,128)S(1)}, u32[]{:S(2)}, u32[]{:S(2)}) %collective-permute-start.35) | collective-permute-done | bytes 327712 | tf_op jit(solution)/shard_map/ppermute | solution.py:1344
  329.2 6.1 %weight_grad.14 = (f32[4,128,384]{2,1,0:T(8,128)}, f32[4,128,384]{2,1,0:T(8,128)}) custom-call(s32[1]{0:T(128)} %bitcast.4.refs_0_.mine_ref, bf16[1024,1024]{1,0:T(8,128)(2,1)} %get-tuple-element.371.refs_6_.refs_7_.refs_8_.refs_9_.refs_1_.refs_2_.refs_3_.refs_4_.refs_11_.refs_12_.refs_13_.refs_14_, ...), custom_call_target="tpu_custom_call" | custom-call | flops 1 | bytes 1 | tf_op jit(solution)/shard_map/weight_grad/pallas_call | solution.py:1137
  340.2 6.1 %weight_grad.15 = (f32[4,128,384]{2,1,0:T(8,128)}, f32[4,128,384]{2,1,0:T(8,128)}) custom-call(s32[1]{0:T(128)} %bitcast.4.refs_0_.mine_ref, bf16[1024,1024]{1,0:T(8,128)(2,1)} %get-tuple-element.371.refs_6_.refs_7_.refs_8_.refs_9_.refs_1_.refs_2_.refs_3_.refs_4_.refs_11_.refs_12_.refs_13_.refs_14_, ...), custom_call_target="tpu_custom_call" | custom-call | flops 1 | bytes 1 | tf_op jit(solution)/shard_map/weight_grad/pallas_call | solution.py:1137
  366.2 13.7 %collective-permute-done.47 = f32[2,128,640]{2,1,0:T(8,128)S(1)} collective-permute-done((f32[2,128,640]{2,1,0:T(8,128)S(1)}, f32[2,128,640]{2,1,0:T(8,128)S(1)}, u32[]{:S(2)}, u32[]{:S(2)}) %collective-permute-start.47) | collective-permute-done | bytes 655392 | tf_op jit(solution)/shard_map/ppermute | solution.py:1344
  392.2 4.5 %place_rows.3 = (f32[1024,1024]{1,0:T(8,128)}, f32[8,1024]{1,0:T(8,128)}) custom-call(s32[4]{0:T(128)} %pad_add_fusion.place_ref, f32[264,1024]{1,0:T(8,128)} %norm_back.3.refs_0_, f32[264,1024]{1,0:T(8,128)} %collective-permute-done.42.refs_1_, f32[264,1024]{1,0:T(8,128)} %copy-done.17, f32[264,1024]{1,0:T(8,128)} %collective-permute-done.49.refs_3_), custom_call_target="tpu_custom_call" | custom-call | flops 1 | bytes 1 | tf_op jit(solution)/shard_map/place_rows/pallas_call | solution.py:549
  409.2 10.7 %collective-permute-done.51 = f32[112,128]{1,0:T(8,128)S(1)} collective-permute-done((f32[112,128]{1,0:T(8,128)S(1)}, f32[112,128]{1,0:T(8,128)S(1)}, u32[]{:S(2)}, u32[]{:S(2)}) %collective-permute-start.51) | collective-permute-done | bytes 57376 | tf_op jit(solution)/shard_map/ppermute | solution.py:1344
  (284 shorter events, 216.1 us)
Async XLA Ops:
  1.8 64.4 %collective-permute-start.7 = (f32[256,1024]{1,0:T(8,128)S(1)}, f32[256,1024]{1,0:T(8,128)}, u32[]{:S(2)}, u32[]{:S(2)}) collective-permute-start(f32[256,1024]{1,0:T(8,128)S(1)} %convert_element_type.27.refs_0_), channel_id=1, source_target_pairs={{0,2},{1,3},{2,0},{3,1},{4,6},{5,7},{6,4},{7,5},{8,10},{9,11},{10,... | collective-permute-start | bytes 3145736 | tf_op jit(solution)/shard_map/ppermute | solution.py:1344
  53.9 29.6 %collective-permute-start.6 = (f32[256,1024]{1,0:T(8,128)S(1)}, f32[256,1024]{1,0:T(8,128)}, u32[]{:S(2)}, u32[]{:S(2)}) collective-permute-start(f32[256,1024]{1,0:T(8,128)S(1)} %convert_element_type.27.refs_0_), channel_id=1, source_target_pairs={{0,1},{1,0},{2,3},{3,2},{4,5},{5,4},{6,7},{7,6},{8,9},{9,8},{10,11... | collective-permute-start | bytes 3145736 | tf_op jit(solution)/shard_map/ppermute | solution.py:1344
  75.5 25.8 %collective-permute-start.5 = (f32[1024,256]{1,0:T(8,128)}, f32[1024,256]{1,0:T(8,128)S(1)}, u32[]{:S(2)}, u32[]{:S(2)}) collective-permute-start(f32[1024,256]{1,0:T(8,128)} %get-tuple-element.229.refs_1_), channel_id=1, source_target_pairs={{0,2},{1,3},{2,0},{3,1},{4,6},{5,7},{6,4},{7,5},{8,10},{9,11},{10,... | collective-permute-start | bytes 3145736 | tf_op jit(solution)/shard_map/ppermute | solution.py:1344
  134.5 34.5 %collective-permute-start.14 = (f32[2,256,1024]{2,1,0:T(8,128)}, f32[2,256,1024]{2,1,0:T(8,128)S(1)}, u32[]{:S(2)}, u32[]{:S(2)}) collective-permute-start(f32[2,256,1024]{2,1,0:T(8,128)} %bitcast.18), channel_id=1, source_target_pairs={{0,1},{1,0},{2,3},{3,2},{4,5},{5,4},{6,7},{7,6},{8,9},{9,8},{10,11... | collective-permute-start | bytes 6291464 | tf_op jit(solution)/shard_map/ppermute | solution.py:1344
  134.9 34.1 %collective-permute-start.13 = (f32[1,256,1024]{2,1,0:T(8,128)}, f32[1,256,1024]{2,1,0:T(8,128)S(1)}, u32[]{:S(2)}, u32[]{:S(2)}) collective-permute-start(f32[1,256,1024]{2,1,0:T(8,128)} %get-tuple-element.253), channel_id=1, source_target_pairs={{0,2},{1,3},{2,0},{3,1},{4,6},{5,7},{6,4},{7,5},{8,10},{9,11},{10,... | collective-permute-start | bytes 3145736 | tf_op jit(solution)/shard_map/ppermute | solution.py:1344
  173.4 29.8 %collective-permute-start.19 = (f32[4,128,640]{2,1,0:T(8,128)S(1)}, f32[4,128,640]{2,1,0:T(8,128)}, u32[]{:S(2)}, u32[]{:S(2)}) collective-permute-start(f32[4,128,640]{2,1,0:T(8,128)S(1)} %copy-done.47), channel_id=1, source_target_pairs={{0,4},{4,0},{8,12},{12,8},{16,20},{20,16},{24,28},{28,24},{1,5},{5... | collective-permute-start | bytes 3932168 | tf_op jit(solution)/shard_map/ppermute | solution.py:1344
  173.8 28.2 %collective-permute-start.20 = (f32[264,1024]{1,0:T(8,128)}, f32[264,1024]{1,0:T(8,128)S(1)}, u32[]{:S(2)}, u32[]{:S(2)}) collective-permute-start(f32[264,1024]{1,0:T(8,128)} %norm_back.2.refs_0_.residual_ref), channel_id=1, source_target_pairs={{0,2},{1,3},{2,0},{3,1},{4,6},{5,7},{6,4},{7,5},{8,10},{9,11},{10,... | collective-permute-start | bytes 3244040 | tf_op jit(solution)/shard_map/ppermute | solution.py:1344
  203.2 30.0 %collective-permute-start.21 = (f32[1,256,1024]{2,1,0:T(8,128)}, f32[1,256,1024]{2,1,0:T(8,128)}, u32[]{:S(2)}, u32[]{:S(2)}) collective-permute-start(f32[1,256,1024]{2,1,0:T(8,128)} %get-tuple-element.284), channel_id=1, source_target_pairs={{0,2},{1,3},{2,0},{3,1},{4,6},{5,7},{6,4},{7,5},{8,10},{9,11},{10,... | collective-permute-start | bytes 3145736 | tf_op jit(solution)/shard_map/ppermute | solution.py:1344
  233.2 39.1 %collective-permute-start.29 = (f32[4,128,768]{2,1,0:T(8,128)S(1)}, f32[4,128,768]{2,1,0:T(8,128)S(1)}, u32[]{:S(2)}, u32[]{:S(2)}) collective-permute-start(f32[4,128,768]{2,1,0:T(8,128)S(1)} %copy-done.46), channel_id=1, source_target_pairs={{0,4},{4,0},{8,12},{12,8},{16,20},{20,16},{24,28},{28,24},{1,5},{5... | collective-permute-start | bytes 4718600 | tf_op jit(solution)/shard_map/ppermute | solution.py:1344
  238.9 33.4 %collective-permute-start.31 = (f32[264,1024]{1,0:T(8,128)}, f32[264,1024]{1,0:T(8,128)S(1)}, u32[]{:S(2)}, u32[]{:S(2)}) collective-permute-start(f32[264,1024]{1,0:T(8,128)} %own_output.1.refs_0_), channel_id=1, source_target_pairs={{0,2},{1,3},{2,0},{3,1},{4,6},{5,7},{6,4},{7,5},{8,10},{9,11},{10,... | collective-permute-start | bytes 3244040 | tf_op jit(solution)/shard_map/ppermute | solution.py:1344
  240.1 32.2 %collective-permute-start.28 = (f32[2,128,640]{2,1,0:T(8,128)S(1)}, f32[2,128,640]{2,1,0:T(8,128)S(1)}, u32[]{:S(2)}, u32[]{:S(2)}) collective-permute-start(f32[2,128,640]{2,1,0:T(8,128)S(1)} %copy-done.48), channel_id=1, source_target_pairs={{0,8},{4,12},{8,0},{12,4},{16,24},{20,28},{24,16},{28,20},{1,9},{5... | collective-permute-start | bytes 1966088 | tf_op jit(solution)/shard_map/ppermute | solution.py:1344
  242.8 29.5 %collective-permute-start.27 = (f32[1,128,384]{2,1,0:T(8,128)S(1)}, f32[1,128,384]{2,1,0:T(8,128)S(1)}, u32[]{:S(2)}, u32[]{:S(2)}) collective-permute-start(f32[1,128,384]{2,1,0:T(8,128)S(1)} %copy-done.50), channel_id=1, source_target_pairs={{0,16},{4,20},{8,24},{12,28},{16,0},{20,4},{24,8},{28,12},{1,17},{... | collective-permute-start | bytes 589832 | tf_op jit(solution)/shard_map/ppermute | solution.py:1344
  273.7 35.1 %collective-permute-start.36 = (f32[264,1024]{1,0:T(8,128)S(1)}, f32[264,1024]{1,0:T(8,128)S(1)}, u32[]{:S(2)}, u32[]{:S(2)}) collective-permute-start(f32[264,1024]{1,0:T(8,128)S(1)} %collective-permute-done.31.refs_2_), channel_id=1, source_target_pairs={{0,1},{1,0},{2,3},{3,2},{4,5},{5,4},{6,7},{7,6},{8,9},{9,8},{10,11... | collective-permute-start | bytes 3244040 | tf_op jit(solution)/shard_map/ppermute | solution.py:1344
  279.2 29.5 %collective-permute-start.33 = (f32[4,128,512]{2,1,0:T(8,128)}, f32[4,128,512]{2,1,0:T(8,128)S(1)}, u32[]{:S(2)}, u32[]{:S(2)}) collective-permute-start(f32[4,128,512]{2,1,0:T(8,128)} %get-tuple-element.334), channel_id=1, source_target_pairs={{0,4},{4,0},{8,12},{12,8},{16,20},{20,16},{24,28},{28,24},{1,5},{5... | collective-permute-start | bytes 3145736 | tf_op jit(solution)/shard_map/ppermute | solution.py:1344
  281.9 26.9 %collective-permute-start.34 = (f32[2,128,768]{2,1,0:T(8,128)}, f32[2,128,768]{2,1,0:T(8,128)S(1)}, u32[]{:S(2)}, u32[]{:S(2)}) collective-permute-start(f32[2,128,768]{2,1,0:T(8,128)} %get-tuple-element.335), channel_id=1, source_target_pairs={{0,8},{4,12},{8,0},{12,4},{16,24},{20,28},{24,16},{28,20},{1,9},{5... | collective-permute-start | bytes 2359304 | tf_op jit(solution)/shard_map/ppermute | solution.py:1344
  282.7 24.8 %collective-permute-start.35 = (f32[1,128,640]{2,1,0:T(8,128)}, f32[1,128,640]{2,1,0:T(8,128)S(1)}, u32[]{:S(2)}, u32[]{:S(2)}) collective-permute-start(f32[1,128,640]{2,1,0:T(8,128)} %get-tuple-element.336), channel_id=1, source_target_pairs={{0,16},{4,20},{8,24},{12,28},{16,0},{20,4},{24,8},{28,12},{1,17},{... | collective-permute-start | bytes 983048 | tf_op jit(solution)/shard_map/ppermute | solution.py:1344
  308.9 37.4 %collective-permute-start.41 = (f32[4,128,640]{2,1,0:T(8,128)}, f32[4,128,640]{2,1,0:T(8,128)S(1)}, u32[]{:S(2)}, u32[]{:S(2)}) collective-permute-start(f32[4,128,640]{2,1,0:T(8,128)} %get-tuple-element.373), channel_id=1, source_target_pairs={{0,4},{4,0},{8,12},{12,8},{16,20},{20,16},{24,28},{28,24},{1,5},{5... | collective-permute-start | bytes 3932168 | tf_op jit(solution)/shard_map/ppermute | solution.py:1344
  318.3 31.9 %collective-permute-start.38 = (f32[1,256,1024]{2,1,0:T(8,128)}, f32[1,256,1024]{2,1,0:T(8,128)S(1)}, u32[]{:S(2)}, u32[]{:S(2)}) collective-permute-start(f32[1,256,1024]{2,1,0:T(8,128)} %get-tuple-element.368), channel_id=1, source_target_pairs={{0,2},{1,3},{2,0},{3,1},{4,6},{5,7},{6,4},{7,5},{8,10},{9,11},{10,... | collective-permute-start | bytes 3145736 | tf_op jit(solution)/shard_map/ppermute | solution.py:1344
  321.8 28.4 %collective-permute-start.39 = (f32[2,128,512]{2,1,0:T(8,128)}, f32[2,128,512]{2,1,0:T(8,128)S(1)}, u32[]{:S(2)}, u32[]{:S(2)}) collective-permute-start(f32[2,128,512]{2,1,0:T(8,128)} %get-tuple-element.369), channel_id=1, source_target_pairs={{0,8},{4,12},{8,0},{12,4},{16,24},{20,28},{24,16},{28,20},{1,9},{5... | collective-permute-start | bytes 1572872 | tf_op jit(solution)/shard_map/ppermute | solution.py:1344
  335.3 23.4 %collective-permute-start.43 = (f32[4,128,384]{2,1,0:T(8,128)}, f32[4,128,384]{2,1,0:T(8,128)S(1)}, u32[]{:S(2)}, u32[]{:S(2)}) collective-permute-start(f32[4,128,384]{2,1,0:T(8,128)} %get-tuple-element.378), channel_id=1, source_target_pairs={{0,4},{4,0},{8,12},{12,8},{16,20},{20,16},{24,28},{28,24},{1,5},{5... | collective-permute-start | bytes 2359304 | tf_op jit(solution)/shard_map/ppermute | solution.py:1344
  354.8 31.1 %collective-permute-start.46 = (f32[264,1024]{1,0:T(8,128)}, f32[264,1024]{1,0:T(8,128)S(1)}, u32[]{:S(2)}, u32[]{:S(2)}) collective-permute-start(f32[264,1024]{1,0:T(8,128)} %norm_back.3.refs_0_), channel_id=1, source_target_pairs={{0,2},{1,3},{2,0},{3,1},{4,6},{5,7},{6,4},{7,5},{8,10},{9,11},{10,... | collective-permute-start | bytes 3244040 | tf_op jit(solution)/shard_map/ppermute | solution.py:1344
  355.8 30.2 %collective-permute-start.45 = (f32[4,128,384]{2,1,0:T(8,128)}, f32[4,128,384]{2,1,0:T(8,128)S(1)}, u32[]{:S(2)}, u32[]{:S(2)}) collective-permute-start(f32[4,128,384]{2,1,0:T(8,128)} %get-tuple-element.386), channel_id=1, source_target_pairs={{0,4},{4,0},{8,12},{12,8},{16,20},{20,16},{24,28},{28,24},{1,5},{5... | collective-permute-start | bytes 2359304 | tf_op jit(solution)/shard_map/ppermute | solution.py:1344
  356.6 23.3 %collective-permute-start.47 = (f32[2,128,640]{2,1,0:T(8,128)S(1)}, f32[2,128,640]{2,1,0:T(8,128)S(1)}, u32[]{:S(2)}, u32[]{:S(2)}) collective-permute-start(f32[2,128,640]{2,1,0:T(8,128)S(1)} %copy-done.49), channel_id=1, source_target_pairs={{0,8},{4,12},{8,0},{12,4},{16,24},{20,28},{24,16},{28,20},{1,9},{5... | collective-permute-start | bytes 1966088 | tf_op jit(solution)/shard_map/ppermute | solution.py:1344
  362.0 23.9 %collective-permute-start.44 = (f32[2,128,384]{2,1,0:T(8,128)}, f32[2,128,384]{2,1,0:T(8,128)S(1)}, u32[]{:S(2)}, u32[]{:S(2)}) collective-permute-start(f32[2,128,384]{2,1,0:T(8,128)} %get-tuple-element.385), channel_id=1, source_target_pairs={{0,8},{4,12},{8,0},{12,4},{16,24},{20,28},{24,16},{28,20},{1,9},{5... | collective-permute-start | bytes 1179656 | tf_op jit(solution)/shard_map/ppermute | solution.py:1344
  (86 other events, 1026.0 us)

commit v3 on v2

--- a/solution.py
+++ b/solution.py
@@ -65,6 +65,15 @@
     return (place < offset) & (offset <= place + reach)
 
 
+def lane_row(ref, heads):
+    lane = iota((1, LANES), 1)
+    row = jnp.zeros((1, LANES), F32)
+    for head in range(heads):
+        here = (lane >= head * (STEPS + 1)) & (lane < (head + 1) * (STEPS + 1))
+        row = jnp.where(here, ref[head], row)
+    return row
+
+
 def rate_parts(raw, rate_row, bias_row):
     shifted_raw = raw + bias_row
     soft = jnp.maximum(shifted_raw, 0.0) + jnp.log1p(jnp.exp(-jnp.abs(shifted_raw)))
@@ -100,16 +109,13 @@
 def local_kernel(
     heads,
     offset_ref,
-    raw_ref,
-    gain_ref,
-    weight_ref,
+    log_rate_ref,
+    rate_bias_ref,
+    edge_ref,
     halo_ref,
     mix_ref,
     taps_ref,
     rates_ref,
-    rate_row_ref,
-    bias_row_ref,
-    edge_ref,
     conv_ref,
     q_ref,
     k_ref,
@@ -133,9 +139,6 @@
 
     @pl.when(step == 0)
     def _():
-        raw = raw_ref[...]
-        scale = lax.rsqrt(jnp.mean(raw * raw, -1, keepdims=True) + EPSILON)
-        edge_ref[...] = dot1(raw * scale * gain_ref[...], weight_ref[...], NN)
         run_ref[...] = jnp.concatenate([jnp.broadcast_to(eye, run_ref.shape[:2] + (width,)), jnp.zeros(run_ref.shape[:2] + (width,), F32)], 2)
 
     place = step * rows + iota((rows, width), 0)
@@ -145,17 +148,20 @@
         cols = slice(part * width, (part + 1) * width)
         before = jnp.where(step == 0, edge_ref[:, cols], halo_ref[:, cols])
         wide = jnp.concatenate([before, mix_ref[:, cols]], 0)
-        conv = taps_ref[CONV - 1 : CONV, cols] * wide[EDGE:]
+        taps = taps_ref[:, cols].astype(F32)
+        conv = taps[CONV - 1 : CONV] * wide[EDGE:]
         for back in range(1, CONV):
             moved = pltpu.roll(wide, back, 0)[EDGE:]
-            conv = conv + taps_ref[CONV - 1 - back : CONV - back, cols] * (moved * keep[back])
+            conv = conv + taps[CONV - 1 - back : CONV - back] * (moved * keep[back])
         conv_ref[:, cols] = conv
         act = conv * jax.nn.sigmoid(conv)
         if 1 <= part % GROUPS < 1 + STEPS:
             act = act * lax.rsqrt(jnp.sum(act * act, -1, keepdims=True) + EPSILON)
         acts.append(act)
 
-    beta_all, decay_all, _ = rate_parts(rates_ref[...], rate_row_ref[...], bias_row_ref[...])
+    beta_all, decay_all, _ = rate_parts(
+        rates_ref[...], lane_row(log_rate_ref, heads), lane_row(rate_bias_ref, heads)
+    )
     lower = (iota((SPAN, SPAN), 1) <= iota((SPAN, SPAN), 0)).astype(F32)
     chains = [(pos, head) for pos in range(rows // SPAN) for head in range(heads)]
     cumuls = [
@@ -259,7 +265,7 @@
 LIGHT = pl.CostEstimate(flops=1, bytes_accessed=1, transcendentals=0)
 
 
-def local_maps(offset, raw, gain, weight, mixing, taps, rates, rate_row, bias_row):
+def local_maps(offset, log_rate, rate_bias, edge, mixing, taps, rates):
     rows, columns = mixing.shape
     width = LANES
     heads = columns // (GROUPS * width)
@@ -285,30 +291,25 @@
         grid=(blocks // PACK,),
         in_specs=[
             SCALARS,
-            whole(raw.shape),
-            whole(gain.shape),
-            whole(weight.shape),
+            SCALARS,
+            SCALARS,
+            whole((EDGE, columns)),
             pl.BlockSpec((EDGE, columns), lambda g: (jnp.maximum(g * (tile // EDGE) - 1, 0), 0)),
             pl.BlockSpec((tile, columns), lambda g: (g, 0)),
             whole(taps.shape),
             pl.BlockSpec((tile, LANES), lambda g: (g, 0)),
-            whole((1, LANES)),
-            whole((1, LANES)),
         ],
-        out_specs=[whole((EDGE, columns)), pl.BlockSpec((tile, columns), lambda g: (g, 0))]
+        out_specs=[pl.BlockSpec((tile, columns), lambda g: (g, 0))]
         + [spec for spec, _, _ in saved]
         + [whole((heads, width, 2 * width))],
-        out_shape=[
-            jax.ShapeDtypeStruct((EDGE, columns), F32),
-            jax.ShapeDtypeStruct((rows, columns), F32),
-        ]
+        out_shape=[jax.ShapeDtypeStruct((rows, columns), F32)]
         + [jax.ShapeDtypeStruct((heads, blocks) + dims, kind) for _, dims, kind in saved]
         + [jax.ShapeDtypeStruct((heads, width, 2 * width), F32)],
         scratch_shapes=[pltpu.VMEM((heads, width, 2 * width), F32)],
         compiler_params=params(),
         cost_estimate=LIGHT,
         name="local_maps",
-    )(offset, raw, gain, weight, mixing, mixing, taps, rates, rate_row, bias_row)
+    )(offset, log_rate, rate_bias, edge, mixing, mixing, taps, rates)
 
 
 def output_kernel(
@@ -355,12 +356,12 @@
     for (pos, head), state, fresh, mixed in zip(chains, states, freshes, outs):
         here = slice(pos * SPAN, (pos + 1) * SPAN)
         cols = slice(head * width, (head + 1) * width)
-        state_ref[head, pos] = state.astype(BF16)
-        fresh_ref[head, pos] = fresh.astype(BF16)
+        state_ref[head, pos] = state
+        fresh_ref[head, pos] = fresh
         mixed_ref[here, cols] = mixed
         scale = lax.rsqrt(jnp.mean(mixed * mixed, -1, keepdims=True) + EPSILON)
         outgate = outgate_ref[here, cols]
-        gated = mixed * scale * gain_ref[...] * (outgate * jax.nn.sigmoid(outgate))
+        gated = mixed * scale * gain_ref[...].astype(F32) * (outgate * jax.nn.sigmoid(outgate))
         gated_ref[here, cols] = gated.astype(BF16).astype(gated_ref.dtype)
 
 
@@ -390,8 +391,8 @@
         ],
         out_specs=[per_block(width, width), per_block(virt, width), flat, flat],
         out_shape=[
-            jax.ShapeDtypeStruct((heads, blocks, width, width), BF16),
-            jax.ShapeDtypeStruct((heads, blocks, virt, width), BF16),
+            jax.ShapeDtypeStruct((heads, blocks, width, width), F32),
+            jax.ShapeDtypeStruct((heads, blocks, virt, width), F32),
             jax.ShapeDtypeStruct((rows, heads * width), F32),
             jax.ShapeDtypeStruct((rows, heads * width), gated_type),
         ],
@@ -415,14 +416,17 @@
         gain_ref,
         query_ref,
         prefix_ref,
+    ) = refs[parts : parts + 6]
+    before = refs[parts + 6 : -7]
+    (
+        grad_gain_ref,
+        total_ref,
+        sum_ref,
         branch_ref,
         grad_mixed_ref,
         grad_outgate_ref,
-        grad_gain_ref,
         term_ref,
-        total_ref,
-        sum_ref,
-    ) = refs[parts:]
+    ) = refs[-7:]
     step = pl.program_id(0)
     pack = prefix_ref.shape[1]
     width = LANES
@@ -433,6 +437,10 @@
         sum_ref[...] = sum(ref[rows:] for ref in piece_refs)
         grad_gain_ref[...] = jnp.zeros_like(grad_gain_ref)
         total_ref[...] = jnp.zeros_like(total_ref)
+        if before:
+            grad_gain_ref[...] = before[0][...]
+            total_ref[...] = before[1][...]
+            sum_ref[...] += before[2][...]
 
     for near in range(parts):
 
@@ -441,7 +449,7 @@
             branch_ref[...] = piece_refs[near][:rows].astype(BF16)
 
     grad_all = dot1(branch_ref[...], weight_ref[...], NT)
-    gain = gain_ref[...]
+    gain = gain_ref[...].astype(F32)
     grads_mixed = []
     for head in range(heads):
         cols = slice(head * width, (head + 1) * width)
@@ -477,13 +485,13 @@
         total_ref[head] = totals[head]
 
 
-def gate_back(place, pieces, weight, mixed, outgate, gain, query, prefix):
+def gate_back(place, pieces, weight, mixed, outgate, gain, query, prefix, before):
     heads, blocks = prefix.shape[:2]
     width = LANES
     parts = len(pieces)
     model = pieces[0].shape[1]
     rows = mixed.shape[0]
-    tile = rows // parts
+    tile = pieces[0].shape[0] - EDGE
     pack = tile // SPAN
 
     def fixed(*shape):
@@ -495,43 +503,43 @@
     def flat(size):
         return pl.BlockSpec((tile, size), lambda g, at: (at[g], 0))
 
+    in_specs = [fixed(tile + EDGE, model)] * parts + [
+        fixed(*weight.shape),
+        flat(heads * width),
+        flat(heads * width),
+        fixed(1, width),
+        per_block(SPAN, width),
+        per_block(width, width),
+    ]
+    operands = [place, *pieces, weight, mixed, outgate, gain, query, prefix]
+    totals = [(8, width), (heads, width, width), (EDGE, model)]
+    aliases = {}
+    if before is not None:
+        aliases = {len(operands) + 3 + index: 3 + index for index in range(4)}
+        in_specs += [fixed(*shape) for shape in totals]
+        in_specs += [pl.BlockSpec(memory_space=pl.ANY)] * 4
+        operands += list(before)
     return pl.pallas_call(
         partial(gate_back_kernel, heads, parts),
         grid_spec=pltpu.PrefetchScalarGridSpec(
             num_scalar_prefetch=1,
             grid=(parts,),
-            in_specs=[fixed(tile + EDGE, model)] * parts
-            + [
-                fixed(*weight.shape),
-                flat(heads * width),
-                flat(heads * width),
-                fixed(1, width),
-                per_block(SPAN, width),
-                per_block(width, width),
-            ],
-            out_specs=[
-                flat(model),
-                flat(heads * width),
-                flat(heads * width),
-                fixed(8, width),
-                per_block(width, width),
-                fixed(heads, width, width),
-                fixed(EDGE, model),
-            ],
+            in_specs=in_specs,
+            out_specs=[fixed(*shape) for shape in totals]
+            + [flat(model), flat(heads * width), flat(heads * width), per_block(width, width)],
         ),
-        out_shape=[
+        out_shape=[jax.ShapeDtypeStruct(shape, F32) for shape in totals]
+        + [
             jax.ShapeDtypeStruct((rows, model), BF16),
             jax.ShapeDtypeStruct((rows, heads * width), BF16),
             jax.ShapeDtypeStruct((rows, heads * width), BF16),
-            jax.ShapeDtypeStruct((8, width), F32),
             jax.ShapeDtypeStruct((heads, blocks, width, width), F32),
-            jax.ShapeDtypeStruct((heads, width, width), F32),
-            jax.ShapeDtypeStruct((EDGE, model), F32),
         ],
+        input_output_aliases=aliases,
         compiler_params=params(),
         cost_estimate=LIGHT,
         name="gate_back",
-    )(place, *pieces, weight, mixed, outgate, gain, query, prefix)
+    )(*operands)
 
 
 def place_kernel(parts, place_ref, *refs):
@@ -588,6 +596,7 @@
 
 
 def first_kernel(
+    raw_ref,
     input_ref,
     gain_ref,
     mix_ref,
@@ -597,33 +606,67 @@
     mixing_ref,
     rates_out_ref,
     outgate_out_ref,
+    edge_ref,
 ):
-    values = input_ref[...].astype(F32)
-    scale = lax.rsqrt(jnp.mean(values * values, -1, keepdims=True) + EPSILON)
-    normed = (values * scale * gain_ref[...]).astype(BF16)
+    gain = gain_ref[...].astype(F32)
+
+    def norm(values):
+        scale = lax.rsqrt(jnp.mean(values * values, -1, keepdims=True) + EPSILON)
+        return (values * scale * gain).astype(BF16)
+
+    normed = norm(input_ref[...].astype(F32))
     normed_ref[...] = normed
     mixing_ref[...] = dot1(normed, mix_ref[...], NN)
-    rates_out_ref[...] = dot1(normed, rates_ref[...], NN)
+    rates_out_ref[...] = jnp.zeros_like(rates_out_ref)
+    rates_out_ref[:, : rates_ref.shape[0]] = dot1(normed, rates_ref[...], NT)
     outgate_out_ref[...] = dot1(normed, outgate_ref[...], NN)
 
-
-def first_projections(block_input, gain, w_mix, w_rates, w_outgate):
+    @pl.when(pl.program_id(0) == 0)
+    def _():
+        edge_ref[...] = dot1(norm(raw_ref[...]), mix_ref[...], NN)
+
+
+def first_projections(raw, block_input, gain, w_mix, w_rates, w_outgate):
     rows, model = block_input.shape
     steps = 4
     tile = rows // steps
     flat = lambda size: pl.BlockSpec((tile, size), lambda g: (g, 0))
     weights = (w_mix, w_rates, w_outgate)
+    sizes = (w_mix.shape[1], LANES, w_outgate.shape[1])
     return pl.pallas_call(
         first_kernel,
         grid=(steps,),
-        in_specs=[flat(model), whole((1, model))] + [whole(weight.shape) for weight in weights],
-        out_specs=[flat(model)] + [flat(weight.shape[1]) for weight in weights],
+        in_specs=[whole(raw.shape), flat(model), whole((1, model))]
+        + [whole(weight.shape) for weight in weights],
+        out_specs=[flat(model)] + [flat(size) for size in sizes] + [whole((EDGE, sizes[0]))],
         out_shape=[jax.ShapeDtypeStruct((rows, model), BF16)]
-        + [jax.ShapeDtypeStruct((rows, weight.shape[1]), F32) for weight in weights],
+        + [jax.ShapeDtypeStruct((rows, size), F32) for size in sizes]
+        + [jax.ShapeDtypeStruct((EDGE, sizes[0]), F32)],
         compiler_params=params(),
         cost_estimate=LIGHT,
         name="first_projections",
-    )(block_input, gain, *weights)
+    )(raw, block_input, gain, *weights)
+
+
+def grad_activ_kernel(grad_ref, weight_ref, out_ref):
+    out_ref[...] = dot1(grad_ref[...], weight_ref[...], NT)
+
+
+def grad_activ_of(grad, w_down):
+    rows, model = grad.shape
+    hidden = w_down.shape[0]
+    steps = 4
+    tile = rows // steps
+    return pl.pallas_call(
+        grad_activ_kernel,
+        grid=(steps,),
+        in_specs=[pl.BlockSpec((tile, model), lambda g: (g, 0)), whole(w_down.shape)],
+        out_specs=pl.BlockSpec((tile, hidden), lambda g: (g, 0)),
+        out_shape=jax.ShapeDtypeStruct((rows, hidden), F32),
+        compiler_params=params(),
+        cost_estimate=LIGHT,
+        name="grad_activ",
+    )(grad, w_down)
 
 
 def dense_kernel(parts, *refs):
@@ -634,7 +677,7 @@
         gain_ref,
         ffn_ref,
         down_ref,
-        grad_ref,
+        grad_activ_ref,
     ) = refs[1 + parts : 7 + parts]
     (
         middle_ref,
@@ -649,11 +692,11 @@
     middle = input_ref[...].astype(F32) + dot1(gated, weight_ref[...], NN)
     middle_ref[...] = middle
     scale = lax.rsqrt(jnp.mean(middle * middle, -1, keepdims=True) + EPSILON)
-    normed = (middle * scale * gain_ref[...]).astype(BF16)
+    normed = (middle * scale * gain_ref[...].astype(F32)).astype(BF16)
     normed_ref[...] = normed
     both = dot1(normed, ffn_ref[...], NN)
     gate, up = both[:, :hidden], both[:, hidden:]
-    grad_activ = dot1(grad_ref[...], down_ref[...], NT)
+    grad_activ = grad_activ_ref[...]
     sigma = jax.nn.sigmoid(gate)
     silu = gate * sigma
     activ = (silu * up).astype(BF16)
@@ -671,7 +714,7 @@
 CUTS = (384, 768)
 
 
-def dense_half(half, gated_near, weight, block_input, gain, ffn, w_down, grad, filled):
+def dense_half(half, gated_near, weight, block_input, gain, ffn, w_down, grad_activ, filled):
     parts = len(gated_near)
     rows, model = block_input.shape
     steps = DENSE_STEPS
@@ -690,14 +733,14 @@
         (model, BF16),
         (hidden + -hidden % LANES, BF16),
     ] + [(high - low, BF16) for low, high in zip((0,) + CUTS, CUTS + (2 * hidden,))]
-    operands = [half, *gated_near, weight, block_input, gain, ffn, w_down, grad]
+    operands = [half, *gated_near, weight, block_input, gain, ffn, w_down, grad_activ]
     in_specs = [flat(depth)] * parts + [
         fixed(parts * depth, model),
         flat(model),
         fixed(1, model),
         fixed(model, 2 * hidden),
         fixed(hidden, model),
-        flat(model),
+        flat(hidden),
     ]
     aliases = {}
     if filled is not None:
@@ -789,8 +832,8 @@
     q_ref,
     k_ref,
     rates_ref,
-    rate_row_ref,
-    bias_row_ref,
+    log_rate_ref,
+    rate_bias_ref,
     conv_ref,
     edge_ref,
     halo_ref,
@@ -828,7 +871,7 @@
     earlier = tok_col < tok_row
     sums = jnp.concatenate([later, earlier.astype(BF16)], 1)
     beta_all, decay_all, slope_all = rate_parts(
-        rates_ref[...], rate_row_ref[...], bias_row_ref[...]
+        rates_ref[...], lane_row(log_rate_ref, heads), lane_row(rate_bias_ref, heads)
     )
     chains = [(pos, head) for pos in reversed(range(rows // SPAN)) for head in range(heads)]
     leavings = []
@@ -860,8 +903,8 @@
         for pos, head in chains
     ]
     scores_low = [score_ref[head, pos].astype(BF16) for pos, head in chains]
-    states = [state_ref[head, pos] for pos, head in chains]
-    freshes = [fresh_ref[head, pos] for pos, head in chains]
+    states = [state_ref[head, pos].astype(BF16) for pos, head in chains]
+    freshes = [fresh_ref[head, pos].astype(BF16) for pos, head in chains]
     queries = [q_ref[head, pos] for pos, head in chains]
     keys = [k_ref[head, pos] for pos, head in chains]
     key_leavings = [
@@ -909,7 +952,7 @@
     for index, (pos, head) in enumerate(chains):
         read = scaled_states[index] * keys[index].astype(F32)
         arriving = grad_states[index] * queries[index] - read[:SPAN] - read[SPAN:]
-        written = key_leavings[index] * freshes[index].astype(F32)
+        written = key_leavings[index] * fresh_ref[head, pos]
         written = written[:SPAN] + written[SPAN:]
         all_ends.append(dot1(sums, jnp.concatenate([arriving, written], 0), NN))
     rates_of = [jnp.zeros((SPAN, width), F32) for _ in range(rows // SPAN)]
@@ -929,10 +972,10 @@
         ):
             at = (head * GROUPS + place_of) * width
             act_ref[here, at : at + width] = part
-        fresh = freshes[index].astype(F32)
+        fresh = fresh_ref[head, pos]
         step_part = (1.0 - betas[index]) * jnp.sum(solveds[index] * fresh, -1, keepdims=True)
         kept = parts_of[index][0][SPAN - 1 :] * jnp.sum(
-            leavings[index] * states[index].astype(F32), 0, keepdims=True
+            leavings[index] * state_ref[head, pos], 0, keepdims=True
         )
         grad_decay = jnp.sum(crossed[index], -1, keepdims=True) + jnp.sum(
             all_ends[index] + kept, -1, keepdims=True
@@ -973,13 +1016,14 @@
         before = jnp.concatenate([jnp.zeros((EDGE, width), F32), grad_conv[:EDGE]], 0)
         above = jnp.where(group == 0, edge_ref[:, cols], halo_ref[:, cols])
         mix_wide = jnp.concatenate([above, mix_ref[:, cols]], 0)
-        tap = taps_ref[CONV - 1 : CONV, cols]
+        taps = taps_ref[:, cols].astype(F32)
+        tap = taps[CONV - 1 : CONV]
         grad_mix = tap * grad_conv
         grad_before = jnp.zeros((EDGE, width), F32)
         sums_of = jnp.sum(grad_conv * mix_wide[EDGE:], 0, keepdims=True)
         grad_taps_ref[CONV - 1 : CONV, cols] += sums_of
         for shift in range(1, CONV):
-            tap = taps_ref[CONV - 1 - shift : CONV - shift, cols]
+            tap = taps[CONV - 1 - shift : CONV - shift]
             moved = pltpu.roll(wide, rows + EDGE - shift, 0)[:rows]
             grad_mix = grad_mix + tap * (moved * keep_fore[shift])
             moved = pltpu.roll(before, 2 * EDGE - shift, 0)[:EDGE]
@@ -997,7 +1041,7 @@
             last_ref[:, cols] = grad_mix[rows - 2 * EDGE :]
 
 
-def recurrence_back(offset, leaving, saved, rates, rate_row, bias_row, conv, edge, mixing, taps):
+def recurrence_back(offset, leaving, saved, rates, log_rate, rate_bias, conv, edge, mixing, taps):
     term, phi, state, fresh, grad, scores, x, n, cumul, q, k = saved
     rows, columns = mixing.shape
     heads, blocks = term.shape[:2]
@@ -1032,8 +1076,8 @@
             per_block(SPAN, width),
             per_block(virt, width),
             flat(LANES),
-            whole((1, LANES)),
-            whole((1, LANES)),
+            SCALARS,
+            SCALARS,
             flat(columns),
             whole((EDGE, columns)),
             pl.BlockSpec(
@@ -1069,7 +1113,7 @@
         name="recurrence_back",
     )(
         offset, leaving, term, phi, state, fresh, grad, scores, x, n, cumul, q, k,
-        rates, rate_row, bias_row, conv, edge, mixing, mixing, taps,
+        rates, log_rate, rate_bias, conv, edge, mixing, mixing, taps,
     )
 
 
@@ -1203,7 +1247,7 @@
     grad = kept_ref[...] + arrived_ref[...]
     scale = lax.rsqrt(jnp.mean(values * values, -1, keepdims=True) + EPSILON)
     normed = values * scale
-    through = grad * gain_ref[...]
+    through = grad * gain_ref[...].astype(F32)
     back = scale * (through - normed * jnp.mean(through * normed, -1, keepdims=True))
     out_ref[pl.ds(pl.multiple_of(step * tile, tile), tile)] = back + residual_ref[...].astype(F32)
     sums = jnp.sum((grad * normed).reshape(-1, EDGE, grad.shape[1]), 0)
@@ -1280,12 +1324,15 @@
     )(place, kept, arrived, middle, grad_gain)
 
 
-def pack_kernel(heads, first_ref, second_ref, gain_ref, *refs):
-    decay_refs, taps_refs, out_ref = refs[:heads], refs[heads : 2 * heads], refs[-1]
+def pack_kernel(parts, heads, *refs):
+    pieces, (second_ref, gain_ref) = refs[:parts], refs[parts : parts + 2]
+    decay_refs, taps_refs = refs[parts + 2 : parts + 2 + heads], refs[parts + 2 + heads : -1]
+    out_ref = refs[-1]
     place = 0
-    for ref in (first_ref, second_ref):
-        for start in range(0, ref.shape[1], LANES):
-            out_ref[place : place + 1] = jnp.sum(ref[:, start : start + LANES], 0, keepdims=True)
+    for rows in (sum(ref[...] for ref in pieces), second_ref[...]):
+        total = jnp.sum(rows, 0, keepdims=True)
+        for start in range(0, total.shape[1], LANES):
+            out_ref[place : place + 1] = total[:, start : start + LANES]
             place += 1
     for ref in taps_refs:
         for start in range(0, ref.shape[1], LANES):
@@ -1295,16 +1342,23 @@
     out_ref[place + EDGE : place + 2 * EDGE] = sum(ref[...] for ref in decay_refs)
 
 
-def pack_small(first, second, gain, decays, taps):
+def pack_small(pieces, second, gain, decays, taps):
+    model = second.shape[1]
     columns = sum(part.shape[1] for part in taps)
-    rows = 2 * (first.shape[1] // LANES) + EDGE * (columns // LANES) + 2 * EDGE
+    rows = 2 * (model // LANES) + EDGE * (columns // LANES) + 2 * EDGE
+    below = pieces[0].shape[0] // EDGE - 1
+    others = (second, gain, *decays, *taps)
     return pl.pallas_call(
-        partial(pack_kernel, len(taps)),
+        partial(pack_kernel, len(pieces), len(decays)),
+        grid=(1,),
+        in_specs=[pl.BlockSpec((EDGE, model), lambda g: (below, 0))] * len(pieces)
+        + [whole(part.shape) for part in others],
+        out_specs=whole((rows, LANES)),
         out_shape=jax.ShapeDtypeStruct((rows, LANES), F32),
         compiler_params=params(),
         cost_estimate=LIGHT,
         name="pack_small",
-    )(first, second, gain, *decays, *taps)
+    )(*pieces, *others)
 
 
 def unpack_kernel(
@@ -1534,12 +1588,7 @@
     quarter = rows // parts
     head_index = lax.axis_index("head")
     seq, seq_index = lax.axis_size("seq"), lax.axis_index("seq")
-    gain1, gain2 = first_gain.astype(F32), second_gain.astype(F32)
-    head_gain_row = head_gain.astype(F32)[None]
-    taps = conv_taps.astype(F32)
-    rate_row, bias_row = lanes_of(log_rate), lanes_of(rate_bias)
     rate_lanes = w_rates.shape[1]
-    w_rates_wide = jnp.pad(w_rates, ((0, 0), (0, LANES - rate_lanes)))
     ffn_flat = w_ffn.reshape(model, -1)
 
     head_bits = bits_of("head")
@@ -1559,26 +1608,33 @@
     head_order, seq_bits = head_bits, bits_of("seq")
 
     raw_edge = shifted(block_input[rows - EDGE :].astype(F32), "seq", 1)
-    normed1_low, mixing, rates, outgate = first_projections(
-        block_input, gain1[None], w_mix, w_rates_wide, w_outgate
-    )
-    w_out_near = gather_near(w_out.astype(F32), "head")
-    edge, conv, q, k, x, system, cumul, u, w, scores, query_map, prefix, phi, total = local_maps(
-        seq_starts, raw_edge, gain1[None], w_mix, mixing, taps, rates, rate_row, bias_row
+    w_out_start = GatherNear(w_out.astype(F32), "head")
+    normed1_low, mixing, rates, outgate, edge = first_projections(
+        raw_edge, block_input, first_gain[None], w_mix, w_rates.T, w_outgate
+    )
+    w_out_near = w_out_start.finish()
+    conv, q, k, x, system, cumul, u, w, scores, query_map, prefix, phi, total = local_maps(
+        seq_starts, log_rate, rate_bias, edge, mixing, conv_taps, rates
     )
     width = LANES
     incoming = carried_in(total, None, "seq", False)
+    head_gain_row = after(head_gain, total)[None]
     state, fresh, mixed, gated = outputs_of(
         seq_starts, incoming, (prefix, u, w, scores, q, cumul), outgate, head_gain_row, F32
     )
+    gain2_row = after(second_gain, gated)[None]
+    w_rates_wide = jnp.pad(after(w_rates, gated), ((0, 0), (0, LANES - rate_lanes)))
     gated_start = GatherNear(gated, "head")
     w_out_low, ffn_flat = low_weight([after(piece, gated) for piece in w_out_near], ffn_flat)
     maps = maps_between(after(total, gated), "seq") or ()
-    ffn_flat, w_out_low, *maps = join(ffn_flat, w_out_low, *maps)
+    grad_activ = grad_activ_of(after(grad_output, w_out_low), w_down)
+    ffn_flat, w_out_low, gain2_row, w_rates_wide, grad_activ, *maps = join(
+        ffn_flat, w_out_low, gain2_row, w_rates_wide, grad_activ, *maps
+    )
     gated_near = gated_start.finish(ffn_flat, w_out_low)
 
     dense = lambda half, filled: dense_half(
-        half, gated_near, w_out_low, block_input, gain2[None], ffn_flat, w_down, grad_output, filled
+        half, gated_near, w_out_low, block_input, gain2_row, ffn_flat, w_down, grad_activ, filled
     )
     *filled, back_sent, fore_sent = dense(sent_half, None)
     split = lambda half: half.reshape(parts // 2, quarter, model)
@@ -1598,6 +1654,11 @@
             return WholeSum(pairs)
         sent, kept = weight_grad(seq_mine, order[0], seq, pairs)
         return Scatter(seq_mine, "seq", order, kept, sent)
+
+    def total_of(one):
+        while one.order:
+            one.step()
+        return one.add().total
 
     ffn_sums, tie = [], back.kept
     for order, right in zip((near_first, far_first, near_first), grads_both):
@@ -1616,7 +1677,7 @@
         back, fore, ffn_one, ffn_two, also=(ffn_three.sent, down_sum.sent)
     )
     grad_middle_own = norm_back(
-        places[:1], back.kept[0], back.arrived[0], middle, gain2[None], grad_output
+        places[:1], back.kept[0], back.arrived[0], middle, gain2_row, grad_output
     )
 
     middle_start = GatherNear(grad_middle_own, "head")
@@ -1629,13 +1690,19 @@
         tie = one.kept
     fore.arrived = after(fore.arrived, tie)
     fore.add()
-    middle_start.found[2], fore.sent = arrive(
-        *ffn_sums, also=(middle_start.found[2], fore.sent)
+    backed = partial(
+        gate_back, weight=w_out, mixed=mixed, outgate=outgate, gain=head_gain_row, query=query_map, prefix=prefix
+    )
+    near_half = parts // 2
+    near_pieces = [grad_middle_own, after(middle_start.found[1], fore.kept)]
+    first_backed = backed(places[:near_half], near_pieces, before=None)
+    middle_start.found[1], middle_start.found[2], fore.sent, *first_backed = arrive(
+        *ffn_sums, also=(near_pieces[1], middle_start.found[2], fore.sent, *first_backed)
     )
 
     fore.send()
-    grad_branch, grad_mixed, outgate_low, grad_gain, term, grad_total, grad_second_gain = gate_back(
-        places, middle_start.finish(), w_out, mixed, outgate, head_gain_row, query_map, prefix
+    grad_gain, grad_total, grad_second_gain, grad_branch, grad_mixed, outgate_low, term = backed(
+        places[near_half:], middle_start.finish()[near_half:], before=first_backed
     )
     leaving = carried_in(total, grad_total, "seq", True, maps)
     out_width, outgate_width = gated.shape[1], outgate_low.shape[1]
@@ -1665,12 +1732,12 @@
         leaving,
         (term, phi, state, fresh, grad_mixed, scores, x, system, cumul, q, k),
         rates,
-        rate_row,
-        bias_row,
+        log_rate,
+        rate_bias,
         conv,
         edge,
         mixing,
-        taps,
+        conv_taps,
     )
     before_rows, output_start.found[2] = arrive(
         ffn_one, ffn_three, down_sum, also=(before_rows, output_start.found[2])
@@ -1731,45 +1798,48 @@
         part, side_sum, down_sum, also=(mix_three.sent, mix_one.kept)
     )
     grad_input_own = norm_back(
-        places[:1], part.kept[0], part.arrived[0], block_input, gain1[None], grad_middle_own
+        places[:1], part.kept[0], part.arrived[0], block_input, first_gain[None], grad_middle_own
     )
 
     input_start = GatherNear(grad_input_own, "head")
-    mix_three.sent, side_sum.arrived, _ = join(mix_three.sent, side_sum.arrived, grad_input_own)
+    mix_three.sent, side_sum.sent, _ = join(mix_three.sent, side_sum.sent, grad_input_own)
     mix_three.send()
     tie = grad_input_own
     for one in (side_sum, mix_two):
         one.arrived = after(one.arrived, tie)
         one.step()
         tie = one.kept
-    mix_one.arrived, side_sum.arrived, _ = join(mix_one.arrived, side_sum.arrived, tie)
+    ffn_two.arrived = after(ffn_two.arrived, tie)
+    ffn_two.step()
+    down_sum.arrived = after(down_sum.arrived, ffn_two.kept)
+    grad_down = total_of(down_sum)[:, : w_down.shape[0]].T
+    mix_one.arrived, side_sum.arrived, _ = join(mix_one.arrived, side_sum.arrived, grad_down)
     mix_one.step()
-    input_start.found[2], tie = arrive(
-        mix_two, mix_three, also=(input_start.found[2], mix_one.kept)
-    )
-    for one in (mix_three, mix_two):
-        one.step()
-    grad_input, grad_first_gain = place_rows(places, input_start.finish(), F32)
-    ffn_two.arrived, mix_three.arrived, _ = join(ffn_two.arrived, mix_three.arrived, grad_input)
-    ffn_two.step()
+    input_start.found[2], grad_down, _ = arrive(
+        mix_two, mix_three, ffn_two, also=(input_start.found[2], grad_down, mix_one.kept)
+    )
+    input_near = input_start.finish()
+    mix_three.step()
+    mix_two.arrived = after(mix_two.arrived, mix_three.kept)
+    mix_two.step()
+    input_near[0] = after(input_near[0], mix_two.kept)
     small = pack_small(
-        grad_first_gain,
-        grad_second_gain,
-        grad_head_gain,
-        [decay_sums],
-        [grad_taps],
-    )
-    for bit in seq_bits:
+        input_near, grad_second_gain, grad_head_gain, [decay_sums], [grad_taps]
+    )
+    arrived = exchange(small, "seq", seq_bits[0])
+    input_near[0] = after(input_near[0], small)
+    grad_input, _ = place_rows(places, input_near, F32)
+    mix_three.arrived = after(mix_three.arrived, grad_input)
+    mix_three.step()
+    small = small + after(arrived, mix_three.kept)
+    for bit in seq_bits[1:]:
         small = small + exchange(small, "seq", bit)
+        for one in (mix_one, mix_two, side_sum, *ffn_sums):
+            one.arrived = after(one.arrived, small)
     gain1_own, gain2_own, gain_sum, decay_sum, taps_sum = unpack_small(
         seq_mine, small, seq, model, mixing.shape[1]
     )
     decay_lanes = decay_sum[:, STEPS : heads * (STEPS + 1) : STEPS + 1]
-
-    def total_of(one):
-        while one.order:
-            one.step()
-        return one.add().total
 
     side_total = total_of(side_sum)
     ffn_total = jnp.concatenate([total_of(one) for one in ffn_sums], 1)
@@ -1788,7 +1858,7 @@
         side_total[:, :out_width].T,
         gain2_own[0],
         ffn_total.reshape((-1,) + w_ffn.shape[1:]),
-        total_of(down_sum)[:, : w_down.shape[0]].T,
+        grad_down,
     )
 
 

time: 449 us -> 431 us (0.960)
  waiting for transfers between devices: 79.8 us -> 66 us
  starting transfers between devices: 89.9 us -> 82.6 us
  Pallas kernels: 230 us -> 236 us
  other arithmetic: 12.7 us -> 7.84 us
    ppermute x48, waiting for transfers between devices: 75.2 us -> 62.7 us  [exchange(): lax.ppermute(value, axis, [(place, place ^ bit) for place in range(count)])]
    ppermute x48, starting transfers between devices: 67.3 us -> 58.6 us  [exchange(): lax.ppermute(value, axis, [(place, place ^ bit) for place in range(count)])]
    pallas_call x2 -> x3, Pallas kernels: 9.97 us -> 16.3 us  [the longest x1 9.16 us: first_projections(): pl.pallas_call(first_kernel, grid=(steps,), in_specs=[whole(raw.shape), f...]
    pallas_call x1 -> x2, Pallas kernels: 10.7 us -> 13.4 us  [gate_back(): pl.pallas_call(partial(gate_back_kernel, heads, parts), grid_spec=pltpu.P...]
    unnamed x108 -> x105, local copies, waits for them, and re-layouts: 12.4 us -> 12.6 us
  transfers between devices with their start and end apart: 58 -> 58, of which waited for: 16 -> 18; matrix products, arithmetic and copies ran while one was open for 6% -> 5% of each run, Pallas kernels for 48% -> 51%
where the time goes in v3:
time: 431 us; the launch traced here: 423 us
  Pallas kernels  236 us (55%)
  starting transfers between devices  82.6 us (19%)
  waiting for transfers between devices  66 us (15%)
  local copies, waits for them, and re-layouts  24.1 us (6%)
  other arithmetic  7.84 us (2%)
  matrix products  4.44 us (1%)
    ppermute x48, waiting for transfers between devices, exchange(): lax.ppermute(value, axis, [(place, place ^ bit) for place in range(count)])  62.7 us
    ppermute x48, starting transfers between devices, exchange(): lax.ppermute(value, axis, [(place, place ^ bit) for place in range(count)])  58.6 us
    pallas_call x19, Pallas kernels, combine(): pl.pallas_call(partial(combine_kernel, bit), in_specs=[SCALARS, IN_VMEM,...  49 us
    pallas_call x8, Pallas kernels, weight_grad(): pl.pallas_call(partial(grad_kernel, half, len(pairs)), grid_spec=pltpu.Pr...  43.7 us
    pallas_call x1, Pallas kernels, recurrence_back(): pl.pallas_call(partial(back_kernel, heads), grid=(steps,), in_specs=[SCAL...  25.9 us
    pallas_call x1, Pallas kernels, local_maps(): pl.pallas_call(partial(local_kernel, heads), grid=(blocks // PACK,), in_s...  24.4 us
    ppermute x10, starting transfers between devices, shifted(): lax.ppermute(value, axis, [(source, source + steps) for source in range(f...  24 us
    pallas_call x2, Pallas kernels, dense_half(): pl.pallas_call(partial(dense_kernel, parts), grid_spec=pltpu.PrefetchScal...  22.9 us
  transfers between devices with their start and end apart: 58, of which 18 were waited for; matrix products, arithmetic and copies ran while one was open for 5% of the time, Pallas kernels for 51%

profile of v3, /device:TPU:0, one launch (start us, length us, event | category | flops | bytes accessed | tf_op | source)
XLA Modules:
  0.0 423.4 jit_solution(3414095253664740978)
XLA Ops:
  11.5 9.2 %first_projections.1 = (bf16[1024,1024]{1,0:T(8,128)(2,1)}, f32[1024,1280]{1,0:T(8,128)}, f32[1024,128]{1,0:T(8,128)}, f32[1024,256]{1,0:T(8,128)}, f32[8,1280]{1,0:T(8,128)}) custom-call(f32[8,1024]{1,0:T(8,128)} %copy-done.44, bf16[1024,1024]{1,0:T(8,128)(2,1)} %value_ref.1, bf16[1,1024]{1,0:T(2,128)(2,1)} %broadcast_in_dim.24.gain_ref, ...), custom_call_target="tpu_custom_call" | custom-call | flops 1 | bytes 1 | tf_op jit(solution)/shard_map/first_projections/pallas_call | solution.py:636
  20.7 24.4 %local_maps.1 = (f32[1024,1280]{1,0:T(8,128)}, f32[2,16,64,128]{3,2,1,0:T(8,128)}, bf16[2,16,128,128]{3,2,1,0:T(8,128)(2,1)}, bf16[2,16,128,128]{3,2,1,0:T(8,128...) custom-call(s32[1]{0:T(128)S(6)} %copy.67.offset_ref, ...), custom_call_target="tpu_custom_call" | custom-call | flops 1 | bytes 1 | tf_op jit(solution)/shard_map/local_maps/pallas_call | solution.py:289
  45.0 4.9 %collective-permute-start.2 = (f32[2,128,256]{2,1,0:T(8,128)}, f32[2,128,256]{2,1,0:T(8,128)S(1)}, u32[]{:S(2)}, u32[]{:S(2)}) collective-permute-start(f32[2,128,256]{2,1,0:T(8,128)} %get-tuple-element.280), channel_id=1, source_target_pairs={{0,8},{4,12},{8,16},{12,20},{16,24},{20,28},{1,9},{5,13},{9,17},{1... | collective-permute-start | bytes 786440 | tf_op jit(solution)/shard_map/ppermute | solution.py:1404
  63.8 8.8 %mixer_outputs.1 = (f32[2,16,128,128]{3,2,1,0:T(8,128)}, f32[2,16,128,128]{3,2,1,0:T(8,128)}, f32[1024,256]{1,0:T(8,128)}, f32[1024,256]{1,0:T(8,128)}) custom-call(s32[1]{0:T(128)S(6)} %copy.67.offset_ref, f32[2,128,128]{2,1,0:T(8,128)} %convolution_add_fusion.2.incoming_ref, f32[2,16,128,256]{3,2,1,0:T(8,128)} %get-tuple-element.262.prefix_ref.refs_7_, ...), custom_call_target="tpu_custom_call" | custom-call | flops 1 | bytes 1 | tf_op jit(solution)/shard_map/mixer_outputs/pallas_call | solution.py:377
  86.2 5.6 %grad_activ.1.refs_10_ = f32[1024,704]{1,0:T(8,128)} custom-call(bf16[1024,1024]{1,0:T(8,128)(2,1)} %residual_ref.1, bf16[704,1024]{1,0:T(8,128)(2,1)} %refs_9_.3), custom_call_target="tpu_custom_call" | custom-call | flops 1 | bytes 1 | tf_op jit(solution)/shard_map/grad_activ/pallas_call | solution.py:660
  97.8 11.4 %dense_half.2 = (f32[1024,1024]{1,0:T(8,128)}, bf16[1024,1024]{1,0:T(8,128)(2,1)}, bf16[1024,768]{1,0:T(8,128)(2,1)}, bf16[1024,384]{1,0:T(8,128)(2,1)}, bf16[10...) custom-call(s32[1]{0:T(128)} %bitcast.9.refs_0_, ...), custom_call_target="tpu_custom_call" | custom-call | flops 1 | bytes 1 | tf_op jit(solution)/shard_map/dense_half/pallas_call | solution.py:750
  109.4 11.5 %dense_half.3 = (f32[1024,1024]{1,0:T(8,128)}, bf16[1024,1024]{1,0:T(8,128)(2,1)}, bf16[1024,768]{1,0:T(8,128)(2,1)}, bf16[1024,384]{1,0:T(8,128)(2,1)}, bf16[10...) custom-call(s32[1]{0:T(128)} %bitcast.5.refs_0_.place_ref, ...), custom_call_target="tpu_custom_call", output_to_operand_aliasing={{0}: (11, {}), {1}: (12, {}), {2}: (13, {}), {3}: (14, {}),... | custom-call | flops 1 | bytes 1 | tf_op jit(solution)/shard_map/dense_half/pallas_call | solution.py:750
  135.5 5.6 %collective-permute-start.16 = (f32[4,128,384]{2,1,0:T(8,128)}, f32[4,128,384]{2,1,0:T(8,128)}, u32[]{:S(2)}, u32[]{:S(2)}) collective-permute-start(f32[4,128,384]{2,1,0:T(8,128)} %get-tuple-element.305), channel_id=1, source_target_pairs={{0,8},{4,12},{8,0},{12,4},{16,24},{20,28},{24,16},{28,20},{1,9},{5... | collective-permute-start | bytes 2359304 | tf_op jit(solution)/shard_map/ppermute | solution.py:1398
  141.9 5.4 %weight_grad.10 = (f32[4,128,640]{2,1,0:T(8,128)}, f32[4,128,640]{2,1,0:T(8,128)}) custom-call(s32[1]{0:T(128)} %bitcast.4.refs_0_.mine_ref, bf16[1024,1024]{1,0:T(8,128)(2,1)} %get-tuple-element.307.refs_1_.refs_2_.refs_3_.refs_4_, bf16[1024,1024]{1,0:T(8,128)(2,1)} %get-tuple-element.307.refs_1_.refs_2_.refs_3_.refs_4_, ...), custom_call_target="tpu_custom_call" | custom-call | flops 1 | bytes 1 | tf_op jit(solution)/shard_map/weight_grad/pallas_call | solution.py:1181
  147.2 6.0 %weight_grad.11 = (f32[4,128,768]{2,1,0:T(8,128)}, f32[4,128,768]{2,1,0:T(8,128)}) custom-call(s32[1]{0:T(128)} %bitcast.4.refs_0_.mine_ref, bf16[1024,1024]{1,0:T(8,128)(2,1)} %residual_ref.1, bf16[1024,1024]{1,0:T(8,128)(2,1)} %residual_ref.1, bf16[1024,1024]{1,0:T(8,128)(2,1)} %residual_ref.1, bf16[1024,1024]{1,0:T(8,128)(2,1)} %residual_ref.1, ...), custom_call_target="tpu_custom_call" | custom-call | flops 1 | bytes 1 | tf_op jit(solution)/shard_map/weight_grad/pallas_call | solution.py:1181
  153.2 5.9 %collective-permute-done.16 = f32[4,128,384]{2,1,0:T(8,128)} collective-permute-done((f32[4,128,384]{2,1,0:T(8,128)}, f32[4,128,384]{2,1,0:T(8,128)}, u32[]{:S(2)}, u32[]{:S(2)}) %collective-permute-start.16) | collective-permute-done | bytes 786464 | tf_op jit(solution)/shard_map/ppermute | solution.py:1398
  180.6 6.6 %gate_back.2 = (f32[8,128]{1,0:T(8,128)}, f32[2,128,128]{2,1,0:T(8,128)}, f32[8,1024]{1,0:T(8,128)}, bf16[1024,1024]{1,0:T(8,128)(2,1)}, bf16[1024,256]{1,0:T(8,...) custom-call(s32[2]{0:T(128)} %pad_add_fusion.1.place_ref, f32[264,1024]{1,0:T(8,128)} %norm_back.2.refs_0_.residual_ref, ...), custom_call_target="tpu_custom_call" | custom-call | flops 1 | bytes 1 | tf_op jit(solution)/shard_map/gate_back/pallas_call | solution.py:522
  187.2 6.6 %collective-permute-done.18 = f32[2,128,384]{2,1,0:T(8,128)S(1)} collective-permute-done((f32[2,128,384]{2,1,0:T(8,128)}, f32[2,128,384]{2,1,0:T(8,128)S(1)}, u32[]{:S(2)}, u32[]{:S(2)}) %collective-permute-start.18) | collective-permute-done | bytes 393248 | tf_op jit(solution)/shard_map/ppermute | solution.py:1398
  198.3 6.7 %gate_back.3 = (f32[8,128]{1,0:T(8,128)}, f32[2,128,128]{2,1,0:T(8,128)}, f32[8,1024]{1,0:T(8,128)}, bf16[1024,1024]{1,0:T(8,128)(2,1)}, bf16[1024,256]{1,0:T(8,...) custom-call(s32[2]{0:T(128)} %pad_add_fusion.2.place_ref, ...), custom_call_target="tpu_custom_call", output_to_operand_aliasing={{3}: (12, {}), {4}: (13, {}), {5}: (14, {}), {6}: (15, {})} | custom-call | flops 1 | bytes 1 | tf_op jit(solution)/shard_map/gate_back/pallas_call | solution.py:522
  209.8 5.5 %weight_grad.12 = (f32[4,128,512]{2,1,0:T(8,128)}, f32[4,128,512]{2,1,0:T(8,128)}) custom-call(s32[1]{0:T(128)} %bitcast.4.refs_0_.mine_ref, bf16[1024,1024]{1,0:T(8,128)(2,1)} %get-tuple-element.354.refs_1_.refs_2_.refs_3_.refs_4_, bf16[1024,1024]{1,0:T(8,128)(2,1)} %get-tuple-element.354.refs_1_.refs_2_.refs_3_.refs_4_, ...), custom_call_target="tpu_custom_call" | custom-call | flops 1 | bytes 1 | tf_op jit(solution)/shard_map/weight_grad/pallas_call | solution.py:1181
  236.6 25.9 %recurrence_back.1 = (bf16[1024,1280]{1,0:T(8,128)(2,1)}, f32[16,1280]{1,0:T(8,128)}, f32[8,1280]{1,0:T(8,128)}, bf16[1024,128]{1,0:T(8,128)(2,1)}, f32[8,128]{1,0:T(8,128)}, /*index=5*/f32[8,1280]{1,0:T(8,128)}) custom-call(s32[1]{0:T(128)S(6)} %copy.67.offset_ref, f32[2,128,128]{2,1,0:T(8,128)} %convolution_add_fusion.leaving_ref, ...), custom_call_target="tpu_custom_call" | custom-call | flops 1 | bytes 1 | tf_op jit(solution)/shard_map/recurrence_back/pallas_call | solution.py:1061
  277.6 5.6 %weight_grad.13 = (f32[4,128,640]{2,1,0:T(8,128)}, f32[4,128,640]{2,1,0:T(8,128)}) custom-call(s32[1]{0:T(128)} %bitcast.4.refs_0_.mine_ref, bf16[1024,1024]{1,0:T(8,128)(2,1)} %get-tuple-element.432.refs_6_.refs_7_.refs_8_.refs_9_.refs_1_.refs_2_.refs_3_.refs_4_.refs_11_.refs_12_.refs_13_.refs_14_, ...), custom_call_target="tpu_custom_call" | custom-call | flops 1 | bytes 1 | tf_op jit(solution)/shard_map/weight_grad/pallas_call | solution.py:1181
  283.2 8.8 %first_back.1 = (f32[512,1024]{1,0:T(8,128)}, f32[512,1024]{1,0:T(8,128)}) custom-call(s32[1]{0:T(128)} %bitcast.5.refs_0_.place_ref, bf16[1024,1280]{1,0:T(8,128)(2,1)} %fusion.2.refs_5_.refs_0_.refs_10_.refs_15_, bf16[1024,256]{1,0:T(8,128)(2,1)} %get-tuple-element.356.refs_10_.refs_1_, bf16[1024,128]{1,0:T(8,128)(2,1)} %get-tuple-element.402.refs_2_.refs_15_, ...), custom_call_target="tpu_custom_call" | custom-call | flops 1 | bytes 1 | tf_op jit(solution)/shard_map/first_back/pallas_call | solution.py:800
  292.0 6.2 %collective-permute-done.35 = f32[1,128,640]{2,1,0:T(8,128)S(1)} collective-permute-done((f32[1,128,640]{2,1,0:T(8,128)}, f32[1,128,640]{2,1,0:T(8,128)S(1)}, u32[]{:S(2)}, u32[]{:S(2)}) %collective-permute-start.35) | collective-permute-done | bytes 327712 | tf_op jit(solution)/shard_map/ppermute | solution.py:1398
  319.8 6.2 %weight_grad.14 = (f32[4,128,384]{2,1,0:T(8,128)}, f32[4,128,384]{2,1,0:T(8,128)}) custom-call(s32[1]{0:T(128)} %bitcast.4.refs_0_.mine_ref, bf16[1024,1024]{1,0:T(8,128)(2,1)} %get-tuple-element.432.refs_6_.refs_7_.refs_8_.refs_9_.refs_1_.refs_2_.refs_3_.refs_4_.refs_11_.refs_12_.refs_13_.refs_14_, ...), custom_call_target="tpu_custom_call" | custom-call | flops 1 | bytes 1 | tf_op jit(solution)/shard_map/weight_grad/pallas_call | solution.py:1181
  330.5 6.4 %weight_grad.15 = (f32[4,128,384]{2,1,0:T(8,128)}, f32[4,128,384]{2,1,0:T(8,128)}) custom-call(s32[1]{0:T(128)} %bitcast.4.refs_0_.mine_ref, bf16[1024,1024]{1,0:T(8,128)(2,1)} %get-tuple-element.432.refs_6_.refs_7_.refs_8_.refs_9_.refs_1_.refs_2_.refs_3_.refs_4_.refs_11_.refs_12_.refs_13_.refs_14_, ...), custom_call_target="tpu_custom_call" | custom-call | flops 1 | bytes 1 | tf_op jit(solution)/shard_map/weight_grad/pallas_call | solution.py:1181
  358.0 12.2 %collective-permute-done.47 = f32[2,128,640]{2,1,0:T(8,128)S(1)} collective-permute-done((f32[2,128,640]{2,1,0:T(8,128)}, f32[2,128,640]{2,1,0:T(8,128)S(1)}, u32[]{:S(2)}, u32[]{:S(2)}) %collective-permute-start.47) | collective-permute-done | bytes 655392 | tf_op jit(solution)/shard_map/ppermute | solution.py:1398
  393.0 5.7 %collective-permute-done.52 = f32[2,128,384]{2,1,0:T(8,128)S(1)} collective-permute-done((f32[2,128,384]{2,1,0:T(8,128)}, f32[2,128,384]{2,1,0:T(8,128)S(1)}, u32[]{:S(2)}, u32[]{:S(2)}) %collective-permute-start.52) | collective-permute-done | bytes 393248 | tf_op jit(solution)/shard_map/ppermute | solution.py:1398
  401.5 5.3 %collective-permute-done.53 = f32[112,128]{1,0:T(8,128)S(1)} collective-permute-done((f32[112,128]{1,0:T(8,128)S(1)}, f32[112,128]{1,0:T(8,128)S(1)}, u32[]{:S(2)}, u32[]{:S(2)}) %collective-permute-start.53) | collective-permute-done | bytes 57376 | tf_op jit(solution)/shard_map/ppermute | solution.py:1398
  (278 shorter events, 214.5 us)
Async XLA Ops:
  1.8 57.3 %collective-permute-start.7 = (f32[256,1024]{1,0:T(8,128)S(1)}, f32[256,1024]{1,0:T(8,128)}, u32[]{:S(2)}, u32[]{:S(2)}) collective-permute-start(f32[256,1024]{1,0:T(8,128)S(1)} %convert_element_type.17.refs_0_), channel_id=1, source_target_pairs={{0,2},{1,3},{2,0},{3,1},{4,6},{5,7},{6,4},{7,5},{8,10},{9,11},{10,... | collective-permute-start | bytes 3145736 | tf_op jit(solution)/shard_map/ppermute | solution.py:1398
  58.7 24.2 %collective-permute-start.6 = (f32[256,1024]{1,0:T(8,128)S(1)}, f32[256,1024]{1,0:T(8,128)}, u32[]{:S(2)}, u32[]{:S(2)}) collective-permute-start(f32[256,1024]{1,0:T(8,128)S(1)} %convert_element_type.17.refs_0_), channel_id=1, source_target_pairs={{0,1},{1,0},{2,3},{3,2},{4,5},{5,4},{6,7},{7,6},{8,9},{9,8},{10,11... | collective-permute-start | bytes 3145736 | tf_op jit(solution)/shard_map/ppermute | solution.py:1398
  59.1 23.9 %collective-permute-start.8 = (f32[256,1024]{1,0:T(8,128)}, f32[256,1024]{1,0:T(8,128)}, u32[]{:S(2)}, u32[]{:S(2)}) collective-permute-start(f32[256,1024]{1,0:T(8,128)} %collective-permute-done.7.refs_2_), channel_id=1, source_target_pairs={{0,1},{1,0},{2,3},{3,2},{4,5},{5,4},{6,7},{7,6},{8,9},{9,8},{10,11... | collective-permute-start | bytes 3145736 | tf_op jit(solution)/shard_map/ppermute | solution.py:1398
  126.0 34.5 %collective-permute-start.14 = (f32[2,256,1024]{2,1,0:T(8,128)}, f32[2,256,1024]{2,1,0:T(8,128)S(1)}, u32[]{:S(2)}, u32[]{:S(2)}) collective-permute-start(f32[2,256,1024]{2,1,0:T(8,128)} %bitcast.15), channel_id=1, source_target_pairs={{0,1},{1,0},{2,3},{3,2},{4,5},{5,4},{6,7},{7,6},{8,9},{9,8},{10,11... | collective-permute-start | bytes 6291464 | tf_op jit(solution)/shard_map/ppermute | solution.py:1398
  126.4 34.1 %collective-permute-start.13 = (f32[1,256,1024]{2,1,0:T(8,128)}, f32[1,256,1024]{2,1,0:T(8,128)S(1)}, u32[]{:S(2)}, u32[]{:S(2)}) collective-permute-start(f32[1,256,1024]{2,1,0:T(8,128)} %get-tuple-element.299), channel_id=1, source_target_pairs={{0,2},{1,3},{2,0},{3,1},{4,6},{5,7},{6,4},{7,5},{8,10},{9,11},{10,... | collective-permute-start | bytes 3145736 | tf_op jit(solution)/shard_map/ppermute | solution.py:1398
  135.5 23.5 %collective-permute-start.16 = (f32[4,128,384]{2,1,0:T(8,128)}, f32[4,128,384]{2,1,0:T(8,128)}, u32[]{:S(2)}, u32[]{:S(2)}) collective-permute-start(f32[4,128,384]{2,1,0:T(8,128)} %get-tuple-element.305), channel_id=1, source_target_pairs={{0,8},{4,12},{8,0},{12,4},{16,24},{20,28},{24,16},{28,20},{1,9},{5... | collective-permute-start | bytes 2359304 | tf_op jit(solution)/shard_map/ppermute | solution.py:1398
  164.9 30.5 %collective-permute-start.19 = (f32[4,128,640]{2,1,0:T(8,128)}, f32[4,128,640]{2,1,0:T(8,128)S(1)}, u32[]{:S(2)}, u32[]{:S(2)}) collective-permute-start(f32[4,128,640]{2,1,0:T(8,128)} %get-tuple-element.324), channel_id=1, source_target_pairs={{0,4},{4,0},{8,12},{12,8},{16,20},{20,16},{24,28},{28,24},{1,5},{5... | collective-permute-start | bytes 3932168 | tf_op jit(solution)/shard_map/ppermute | solution.py:1398
  165.6 29.8 %collective-permute-start.21 = (f32[264,1024]{1,0:T(8,128)}, f32[264,1024]{1,0:T(8,128)S(1)}, u32[]{:S(2)}, u32[]{:S(2)}) collective-permute-start(f32[264,1024]{1,0:T(8,128)} %norm_back.2.refs_0_.residual_ref), channel_id=1, source_target_pairs={{0,2},{1,3},{2,0},{3,1},{4,6},{5,7},{6,4},{7,5},{8,10},{9,11},{10,... | collective-permute-start | bytes 3244040 | tf_op jit(solution)/shard_map/ppermute | solution.py:1398
  195.5 28.0 %collective-permute-start.22 = (f32[1,256,1024]{2,1,0:T(8,128)}, f32[1,256,1024]{2,1,0:T(8,128)}, u32[]{:S(2)}, u32[]{:S(2)}) collective-permute-start(f32[1,256,1024]{2,1,0:T(8,128)} %get-tuple-element.341), channel_id=1, source_target_pairs={{0,2},{1,3},{2,0},{3,1},{4,6},{5,7},{6,4},{7,5},{8,10},{9,11},{10,... | collective-permute-start | bytes 3145736 | tf_op jit(solution)/shard_map/ppermute | solution.py:1398
  223.5 39.1 %collective-permute-start.29 = (f32[4,128,768]{2,1,0:T(8,128)S(1)}, f32[4,128,768]{2,1,0:T(8,128)S(1)}, u32[]{:S(2)}, u32[]{:S(2)}) collective-permute-start(f32[4,128,768]{2,1,0:T(8,128)S(1)} %copy-done.46), channel_id=1, source_target_pairs={{0,4},{4,0},{8,12},{12,8},{16,20},{20,16},{24,28},{28,24},{1,5},{5... | collective-permute-start | bytes 4718600 | tf_op jit(solution)/shard_map/ppermute | solution.py:1398
  229.2 33.3 %collective-permute-start.31 = (f32[264,1024]{1,0:T(8,128)}, f32[264,1024]{1,0:T(8,128)S(1)}, u32[]{:S(2)}, u32[]{:S(2)}) collective-permute-start(f32[264,1024]{1,0:T(8,128)} %own_output.1.refs_0_), channel_id=1, source_target_pairs={{0,2},{1,3},{2,0},{3,1},{4,6},{5,7},{6,4},{7,5},{8,10},{9,11},{10,... | collective-permute-start | bytes 3244040 | tf_op jit(solution)/shard_map/ppermute | solution.py:1398
  230.7 31.8 %collective-permute-start.28 = (f32[2,128,640]{2,1,0:T(8,128)S(1)}, f32[2,128,640]{2,1,0:T(8,128)S(1)}, u32[]{:S(2)}, u32[]{:S(2)}) collective-permute-start(f32[2,128,640]{2,1,0:T(8,128)S(1)} %copy-done.48), channel_id=1, source_target_pairs={{0,8},{4,12},{8,0},{12,4},{16,24},{20,28},{24,16},{28,20},{1,9},{5... | collective-permute-start | bytes 1966088 | tf_op jit(solution)/shard_map/ppermute | solution.py:1398
  233.5 29.1 %collective-permute-start.27 = (f32[1,128,384]{2,1,0:T(8,128)S(1)}, f32[1,128,384]{2,1,0:T(8,128)S(1)}, u32[]{:S(2)}, u32[]{:S(2)}) collective-permute-start(f32[1,128,384]{2,1,0:T(8,128)S(1)} %copy-done.50), channel_id=1, source_target_pairs={{0,16},{4,20},{8,24},{12,28},{16,0},{20,4},{24,8},{28,12},{1,17},{... | collective-permute-start | bytes 589832 | tf_op jit(solution)/shard_map/ppermute | solution.py:1398
  263.9 35.2 %collective-permute-start.36 = (f32[264,1024]{1,0:T(8,128)S(1)}, f32[264,1024]{1,0:T(8,128)S(1)}, u32[]{:S(2)}, u32[]{:S(2)}) collective-permute-start(f32[264,1024]{1,0:T(8,128)S(1)} %collective-permute-done.31.refs_2_), channel_id=1, source_target_pairs={{0,1},{1,0},{2,3},{3,2},{4,5},{5,4},{6,7},{7,6},{8,9},{9,8},{10,11... | collective-permute-start | bytes 3244040 | tf_op jit(solution)/shard_map/ppermute | solution.py:1398
  269.6 29.6 %collective-permute-start.33 = (f32[4,128,512]{2,1,0:T(8,128)S(1)}, f32[4,128,512]{2,1,0:T(8,128)S(1)}, u32[]{:S(2)}, u32[]{:S(2)}) collective-permute-start(f32[4,128,512]{2,1,0:T(8,128)S(1)} %copy-done.47), channel_id=1, source_target_pairs={{0,4},{4,0},{8,12},{12,8},{16,20},{20,16},{24,28},{28,24},{1,5},{5... | collective-permute-start | bytes 3145736 | tf_op jit(solution)/shard_map/ppermute | solution.py:1398
  272.2 26.9 %collective-permute-start.34 = (f32[2,128,768]{2,1,0:T(8,128)}, f32[2,128,768]{2,1,0:T(8,128)S(1)}, u32[]{:S(2)}, u32[]{:S(2)}) collective-permute-start(f32[2,128,768]{2,1,0:T(8,128)} %get-tuple-element.395), channel_id=1, source_target_pairs={{0,8},{4,12},{8,0},{12,4},{16,24},{20,28},{24,16},{28,20},{1,9},{5... | collective-permute-start | bytes 2359304 | tf_op jit(solution)/shard_map/ppermute | solution.py:1398
  273.5 24.8 %collective-permute-start.35 = (f32[1,128,640]{2,1,0:T(8,128)}, f32[1,128,640]{2,1,0:T(8,128)S(1)}, u32[]{:S(2)}, u32[]{:S(2)}) collective-permute-start(f32[1,128,640]{2,1,0:T(8,128)} %get-tuple-element.396), channel_id=1, source_target_pairs={{0,16},{4,20},{8,24},{12,28},{16,0},{20,4},{24,8},{28,12},{1,17},{... | collective-permute-start | bytes 983048 | tf_op jit(solution)/shard_map/ppermute | solution.py:1398
  299.2 37.7 %collective-permute-start.41 = (f32[4,128,640]{2,1,0:T(8,128)}, f32[4,128,640]{2,1,0:T(8,128)S(1)}, u32[]{:S(2)}, u32[]{:S(2)}) collective-permute-start(f32[4,128,640]{2,1,0:T(8,128)} %get-tuple-element.434), channel_id=1, source_target_pairs={{0,4},{4,0},{8,12},{12,8},{16,20},{20,16},{24,28},{28,24},{1,5},{5... | collective-permute-start | bytes 3932168 | tf_op jit(solution)/shard_map/ppermute | solution.py:1398
  308.7 32.2 %collective-permute-start.38 = (f32[1,256,1024]{2,1,0:T(8,128)}, f32[1,256,1024]{2,1,0:T(8,128)S(1)}, u32[]{:S(2)}, u32[]{:S(2)}) collective-permute-start(f32[1,256,1024]{2,1,0:T(8,128)} %get-tuple-element.429), channel_id=1, source_target_pairs={{0,2},{1,3},{2,0},{3,1},{4,6},{5,7},{6,4},{7,5},{8,10},{9,11},{10,... | collective-permute-start | bytes 3145736 | tf_op jit(solution)/shard_map/ppermute | solution.py:1398
  312.8 28.1 %collective-permute-start.39 = (f32[2,128,512]{2,1,0:T(8,128)}, f32[2,128,512]{2,1,0:T(8,128)S(1)}, u32[]{:S(2)}, u32[]{:S(2)}) collective-permute-start(f32[2,128,512]{2,1,0:T(8,128)} %get-tuple-element.430), channel_id=1, source_target_pairs={{0,8},{4,12},{8,0},{12,4},{16,24},{20,28},{24,16},{28,20},{1,9},{5... | collective-permute-start | bytes 1572872 | tf_op jit(solution)/shard_map/ppermute | solution.py:1398
  345.4 31.0 %collective-permute-start.46 = (f32[264,1024]{1,0:T(8,128)}, f32[264,1024]{1,0:T(8,128)S(1)}, u32[]{:S(2)}, u32[]{:S(2)}) collective-permute-start(f32[264,1024]{1,0:T(8,128)} %norm_back.3.refs_0_), channel_id=1, source_target_pairs={{0,2},{1,3},{2,0},{3,1},{4,6},{5,7},{6,4},{7,5},{8,10},{9,11},{10,... | collective-permute-start | bytes 3244040 | tf_op jit(solution)/shard_map/ppermute | solution.py:1398
  346.9 29.5 %collective-permute-start.44 = (f32[4,128,384]{2,1,0:T(8,128)}, f32[4,128,384]{2,1,0:T(8,128)S(1)}, u32[]{:S(2)}, u32[]{:S(2)}) collective-permute-start(f32[4,128,384]{2,1,0:T(8,128)} %get-tuple-element.447), channel_id=1, source_target_pairs={{0,4},{4,0},{8,12},{12,8},{16,20},{20,16},{24,28},{28,24},{1,5},{5... | collective-permute-start | bytes 2359304 | tf_op jit(solution)/shard_map/ppermute | solution.py:1398
  380.0 30.7 %collective-permute-start.55 = (f32[1,128,640]{2,1,0:T(8,128)}, f32[1,128,640]{2,1,0:T(8,128)S(1)}, u32[]{:S(2)}, u32[]{:S(2)}) collective-permute-start(f32[1,128,640]{2,1,0:T(8,128)} %get-tuple-element.476), channel_id=1, source_target_pairs={{0,16},{4,20},{8,24},{12,28},{16,0},{20,4},{24,8},{28,12},{1,17},{... | collective-permute-start | bytes 983048 | tf_op jit(solution)/shard_map/ppermute | solution.py:1398
  383.0 27.7 %collective-permute-start.56 = (f32[1,128,384]{2,1,0:T(8,128)}, f32[1,128,384]{2,1,0:T(8,128)S(1)}, u32[]{:S(2)}, u32[]{:S(2)}) collective-permute-start(f32[1,128,384]{2,1,0:T(8,128)} %get-tuple-element.479), channel_id=1, source_target_pairs={{0,16},{4,20},{8,24},{12,28},{16,0},{20,4},{24,8},{28,12},{1,17},{... | collective-permute-start | bytes 589832 | tf_op jit(solution)/shard_map/ppermute | solution.py:1398
  (85 other events, 897.9 us)

commit v4 on v3

--- a/solution.py
+++ b/solution.py
@@ -1237,14 +1237,57 @@
     )(mine, view(kept), view(arrived))
 
 
+def carry_kernel(count, dims, *refs):
+    maps, terms, out_ref = refs[: count - 1], refs[count - 1 : -1], refs[-1]
+    for head in range(out_ref.shape[0]):
+        state = terms[-1][head]
+        for map_ref, term_ref in zip(reversed(maps), reversed(terms[:-1])):
+            state = dot3(map_ref[head], state, dims) + term_ref[head]
+        out_ref[head] = state
+
+
+def carry(maps, terms, dims):
+    return pl.pallas_call(
+        partial(carry_kernel, len(terms), dims),
+        out_shape=jax.ShapeDtypeStruct(terms[0].shape, F32),
+        compiler_params=params(),
+        cost_estimate=LIGHT,
+        name="carry",
+    )(*maps, *terms)
+
+
+def quarter_kernel(place_ref, kept_ref, near_ref, out_ref):
+    out_ref[...] = kept_ref[...] + near_ref[...]
+
+
+def quarter_sum(place, kept, near):
+    rows, model = kept.shape
+    steps = 2
+    tile = rows // (2 * steps)
+    other = pl.BlockSpec((tile, model), lambda g, at: ((1 - at[0] % 2) * steps + g, 0))
+    return pl.pallas_call(
+        quarter_kernel,
+        grid_spec=pltpu.PrefetchScalarGridSpec(
+            num_scalar_prefetch=1,
+            grid=(steps,),
+            in_specs=[other, other],
+            out_specs=pl.BlockSpec((tile, model), lambda g, at: (g, 0)),
+        ),
+        out_shape=jax.ShapeDtypeStruct((rows // 2, model), F32),
+        compiler_params=params(),
+        cost_estimate=LIGHT,
+        name="quarter_sum",
+    )(place, kept, near)
+
+
 def norm_back_kernel(
-    place_ref, kept_ref, arrived_ref, value_ref, gain_ref, residual_ref, out_ref
+    place_ref, kept_ref, near_ref, arrived_ref, value_ref, gain_ref, residual_ref, out_ref
 ):
     step = pl.program_id(0)
     tile = kept_ref.shape[0]
     rows = out_ref.shape[0] - EDGE
     values = value_ref[...].astype(F32)
-    grad = kept_ref[...] + arrived_ref[...]
+    grad = kept_ref[...] + near_ref[...] + arrived_ref[...]
     scale = lax.rsqrt(jnp.mean(values * values, -1, keepdims=True) + EPSILON)
     normed = values * scale
     through = grad * gain_ref[...].astype(F32)
@@ -1261,11 +1304,13 @@
         out_ref[rows:] += sums
 
 
-def norm_back(place, kept, arrived, values, gain, residual):
-    rows, model = kept.shape
+def norm_back(place, kept, near, arrived, values, gain, residual):
+    rows, model = arrived.shape
     steps = 2
     tile = rows // steps
     local = pl.BlockSpec((tile, model), lambda g, at: (g, 0))
+
+    own = pl.BlockSpec((tile, model), lambda g, at: (at[0] % 2 * steps + g, 0))
 
     def spec_of(array):
         if array.shape[0] == rows + EDGE:
@@ -1278,7 +1323,8 @@
             num_scalar_prefetch=1,
             grid=(steps,),
             in_specs=[
-                local,
+                own,
+                own,
                 local,
                 spec_of(values),
                 pl.BlockSpec((1, model), lambda g, at: (0, 0)),
@@ -1290,7 +1336,7 @@
         compiler_params=params(),
         cost_estimate=LIGHT,
         name="norm_back",
-    )(place, kept, arrived, values, gain, residual)
+    )(place, kept, near, arrived, values, gain, residual)
 
 
 def own_output_kernel(kept_ref, arrived_ref, middle_ref, gain_ref, out_ref):
@@ -1472,6 +1518,17 @@
         return self.send() if self.order else self
 
 
+class HeadSum:
+    def __init__(self, place, sent):
+        self.place = place
+        self.near = exchange(sent, "head", 1)
+
+    def send(self, half):
+        self.half = half
+        self.kept = quarter_sum(self.place, half, self.near)
+        self.arrived = exchange(self.kept, "head", 2)
+
+
 class WholeSum:
     def __init__(self, pairs):
         self.kept = self.sent = jnp.concatenate(
@@ -1542,6 +1599,8 @@
 
         maps = [at(every_map, step) for step in range(1, reach)]
         terms = [at(every_term, step) for step in range(1, reach + 1)]
+    if reach < count - 1:
+        return carry(maps, terms, TN if backward else NN)
     state = terms[-1]
     for map_of, term in zip(reversed(maps), reversed(terms[:-1])):
         state = move(map_of, state) + term
@@ -1638,11 +1697,10 @@
     )
     *filled, back_sent, fore_sent = dense(sent_half, None)
     split = lambda half: half.reshape(parts // 2, quarter, model)
-    back = Scatter(head_mine, "head", head_order, None, split(back_sent)).send()
+    back = HeadSum(places[:1], back_sent)
     *filled, back_kept, fore_kept = dense(kept_half, filled)
     middle, normed2_low, activ_low, *grads_both = filled
-    back.kept = split(back_kept)
-    back.step()
+    back.send(back_kept)
 
     near_first, far_first = seq_bits, seq_bits[1:] + seq_bits[:1]
     tiled = model // seq % LANES == 0
@@ -1677,7 +1735,7 @@
         back, fore, ffn_one, ffn_two, also=(ffn_three.sent, down_sum.sent)
     )
     grad_middle_own = norm_back(
-        places[:1], back.kept[0], back.arrived[0], middle, gain2_row, grad_output
+        places[:1], back.half, back.near, back.arrived, middle, gain2_row, grad_output
     )
 
     middle_start = GatherNear(grad_middle_own, "head")
@@ -1769,8 +1827,8 @@
         side_sum, down_sum, ffn_three,
         also=(part_sent, part_kept, mix_one.sent, *output_near),
     )
-    part = Scatter(head_mine, "head", head_order, split(part_kept), split(part_sent)).send()
-    part.step()
+    part = HeadSum(places[:1], part_sent)
+    part.send(part_kept)
     mix_one.send()
     tie = part.kept
     for one in (side_sum, down_sum):
@@ -1798,7 +1856,7 @@
         part, side_sum, down_sum, also=(mix_three.sent, mix_one.kept)
     )
     grad_input_own = norm_back(
-        places[:1], part.kept[0], part.arrived[0], block_input, first_gain[None], grad_middle_own
+        places[:1], part.half, part.near, part.arrived, block_input, first_gain[None], grad_middle_own
     )
 
     input_start = GatherNear(grad_input_own, "head")

time: 431 us -> 430 us (level)
  matrix products: 4.44 us -> 0 us
    pallas_call x0 -> x4, Pallas kernels: none -> 9.49 us  [the longest x2 4.76 us: quarter_sum(): pl.pallas_call(quarter_kernel, grid_spec=pltpu.PrefetchScalarGridSpec(num...]
    pallas_call x19 -> x17, Pallas kernels: 49 us -> 41.5 us  [combine(): pl.pallas_call(partial(combine_kernel, bit), in_specs=[SCALARS, IN_VMEM,...]
    dot_general x4 -> x0, matrix products: 4.44 us -> none  [move(): lax.dot_general(map_of, state, (((dims[0],), (1,)), ((0,), (0,))), precis...]
    unnamed x105 -> x119, local copies, waits for them, and re-layouts: 12.6 us -> 14.6 us
  transfers between devices with their start and end apart: 58 -> 58, of which waited for: 18 -> 18; matrix products, arithmetic and copies ran while one was open for 5% -> 5% of each run, Pallas kernels for 51% -> 52%
where the time goes in v4:
time: 430 us; the launch traced here: 422 us
  Pallas kernels  239 us (56%)
  starting transfers between devices  81.9 us (19%)
  waiting for transfers between devices  63.4 us (15%)
  local copies, waits for them, and re-layouts  27.6 us (6%)
  other arithmetic  7.84 us (2%)
    ppermute x48, waiting for transfers between devices, exchange(): lax.ppermute(value, axis, [(place, place ^ bit) for place in range(count)])  61.6 us
    ppermute x48, starting transfers between devices, exchange(): lax.ppermute(value, axis, [(place, place ^ bit) for place in range(count)])  57.9 us
    pallas_call x8, Pallas kernels, weight_grad(): pl.pallas_call(partial(grad_kernel, half, len(pairs)), grid_spec=pltpu.Pr...  43.7 us
    pallas_call x17, Pallas kernels, combine(): pl.pallas_call(partial(combine_kernel, bit), in_specs=[SCALARS, IN_VMEM,...  41.5 us
    pallas_call x1, Pallas kernels, recurrence_back(): pl.pallas_call(partial(back_kernel, heads), grid=(steps,), in_specs=[SCAL...  25.9 us
    pallas_call x1, Pallas kernels, local_maps(): pl.pallas_call(partial(local_kernel, heads), grid=(blocks // PACK,), in_s...  24.4 us
    ppermute x10, starting transfers between devices, shifted(): lax.ppermute(value, axis, [(source, source + steps) for source in range(f...  24 us
    pallas_call x2, Pallas kernels, dense_half(): pl.pallas_call(partial(dense_kernel, parts), grid_spec=pltpu.PrefetchScal...  22.9 us
  transfers between devices with their start and end apart: 58, of which 18 were waited for; matrix products, arithmetic and copies ran while one was open for 5% of the time, Pallas kernels for 52%

profile of v4, /device:TPU:0, one launch (start us, length us, event | category | flops | bytes accessed | tf_op | source)
XLA Modules:
  0.0 422.0 jit_solution(16962948388459633919)
XLA Ops:
  11.5 9.2 %first_projections.1 = (bf16[1024,1024]{1,0:T(8,128)(2,1)}, f32[1024,1280]{1,0:T(8,128)}, f32[1024,128]{1,0:T(8,128)}, f32[1024,256]{1,0:T(8,128)}, f32[8,1280]{1,0:T(8,128)}) custom-call(f32[8,1024]{1,0:T(8,128)} %copy-done.50, bf16[1024,1024]{1,0:T(8,128)(2,1)} %value_ref.1, bf16[1,1024]{1,0:T(2,128)(2,1)} %broadcast_in_dim.24.gain_ref, ...), custom_call_target="tpu_custom_call" | custom-call | flops 1 | bytes 1 | tf_op jit(solution)/shard_map/first_projections/pallas_call | solution.py:636
  20.7 24.4 %local_maps.1 = (f32[1024,1280]{1,0:T(8,128)}, f32[2,16,64,128]{3,2,1,0:T(8,128)}, bf16[2,16,128,128]{3,2,1,0:T(8,128)(2,1)}, bf16[2,16,128,128]{3,2,1,0:T(8,128...) custom-call(s32[1]{0:T(128)S(6)} %copy.64.offset_ref, ...), custom_call_target="tpu_custom_call" | custom-call | flops 1 | bytes 1 | tf_op jit(solution)/shard_map/local_maps/pallas_call | solution.py:289
  45.1 4.9 %collective-permute-start.2 = (f32[2,128,256]{2,1,0:T(8,128)}, f32[2,128,256]{2,1,0:T(8,128)S(1)}, u32[]{:S(2)}, u32[]{:S(2)}) collective-permute-start(f32[2,128,256]{2,1,0:T(8,128)} %get-tuple-element.276), channel_id=1, source_target_pairs={{0,8},{4,12},{8,16},{12,20},{16,24},{20,28},{1,9},{5,13},{9,17},{1... | collective-permute-start | bytes 786440 | tf_op jit(solution)/shard_map/ppermute | solution.py:1450
  53.5 5.3 %collective-permute-start.3 = (f32[2,128,128]{2,1,0:T(8,128)S(1)}, f32[2,128,128]{2,1,0:T(8,128)S(1)}, u32[]{:S(2)}, u32[]{:S(2)}) collective-permute-start(f32[2,128,128]{2,1,0:T(8,128)S(1)} %slice.55), channel_id=1, source_target_pairs={{0,12},{4,16},{8,20},{12,24},{16,28},{1,13},{5,17},{9,21},{13,25},... | collective-permute-start | bytes 393224 | tf_op jit(solution)/shard_map/ppermute | solution.py:1450
  65.2 8.8 %mixer_outputs.1 = (f32[2,16,128,128]{3,2,1,0:T(8,128)}, f32[2,16,128,128]{3,2,1,0:T(8,128)}, f32[1024,256]{1,0:T(8,128)}, f32[1024,256]{1,0:T(8,128)}) custom-call(s32[1]{0:T(128)S(6)} %copy.64.offset_ref, f32[2,128,128]{2,1,0:T(8,128)} %carry.2.incoming_ref, f32[2,16,128,256]{3,2,1,0:T(8,128)} %get-tuple-element.258.prefix_ref.refs_7_, ...), custom_call_target="tpu_custom_call" | custom-call | flops 1 | bytes 1 | tf_op jit(solution)/shard_map/mixer_outputs/pallas_call | solution.py:377
  87.6 5.6 %grad_activ.1.refs_10_ = f32[1024,704]{1,0:T(8,128)} custom-call(bf16[1024,1024]{1,0:T(8,128)(2,1)} %residual_ref.1, bf16[704,1024]{1,0:T(8,128)(2,1)} %refs_9_.3), custom_call_target="tpu_custom_call" | custom-call | flops 1 | bytes 1 | tf_op jit(solution)/shard_map/grad_activ/pallas_call | solution.py:660
  93.2 5.9 %collective-permute-done.5.refs_3_ = f32[1024,256]{1,0:T(8,128)S(1)} collective-permute-done((f32[1024,256]{1,0:T(8,128)}, f32[1024,256]{1,0:T(8,128)S(1)}, u32[]{:S(2)}, u32[]{:S(2)}) %collective-permute-start.5) | collective-permute-done | bytes 1048608 | tf_op jit(solution)/shard_map/ppermute | solution.py:1444
  101.9 11.4 %dense_half.2 = (f32[1024,1024]{1,0:T(8,128)}, bf16[1024,1024]{1,0:T(8,128)(2,1)}, bf16[1024,768]{1,0:T(8,128)(2,1)}, bf16[1024,384]{1,0:T(8,128)(2,1)}, bf16[10...) custom-call(s32[1]{0:T(128)} %bitcast.9.refs_0_, ...), custom_call_target="tpu_custom_call" | custom-call | flops 1 | bytes 1 | tf_op jit(solution)/shard_map/dense_half/pallas_call | solution.py:750
  113.6 11.5 %dense_half.3 = (f32[1024,1024]{1,0:T(8,128)}, bf16[1024,1024]{1,0:T(8,128)(2,1)}, bf16[1024,768]{1,0:T(8,128)(2,1)}, bf16[1024,384]{1,0:T(8,128)(2,1)}, bf16[10...) custom-call(s32[1]{0:T(128)} %bitcast.5.refs_0_.place_ref, ...), custom_call_target="tpu_custom_call", output_to_operand_aliasing={{0}: (11, {}), {1}: (12, {}), {2}: (13, {}), {3}: (14, {}),... | custom-call | flops 1 | bytes 1 | tf_op jit(solution)/shard_map/dense_half/pallas_call | solution.py:750
  142.8 5.4 %weight_grad.10 = (f32[4,128,640]{2,1,0:T(8,128)}, f32[4,128,640]{2,1,0:T(8,128)}) custom-call(s32[1]{0:T(128)} %bitcast.4.refs_0_.mine_ref, bf16[1024,1024]{1,0:T(8,128)(2,1)} %get-tuple-element.301.refs_1_.refs_2_.refs_3_.refs_4_, bf16[1024,1024]{1,0:T(8,128)(2,1)} %get-tuple-element.301.refs_1_.refs_2_.refs_3_.refs_4_, ...), custom_call_target="tpu_custom_call" | custom-call | flops 1 | bytes 1 | tf_op jit(solution)/shard_map/weight_grad/pallas_call | solution.py:1181
  148.2 5.9 %weight_grad.11 = (f32[4,128,768]{2,1,0:T(8,128)}, f32[4,128,768]{2,1,0:T(8,128)}) custom-call(s32[1]{0:T(128)} %bitcast.4.refs_0_.mine_ref, bf16[1024,1024]{1,0:T(8,128)(2,1)} %residual_ref.1, bf16[1024,1024]{1,0:T(8,128)(2,1)} %residual_ref.1, bf16[1024,1024]{1,0:T(8,128)(2,1)} %residual_ref.1, bf16[1024,1024]{1,0:T(8,128)(2,1)} %residual_ref.1, ...), custom_call_target="tpu_custom_call" | custom-call | flops 1 | bytes 1 | tf_op jit(solution)/shard_map/weight_grad/pallas_call | solution.py:1181
  181.6 6.7 %gate_back.2 = (f32[8,128]{1,0:T(8,128)}, f32[2,128,128]{2,1,0:T(8,128)}, f32[8,1024]{1,0:T(8,128)}, bf16[1024,1024]{1,0:T(8,128)(2,1)}, bf16[1024,256]{1,0:T(8,...) custom-call(s32[2]{0:T(128)} %pad_add_fusion.1.place_ref, f32[264,1024]{1,0:T(8,128)} %norm_back.2.refs_0_.residual_ref, ...), custom_call_target="tpu_custom_call" | custom-call | flops 1 | bytes 1 | tf_op jit(solution)/shard_map/gate_back/pallas_call | solution.py:522
  188.2 6.5 %collective-permute-done.18 = f32[2,128,384]{2,1,0:T(8,128)S(1)} collective-permute-done((f32[2,128,384]{2,1,0:T(8,128)}, f32[2,128,384]{2,1,0:T(8,128)S(1)}, u32[]{:S(2)}, u32[]{:S(2)}) %collective-permute-start.18) | collective-permute-done | bytes 393248 | tf_op jit(solution)/shard_map/ppermute | solution.py:1444
  198.7 6.8 %gate_back.3 = (f32[8,128]{1,0:T(8,128)}, f32[2,128,128]{2,1,0:T(8,128)}, f32[8,1024]{1,0:T(8,128)}, bf16[1024,1024]{1,0:T(8,128)(2,1)}, bf16[1024,256]{1,0:T(8,...) custom-call(s32[2]{0:T(128)} %pad_add_fusion.2.place_ref, ...), custom_call_target="tpu_custom_call", output_to_operand_aliasing={{3}: (12, {}), {4}: (13, {}), {5}: (14, {}), {6}: (15, {})} | custom-call | flops 1 | bytes 1 | tf_op jit(solution)/shard_map/gate_back/pallas_call | solution.py:522
  210.3 5.3 %weight_grad.12 = (f32[4,128,512]{2,1,0:T(8,128)}, f32[4,128,512]{2,1,0:T(8,128)}) custom-call(s32[1]{0:T(128)} %bitcast.4.refs_0_.mine_ref, bf16[1024,1024]{1,0:T(8,128)(2,1)} %get-tuple-element.348.refs_1_.refs_2_.refs_3_.refs_4_, bf16[1024,1024]{1,0:T(8,128)(2,1)} %get-tuple-element.348.refs_1_.refs_2_.refs_3_.refs_4_, ...), custom_call_target="tpu_custom_call" | custom-call | flops 1 | bytes 1 | tf_op jit(solution)/shard_map/weight_grad/pallas_call | solution.py:1181
  238.0 25.9 %recurrence_back.1 = (bf16[1024,1280]{1,0:T(8,128)(2,1)}, f32[16,1280]{1,0:T(8,128)}, f32[8,1280]{1,0:T(8,128)}, bf16[1024,128]{1,0:T(8,128)(2,1)}, f32[8,128]{1,0:T(8,128)}, /*index=5*/f32[8,1280]{1,0:T(8,128)}) custom-call(s32[1]{0:T(128)S(6)} %copy.64.offset_ref, f32[2,128,128]{2,1,0:T(8,128)} %carry.3.leaving_ref, ...), custom_call_target="tpu_custom_call" | custom-call | flops 1 | bytes 1 | tf_op jit(solution)/shard_map/recurrence_back/pallas_call | solution.py:1061
  278.4 5.9 %weight_grad.13 = (f32[4,128,640]{2,1,0:T(8,128)}, f32[4,128,640]{2,1,0:T(8,128)}) custom-call(s32[1]{0:T(128)} %bitcast.4.refs_0_.mine_ref, bf16[1024,1024]{1,0:T(8,128)(2,1)} %get-tuple-element.424.refs_6_.refs_7_.refs_8_.refs_9_.refs_1_.refs_2_.refs_3_.refs_4_.refs_11_.refs_12_.refs_13_.refs_14_, ...), custom_call_target="tpu_custom_call" | custom-call | flops 1 | bytes 1 | tf_op jit(solution)/shard_map/weight_grad/pallas_call | solution.py:1181
  284.3 8.8 %first_back.1 = (f32[512,1024]{1,0:T(8,128)}, f32[512,1024]{1,0:T(8,128)}) custom-call(s32[1]{0:T(128)} %bitcast.5.refs_0_.place_ref, bf16[1024,1280]{1,0:T(8,128)(2,1)} %fusion.refs_5_.refs_0_.refs_10_.refs_15_, bf16[1024,256]{1,0:T(8,128)(2,1)} %get-tuple-element.350.refs_10_.refs_1_, bf16[1024,128]{1,0:T(8,128)(2,1)} %get-tuple-element.396.refs_2_.refs_15_, ...), custom_call_target="tpu_custom_call" | custom-call | flops 1 | bytes 1 | tf_op jit(solution)/shard_map/first_back/pallas_call | solution.py:800
  293.1 5.9 %collective-permute-done.35 = f32[1,128,640]{2,1,0:T(8,128)S(1)} collective-permute-done((f32[1,128,640]{2,1,0:T(8,128)}, f32[1,128,640]{2,1,0:T(8,128)S(1)}, u32[]{:S(2)}, u32[]{:S(2)}) %collective-permute-start.35) | collective-permute-done | bytes 327712 | tf_op jit(solution)/shard_map/ppermute | solution.py:1444
  319.3 6.2 %weight_grad.14 = (f32[4,128,384]{2,1,0:T(8,128)}, f32[4,128,384]{2,1,0:T(8,128)}) custom-call(s32[1]{0:T(128)} %bitcast.4.refs_0_.mine_ref, bf16[1024,1024]{1,0:T(8,128)(2,1)} %get-tuple-element.424.refs_6_.refs_7_.refs_8_.refs_9_.refs_1_.refs_2_.refs_3_.refs_4_.refs_11_.refs_12_.refs_13_.refs_14_, ...), custom_call_target="tpu_custom_call" | custom-call | flops 1 | bytes 1 | tf_op jit(solution)/shard_map/weight_grad/pallas_call | solution.py:1181
  330.1 6.2 %weight_grad.15 = (f32[4,128,384]{2,1,0:T(8,128)}, f32[4,128,384]{2,1,0:T(8,128)}) custom-call(s32[1]{0:T(128)} %bitcast.4.refs_0_.mine_ref, bf16[1024,1024]{1,0:T(8,128)(2,1)} %get-tuple-element.424.refs_6_.refs_7_.refs_8_.refs_9_.refs_1_.refs_2_.refs_3_.refs_4_.refs_11_.refs_12_.refs_13_.refs_14_, ...), custom_call_target="tpu_custom_call" | custom-call | flops 1 | bytes 1 | tf_op jit(solution)/shard_map/weight_grad/pallas_call | solution.py:1181
  358.7 10.7 %collective-permute-done.47 = f32[2,128,640]{2,1,0:T(8,128)S(1)} collective-permute-done((f32[2,128,640]{2,1,0:T(8,128)S(1)}, f32[2,128,640]{2,1,0:T(8,128)S(1)}, u32[]{:S(2)}, u32[]{:S(2)}) %collective-permute-start.47) | collective-permute-done | bytes 655392 | tf_op jit(solution)/shard_map/ppermute | solution.py:1444
  392.6 5.2 %collective-permute-done.52 = f32[2,128,384]{2,1,0:T(8,128)S(1)} collective-permute-done((f32[2,128,384]{2,1,0:T(8,128)}, f32[2,128,384]{2,1,0:T(8,128)S(1)}, u32[]{:S(2)}, u32[]{:S(2)}) %collective-permute-start.52) | collective-permute-done | bytes 393248 | tf_op jit(solution)/shard_map/ppermute | solution.py:1444
  400.5 5.3 %collective-permute-done.53 = f32[112,128]{1,0:T(8,128)S(1)} collective-permute-done((f32[112,128]{1,0:T(8,128)S(1)}, f32[112,128]{1,0:T(8,128)S(1)}, u32[]{:S(2)}, u32[]{:S(2)}) %collective-permute-start.53) | collective-permute-done | bytes 57376 | tf_op jit(solution)/shard_map/ppermute | solution.py:1444
  (292 shorter events, 216.2 us)
Async XLA Ops:
  1.8 57.7 %collective-permute-start.7 = (f32[256,1024]{1,0:T(8,128)S(1)}, f32[256,1024]{1,0:T(8,128)}, u32[]{:S(2)}, u32[]{:S(2)}) collective-permute-start(f32[256,1024]{1,0:T(8,128)S(1)} %convert_element_type.17.refs_0_), channel_id=1, source_target_pairs={{0,2},{1,3},{2,0},{3,1},{4,6},{5,7},{6,4},{7,5},{8,10},{9,11},{10,... | collective-permute-start | bytes 3145736 | tf_op jit(solution)/shard_map/ppermute | solution.py:1444
  52.5 31.8 %collective-permute-start.6 = (f32[256,1024]{1,0:T(8,128)S(1)}, f32[256,1024]{1,0:T(8,128)}, u32[]{:S(2)}, u32[]{:S(2)}) collective-permute-start(f32[256,1024]{1,0:T(8,128)S(1)} %convert_element_type.17.refs_0_), channel_id=1, source_target_pairs={{0,1},{1,0},{2,3},{3,2},{4,5},{5,4},{6,7},{7,6},{8,9},{9,8},{10,11... | collective-permute-start | bytes 3145736 | tf_op jit(solution)/shard_map/ppermute | solution.py:1444
  59.5 24.8 %collective-permute-start.8 = (f32[256,1024]{1,0:T(8,128)}, f32[256,1024]{1,0:T(8,128)}, u32[]{:S(2)}, u32[]{:S(2)}) collective-permute-start(f32[256,1024]{1,0:T(8,128)} %collective-permute-done.7.refs_2_), channel_id=1, source_target_pairs={{0,1},{1,0},{2,3},{3,2},{4,5},{5,4},{6,7},{7,6},{8,9},{9,8},{10,11... | collective-permute-start | bytes 3145736 | tf_op jit(solution)/shard_map/ppermute | solution.py:1444
  74.0 25.0 %collective-permute-start.5 = (f32[1024,256]{1,0:T(8,128)}, f32[1024,256]{1,0:T(8,128)S(1)}, u32[]{:S(2)}, u32[]{:S(2)}) collective-permute-start(f32[1024,256]{1,0:T(8,128)} %get-tuple-element.266.refs_1_), channel_id=1, source_target_pairs={{0,2},{1,3},{2,0},{3,1},{4,6},{5,7},{6,4},{7,5},{8,10},{9,11},{10,... | collective-permute-start | bytes 3145736 | tf_op jit(solution)/shard_map/ppermute | solution.py:1444
  128.8 31.4 %collective-permute-start.14 = (f32[2,256,1024]{2,1,0:T(8,128)}, f32[2,256,1024]{2,1,0:T(8,128)S(1)}, u32[]{:S(2)}, u32[]{:S(2)}) collective-permute-start(f32[2,256,1024]{2,1,0:T(8,128)} %bitcast.11), channel_id=1, source_target_pairs={{0,1},{1,0},{2,3},{3,2},{4,5},{5,4},{6,7},{7,6},{8,9},{9,8},{10,11... | collective-permute-start | bytes 6291464 | tf_op jit(solution)/shard_map/ppermute | solution.py:1444
  129.1 31.2 %collective-permute-start.13 = (f32[256,1024]{1,0:T(8,128)}, f32[256,1024]{1,0:T(8,128)S(1)}, u32[]{:S(2)}, u32[]{:S(2)}) collective-permute-start(f32[256,1024]{1,0:T(8,128)} %quarter_sum.2), channel_id=1, source_target_pairs={{0,2},{1,3},{2,0},{3,1},{4,6},{5,7},{6,4},{7,5},{8,10},{9,11},{10,... | collective-permute-start | bytes 3145736 | tf_op jit(solution)/shard_map/ppermute | solution.py:1444
  165.2 30.6 %collective-permute-start.19 = (f32[4,128,640]{2,1,0:T(8,128)}, f32[4,128,640]{2,1,0:T(8,128)S(1)}, u32[]{:S(2)}, u32[]{:S(2)}) collective-permute-start(f32[4,128,640]{2,1,0:T(8,128)} %get-tuple-element.318), channel_id=1, source_target_pairs={{0,4},{4,0},{8,12},{12,8},{16,20},{20,16},{24,28},{28,24},{1,5},{5... | collective-permute-start | bytes 3932168 | tf_op jit(solution)/shard_map/ppermute | solution.py:1444
  167.0 28.8 %collective-permute-start.21 = (f32[264,1024]{1,0:T(8,128)}, f32[264,1024]{1,0:T(8,128)S(1)}, u32[]{:S(2)}, u32[]{:S(2)}) collective-permute-start(f32[264,1024]{1,0:T(8,128)} %norm_back.2.refs_0_.residual_ref), channel_id=1, source_target_pairs={{0,2},{1,3},{2,0},{3,1},{4,6},{5,7},{6,4},{7,5},{8,10},{9,11},{10,... | collective-permute-start | bytes 3244040 | tf_op jit(solution)/shard_map/ppermute | solution.py:1444
  195.9 28.4 %collective-permute-start.22 = (f32[1,256,1024]{2,1,0:T(8,128)}, f32[1,256,1024]{2,1,0:T(8,128)}, u32[]{:S(2)}, u32[]{:S(2)}) collective-permute-start(f32[1,256,1024]{2,1,0:T(8,128)} %get-tuple-element.335), channel_id=1, source_target_pairs={{0,2},{1,3},{2,0},{3,1},{4,6},{5,7},{6,4},{7,5},{8,10},{9,11},{10,... | collective-permute-start | bytes 3145736 | tf_op jit(solution)/shard_map/ppermute | solution.py:1444
  224.3 39.6 %collective-permute-start.29 = (f32[4,128,768]{2,1,0:T(8,128)S(1)}, f32[4,128,768]{2,1,0:T(8,128)S(1)}, u32[]{:S(2)}, u32[]{:S(2)}) collective-permute-start(f32[4,128,768]{2,1,0:T(8,128)S(1)} %copy-done.52), channel_id=1, source_target_pairs={{0,4},{4,0},{8,12},{12,8},{16,20},{20,16},{24,28},{28,24},{1,5},{5... | collective-permute-start | bytes 4718600 | tf_op jit(solution)/shard_map/ppermute | solution.py:1444
  231.0 32.9 %collective-permute-start.31 = (f32[264,1024]{1,0:T(8,128)}, f32[264,1024]{1,0:T(8,128)S(1)}, u32[]{:S(2)}, u32[]{:S(2)}) collective-permute-start(f32[264,1024]{1,0:T(8,128)} %own_output.1.refs_0_), channel_id=1, source_target_pairs={{0,2},{1,3},{2,0},{3,1},{4,6},{5,7},{6,4},{7,5},{8,10},{9,11},{10,... | collective-permute-start | bytes 3244040 | tf_op jit(solution)/shard_map/ppermute | solution.py:1444
  232.3 31.6 %collective-permute-start.28 = (f32[2,128,640]{2,1,0:T(8,128)S(1)}, f32[2,128,640]{2,1,0:T(8,128)S(1)}, u32[]{:S(2)}, u32[]{:S(2)}) collective-permute-start(f32[2,128,640]{2,1,0:T(8,128)S(1)} %copy-done.55), channel_id=1, source_target_pairs={{0,8},{4,12},{8,0},{12,4},{16,24},{20,28},{24,16},{28,20},{1,9},{5... | collective-permute-start | bytes 1966088 | tf_op jit(solution)/shard_map/ppermute | solution.py:1444
  234.7 29.1 %collective-permute-start.27 = (f32[1,128,384]{2,1,0:T(8,128)S(1)}, f32[1,128,384]{2,1,0:T(8,128)S(1)}, u32[]{:S(2)}, u32[]{:S(2)}) collective-permute-start(f32[1,128,384]{2,1,0:T(8,128)S(1)} %copy-done.57), channel_id=1, source_target_pairs={{0,16},{4,20},{8,24},{12,28},{16,0},{20,4},{24,8},{28,12},{1,17},{... | collective-permute-start | bytes 589832 | tf_op jit(solution)/shard_map/ppermute | solution.py:1444
  265.2 35.2 %collective-permute-start.36 = (f32[264,1024]{1,0:T(8,128)S(1)}, f32[264,1024]{1,0:T(8,128)S(1)}, u32[]{:S(2)}, u32[]{:S(2)}) collective-permute-start(f32[264,1024]{1,0:T(8,128)S(1)} %collective-permute-done.31.refs_2_), channel_id=1, source_target_pairs={{0,1},{1,0},{2,3},{3,2},{4,5},{5,4},{6,7},{7,6},{8,9},{9,8},{10,11... | collective-permute-start | bytes 3244040 | tf_op jit(solution)/shard_map/ppermute | solution.py:1444
  270.9 29.6 %collective-permute-start.33 = (f32[4,128,512]{2,1,0:T(8,128)S(1)}, f32[4,128,512]{2,1,0:T(8,128)S(1)}, u32[]{:S(2)}, u32[]{:S(2)}) collective-permute-start(f32[4,128,512]{2,1,0:T(8,128)S(1)} %copy-done.53), channel_id=1, source_target_pairs={{0,4},{4,0},{8,12},{12,8},{16,20},{20,16},{24,28},{28,24},{1,5},{5... | collective-permute-start | bytes 3145736 | tf_op jit(solution)/shard_map/ppermute | solution.py:1444
  273.6 26.9 %collective-permute-start.34 = (f32[2,128,768]{2,1,0:T(8,128)}, f32[2,128,768]{2,1,0:T(8,128)S(1)}, u32[]{:S(2)}, u32[]{:S(2)}) collective-permute-start(f32[2,128,768]{2,1,0:T(8,128)} %get-tuple-element.389), channel_id=1, source_target_pairs={{0,8},{4,12},{8,0},{12,4},{16,24},{20,28},{24,16},{28,20},{1,9},{5... | collective-permute-start | bytes 2359304 | tf_op jit(solution)/shard_map/ppermute | solution.py:1444
  274.2 24.8 %collective-permute-start.35 = (f32[1,128,640]{2,1,0:T(8,128)}, f32[1,128,640]{2,1,0:T(8,128)S(1)}, u32[]{:S(2)}, u32[]{:S(2)}) collective-permute-start(f32[1,128,640]{2,1,0:T(8,128)} %get-tuple-element.390), channel_id=1, source_target_pairs={{0,16},{4,20},{8,24},{12,28},{16,0},{20,4},{24,8},{28,12},{1,17},{... | collective-permute-start | bytes 983048 | tf_op jit(solution)/shard_map/ppermute | solution.py:1444
  300.5 35.7 %collective-permute-start.41 = (f32[4,128,640]{2,1,0:T(8,128)}, f32[4,128,640]{2,1,0:T(8,128)S(1)}, u32[]{:S(2)}, u32[]{:S(2)}) collective-permute-start(f32[4,128,640]{2,1,0:T(8,128)} %get-tuple-element.426), channel_id=1, source_target_pairs={{0,4},{4,0},{8,12},{12,8},{16,20},{20,16},{24,28},{28,24},{1,5},{5... | collective-permute-start | bytes 3932168 | tf_op jit(solution)/shard_map/ppermute | solution.py:1444
  308.6 31.6 %collective-permute-start.38 = (f32[256,1024]{1,0:T(8,128)}, f32[256,1024]{1,0:T(8,128)S(1)}, u32[]{:S(2)}, u32[]{:S(2)}) collective-permute-start(f32[256,1024]{1,0:T(8,128)} %quarter_sum.3), channel_id=1, source_target_pairs={{0,2},{1,3},{2,0},{3,1},{4,6},{5,7},{6,4},{7,5},{8,10},{9,11},{10,... | collective-permute-start | bytes 3145736 | tf_op jit(solution)/shard_map/ppermute | solution.py:1444
  312.3 28.0 %collective-permute-start.39 = (f32[2,128,512]{2,1,0:T(8,128)}, f32[2,128,512]{2,1,0:T(8,128)S(1)}, u32[]{:S(2)}, u32[]{:S(2)}) collective-permute-start(f32[2,128,512]{2,1,0:T(8,128)} %get-tuple-element.422), channel_id=1, source_target_pairs={{0,8},{4,12},{8,0},{12,4},{16,24},{20,28},{24,16},{28,20},{1,9},{5... | collective-permute-start | bytes 1572872 | tf_op jit(solution)/shard_map/ppermute | solution.py:1444
  345.1 30.4 %collective-permute-start.46 = (f32[264,1024]{1,0:T(8,128)}, f32[264,1024]{1,0:T(8,128)S(1)}, u32[]{:S(2)}, u32[]{:S(2)}) collective-permute-start(f32[264,1024]{1,0:T(8,128)} %norm_back.3.refs_0_), channel_id=1, source_target_pairs={{0,2},{1,3},{2,0},{3,1},{4,6},{5,7},{6,4},{7,5},{8,10},{9,11},{10,... | collective-permute-start | bytes 3244040 | tf_op jit(solution)/shard_map/ppermute | solution.py:1444
  346.5 29.0 %collective-permute-start.44 = (f32[4,128,384]{2,1,0:T(8,128)}, f32[4,128,384]{2,1,0:T(8,128)S(1)}, u32[]{:S(2)}, u32[]{:S(2)}) collective-permute-start(f32[4,128,384]{2,1,0:T(8,128)} %get-tuple-element.439), channel_id=1, source_target_pairs={{0,4},{4,0},{8,12},{12,8},{16,20},{20,16},{24,28},{28,24},{1,5},{5... | collective-permute-start | bytes 2359304 | tf_op jit(solution)/shard_map/ppermute | solution.py:1444
  379.2 30.5 %collective-permute-start.55 = (f32[1,128,640]{2,1,0:T(8,128)}, f32[1,128,640]{2,1,0:T(8,128)S(1)}, u32[]{:S(2)}, u32[]{:S(2)}) collective-permute-start(f32[1,128,640]{2,1,0:T(8,128)} %get-tuple-element.468), channel_id=1, source_target_pairs={{0,16},{4,20},{8,24},{12,28},{16,0},{20,4},{24,8},{28,12},{1,17},{... | collective-permute-start | bytes 983048 | tf_op jit(solution)/shard_map/ppermute | solution.py:1444
  382.2 27.6 %collective-permute-start.56 = (f32[1,128,384]{2,1,0:T(8,128)}, f32[1,128,384]{2,1,0:T(8,128)S(1)}, u32[]{:S(2)}, u32[]{:S(2)}) collective-permute-start(f32[1,128,384]{2,1,0:T(8,128)} %get-tuple-element.471), channel_id=1, source_target_pairs={{0,16},{4,20},{8,24},{12,28},{16,0},{20,4},{24,8},{28,12},{1,17},{... | collective-permute-start | bytes 589832 | tf_op jit(solution)/shard_map/ppermute | solution.py:1444
  (92 other events, 903.8 us)
